TPU v7x, 512 devices: a whole 4x8x8 slice. The times are simulated.
512 devices in a mesh: dp: 8 (over z), space: 64 (over y, x, core).
Axes of the slice: x: 4, y: 8, z: 8, core: 2. Of those that a mesh axis runs over, the one named last changes fastest.
Arguments:
- mesh_latent: bfloat16 [8, 8192, 512], P('dp', 'space'), may hold values from -6 to 6
- grid_latent: bfloat16 [8, 32768, 512], P('dp', 'space'), may hold values from -6 to 6
- cotangent: bfloat16 [8, 32768, 512], P('dp', 'space'), may hold values from -6 to 6
- sender_slot: int32 [98304], P('space'), may hold values from 0 to 191, as said below
- send_rows: int32 [64, 4, 16], P('space'), may hold values from 0 to 127, as said below
- w_send: bfloat16 [512, 512], replicated, may hold values from -0.25 to 0.25
- w_recv: bfloat16 [512, 512], replicated, may hold values from -0.25 to 0.25
- w_node: bfloat16 [512, 512], replicated, may hold values from -0.25 to 0.25
- edge_bias: float32 [512], replicated, may hold values from -3 to 3
Outputs:
- grad_mesh: float32 [8, 8192, 512], P('dp', 'space')
- grad_grid: bfloat16 [8, 32768, 512], P('dp', 'space')
- grad_w_send: bfloat16 [512, 512], replicated
- grad_w_recv: bfloat16 [512, 512], replicated
- grad_w_node: bfloat16 [512, 512], replicated
- grad_bias: float32 [512], replicated
Inputs may be any that keep to these rules, and one draw needn't show every extreme that they name: `sender_slot`: on partition p, a value v >= 128 with h = v - 128 names a halo position i = h % 16 that is filled by partition q of the steps; positions of one neighbour block that no edge names may exist. `send_rows`: within one partition and one neighbour block the rows are distinct.
All inputs are finite; a program needn't handle non-finite values.
Results may differ from a plain program's by a relative error of at most 0.012.
Values may be sent and summed in bfloat16 or wider, within the bound.
No kernel may reach another device: no remote copies, remote signals or barrier semaphores. Data moves between devices by JAX's collectives and lax.ppermute only.
A program may use at most 64 MiB of HBM per device.

v0:
```python
import jax
import jax.numpy as jnp
from jax import lax
from jax.sharding import PartitionSpec as P


def silu_slope(preact):
    sigmoid_value = jax.nn.sigmoid(preact)
    return sigmoid_value * (1.0 + preact * (1.0 - sigmoid_value))


def neighbour_offsets():
    pieces = lax.axis_size("space")
    stride = max(2, pieces // 8)
    return (pieces, [1, -1, stride, pieces // 2])


def fetch_halo(outgoing):
    pieces, offset_list = neighbour_offsets()
    position = lax.axis_index("space")
    buffer = jnp.zeros((pieces,) + outgoing.shape[1:], outgoing.dtype)
    for block_index in range(4):
        target = (position + offset_list[block_index]) % pieces
        buffer = lax.dynamic_update_slice(
            buffer, outgoing[block_index][None], (target, jnp.int32(0), jnp.int32(0))
        )
    arrived = lax.all_to_all(buffer, "space", split_axis=0, concat_axis=0, tiled=True)
    blocks = [
        lax.dynamic_index_in_dim(
            arrived, (position - offset_list[block_index]) % pieces, 0, keepdims=False
        )
        for block_index in range(4)
    ]
    return jnp.stack(blocks)


def return_halo(values):
    pieces, offset_list = neighbour_offsets()
    position = lax.axis_index("space")
    buffer = jnp.zeros((pieces,) + values.shape[1:], values.dtype)
    for block_index in range(4):
        target = (position - offset_list[block_index]) % pieces
        buffer = lax.dynamic_update_slice(
            buffer, values[block_index][None], (target, jnp.int32(0), jnp.int32(0))
        )
    arrived = lax.all_to_all(
        buffer.astype(jnp.bfloat16), "space", split_axis=0, concat_axis=0, tiled=True
    ).astype(buffer.dtype)
    blocks = [
        lax.dynamic_index_in_dim(
            arrived, (position + offset_list[block_index]) % pieces, 0, keepdims=False
        )
        for block_index in range(4)
    ]
    return jnp.stack(blocks)


def contract_rows(left, right, precision=None):
    return lax.dot_general(
        left,
        right,
        (((0,), (0,)), ((), ())),
        precision=precision,
        preferred_element_type=jnp.float32,
    )


def per_device(
    mesh_latent, grid_latent, cotangent, sender_slot, send_rows, w_send, w_recv, w_node, edge_bias
):
    mesh_rows = mesh_latent[0]
    grid_rows = grid_latent[0]
    upstream = cotangent[0]
    send_list = send_rows[0]
    count_mesh = mesh_rows.shape[0]
    count_grid = grid_rows.shape[0]
    width = mesh_rows.shape[1]
    arrived = fetch_halo(mesh_rows[send_list])
    known = jnp.concatenate([mesh_rows, arrived.reshape(-1, width)], axis=0)
    sent_proj = jnp.dot(known, w_send, preferred_element_type=jnp.float32)
    recv_proj = jnp.dot(grid_rows, w_recv, preferred_element_type=jnp.float32)
    preact = (
        sent_proj[sender_slot].reshape(count_grid, 3, width) + recv_proj[:, None, :] + edge_bias
    )
    aggregate = jnp.sum(jax.nn.silu(preact), axis=1).astype(jnp.bfloat16)
    agg_grad = jnp.dot(upstream, w_node.T, preferred_element_type=jnp.float32)
    edge_grad = (agg_grad[:, None, :] * silu_slope(preact)).astype(jnp.bfloat16)
    edge_flat = edge_grad.reshape(-1, width)
    recv_grad = jnp.sum(edge_grad, axis=1, dtype=jnp.float32).astype(jnp.bfloat16)
    grad_grid = (
        upstream.astype(jnp.float32)
        + jnp.dot(recv_grad, w_recv.T, preferred_element_type=jnp.float32)
    ).astype(jnp.bfloat16)
    node_term = contract_rows(aggregate, upstream)
    recv_term = contract_rows(grid_rows, recv_grad)
    bias_term = jnp.sum(edge_flat, axis=0, dtype=jnp.float32)
    slot_table = (
        sender_slot[:, None] == jnp.arange(known.shape[0], dtype=jnp.int32)[None, :]
    ).astype(jnp.bfloat16)
    slot_grad = contract_rows(slot_table, edge_flat)
    w_send32 = w_send.astype(jnp.float32)
    flat_list = send_list.reshape(-1)
    send_term = contract_rows(known.astype(jnp.float32), slot_grad, lax.Precision.HIGHEST)
    mesh_all = jnp.dot(slot_grad, w_send32.T, precision=lax.Precision.HIGHEST)
    returned = return_halo(mesh_all[count_mesh:].reshape(4, -1, width))
    grad_mesh = mesh_all[:count_mesh].at[flat_list].add(returned.reshape(-1, width))
    totals = lax.psum((send_term, recv_term, node_term, bias_term), ("dp", "space"))
    send_sum, recv_sum, node_sum, bias_sum = totals
    factor = float(lax.axis_size("dp") * lax.axis_size("space") * count_grid) ** (-0.5)
    grad_w_send = (send_sum * factor).astype(jnp.bfloat16)
    grad_w_recv = (recv_sum * factor).astype(jnp.bfloat16)
    grad_w_node = (node_sum * factor).astype(jnp.bfloat16)
    grad_bias = bias_sum * factor
    return (grad_mesh[None], grad_grid[None], grad_w_send, grad_w_recv, grad_w_node, grad_bias)


def solution(mesh):
    placed = (
        P("dp", "space", None),
        P("dp", "space", None),
        P("dp", "space", None),
        P("space"),
        P("space", None, None),
        P(),
        P(),
        P(),
        P(),
    )
    return jax.shard_map(
        per_device,
        mesh=mesh,
        in_specs=placed,
        out_specs=(P("dp", "space", None), P("dp", "space", None), P(), P(), P(), P()),
        check_vma=False,
    )
```

profile of v0, /device:TPU:1, one launch (start us, length us, event | category | flops | bytes accessed | tf_op | source)
XLA Modules:
  0.0 398.3 jit_solution(9465606937656309920)
XLA Ops:
  8.1 1.6 gather_fusion
  9.7 1.1 broadcast_in_dim.10
  13.3 11.8 %all-to-all-start = ((bf16[64,16,512]{2,1,0:T(8,128)(2,1)}), bf16[64,16,512]{2,1,0:T(8,128)(2,1)}, u32[]{:S(2)}, u32[]{:S(2)}) async-start(bf16[64,16,512]{2,1,0:T(8,128)(2,1)} %fusion.19), calls=%async_computation | async-start | bytes 2097152 | tf_op jit(solution)/shard_map/all_to_all | solution.py:27
  25.6 2.7 add.200
  28.3 6.0 %add.201 = f32[1536,512]{1,0:T(8,128)} reshape(f32[512,3,512]{2,1,0:T(4,128)} %add.200) | data formatting | bytes 6291456 | tf_op jit(solution)/shard_map/add | solution.py:83
  34.3 1.5 fusion.10
  35.8 2.7 mul.56
  38.5 6.0 %mul.57 = f32[1536,512]{1,0:T(8,128)} reshape(f32[512,3,512]{2,1,0:T(4,128)} %mul.56) | data formatting | bytes 6291456 | tf_op jit(solution)/shard_map/mul | solution.py:87
  44.6 8.4 %all-to-all-done = bf16[64,16,512]{2,1,0:T(8,128)(2,1)} async-done(((bf16[64,16,512]{2,1,0:T(8,128)(2,1)}), bf16[64,16,512]{2,1,0:T(8,128)(2,1)}, u32[]{:S(2)}, u32[]{:S(2)}) %all-to-all-start) | async-done | bytes 1048608 | tf_op jit(solution)/shard_map/all_to_all | solution.py:27
  53.8 1.3 fusion.14
  55.1 5.0 %gather_fusion.1 = f32[1536,512]{1,0:T(8,128)} fusion(f32[192,512]{1,0:T(8,128)S(1)} %fusion.14, s32[2048]{0:T(1024)S(1)} %pad_clamp_fusion), kind=kCustom, calls=%fused_computation.1 | custom fusion | bytes 6297600 | tf_op jit(solution)/shard_map/gather | solution.py:83
  60.0 5.8 %reshape.105 = f32[512,3,512]{2,1,0:T(4,128)} reshape(f32[1536,512]{1,0:T(8,128)} %gather_fusion.1) | data formatting | bytes 6291456 | tf_op jit(solution)/shard_map/reshape | solution.py:83
  65.9 8.1 %fusion = bf16[512,512]{1,0:T(8,128)(2,1)S(1)} fusion(f32[512]{0:T(512)S(1)} %copy-done.13, f32[512,3,512]{2,1,0:T(4,128)} %reshape.105, f32[512,512]{1,0:T(8,128)S(1)} %fusion.6, f32[512,512]{1,0:T(8,128)S(1)} %fusion.10), kind=kLoop, calls=%fused_computation.9 | loop fusion | flops 9175040 | bytes 5769216 | tf_op jit(solution)/shard_map/reduce_sum | solution.py:89
  74.0 4.8 %multiply_reduce_fusion = bf16[512,512]{1,0:T(8,128)(2,1)S(1)} fusion(f32[512,3,512]{2,1,0:T(4,128)S(1)} %copy-done.1, f32[512]{0:T(512)S(1)} %copy-done.13, f32[512,512]{1,0:T(8,128)S(1)} %fusion.6), kind=kLoop, calls=%fused_computation.3 | loop fusion | flops 5242880 | bytes 4720640 | tf_op jit(solution)/shard_map/reduce_sum | solution.py:85
  78.8 3.3 convert_reduce_fusion
  83.0 1.6 fusion.13
  84.7 1.4 fusion.26
  86.1 1.5 convolution_bitcast_fusion
  87.6 1.4 fusion.8
  89.0 1.1 broadcast_in_dim.24
  90.2 1.4 fusion.18
  91.6 1.4 fusion.17
  93.0 1.4 fusion.16
  94.3 1.4 fusion.15
  95.7 6.5 %all-to-all-start.1 = ((bf16[64,16,512]{2,1,0:T(8,128)(2,1)}), bf16[64,16,512]{2,1,0:T(8,128)(2,1)S(1)}, u32[]{:S(2)}, u32[]{:S(2)}) async-start(bf16[64,16,512]{2,1,0:T(8,128)(2,1)} %fusion.15), calls=%async_computation.1 | async-start | bytes 2097152 | tf_op jit(solution)/shard_map/all_to_all | solution.py:46
  102.4 1.0 slice.69
  103.3 122.8 %psum.31 = f32[512]{0:T(512)S(1)} all-reduce(f32[512]{0:T(512)S(1)} %get-tuple-element.9), channel_id=1, replica_groups=mesh['dp'=8,'space'=64] {'dp','space'}, use_global_device_ids=true, to_apply=%region_7.8 | all-reduce | flops 512 | bytes 4096 | tf_op jit(solution)/shard_map/psum | solution.py:107
  226.2 1.3 fusion.3
  228.0 156.4 %all-reduce.3.cloned.1.call-done = (f32[512,512]{1,0:T(8,128)}, f32[512,512]{1,0:T(8,128)}, f32[512,512]{1,0:T(8,128)}) async-done(((f32[512,512]{1,0:T(8,128)}, f32[512,512]{1,0:T(8,128)}, f32[512,512]{1,0:T(8,128)}), (f32[512,512]{1,0:T(8,128)}, f32[512,512]{1,0:T(8,128)}, f32[512,512]{1,0:T(8,128)})) %all-reduce.3.cloned.1.call-update) | async-done | bytes 3145744 | tf_op jit(solution)/shard_map/psum | solution.py:107
  384.4 2.1 multiply_convert_fusion.4
  386.5 2.8 multiply_convert_fusion.2
  389.7 1.1 scatter_fusion
  (54 shorter events, 7.2 us)
Async XLA Ops:
  7.2 18.0 %copy-start = (bf16[1,512,512]{2,1,0:T(8,128)(2,1)S(1)}, bf16[1,512,512]{2,1,0:T(8,128)(2,1)}, u32[]{:S(2)}) copy-start(bf16[1,512,512]{2,1,0:T(8,128)(2,1)} %param.10) | copy-start | bytes 1572868
  7.2 18.0 %copy-start.11 = (bf16[512,512]{1,0:T(8,128)(2,1)S(1)}, bf16[512,512]{1,0:T(8,128)(2,1)}, u32[]{:S(2)}) copy-start(bf16[512,512]{1,0:T(8,128)(2,1)} %param.15) | copy-start | bytes 1572868
  13.3 39.7 %all-to-all-start = ((bf16[64,16,512]{2,1,0:T(8,128)(2,1)}), bf16[64,16,512]{2,1,0:T(8,128)(2,1)}, u32[]{:S(2)}, u32[]{:S(2)}) async-start(bf16[64,16,512]{2,1,0:T(8,128)(2,1)} %fusion.19), calls=%async_computation | async-start | bytes 2097152 | tf_op jit(solution)/shard_map/all_to_all | solution.py:27
  25.1 359.3 %all-reduce.3.cloned.1.call-start = ((), (), s32[]{:S(2)}) async-start(), calls=%async_computation.2 | async-start | bytes 6291456 | tf_op jit(solution)/shard_map/psum | solution.py:107
  28.3 6.0 %copy-start.8 = (bf16[1,512,512]{2,1,0:T(8,128)(2,1)S(1)}, bf16[1,512,512]{2,1,0:T(8,128)(2,1)}, u32[]{:S(2)}) copy-start(bf16[1,512,512]{2,1,0:T(8,128)(2,1)} %param.11) | copy-start | bytes 1572868
  38.5 6.0 %copy-start.15 = (s32[1536]{0:T(1024)S(1)}, s32[1536]{0:T(1024)}, u32[]{:S(2)}) copy-start(s32[1536]{0:T(1024)} %param.12) | copy-start | bytes 18436
  38.5 15.2 %copy-start.5 = (bf16[1,128,512]{2,1,0:T(8,128)(2,1)S(1)}, bf16[1,128,512]{2,1,0:T(8,128)(2,1)}, u32[]{:S(2)}) copy-start(bf16[1,128,512]{2,1,0:T(8,128)(2,1)} %param.9) | copy-start | bytes 393220
  60.0 5.8 %copy-start.13 = (f32[512]{0:T(512)S(1)}, f32[512]{0:T(512)}, u32[]{:S(2)}) copy-start(f32[512]{0:T(512)} %param.17) | copy-start | bytes 6148
  65.9 8.1 %copy-start.1 = (f32[512,3,512]{2,1,0:T(4,128)S(1)}, f32[512,3,512]{2,1,0:T(4,128)}, u32[]{:S(2)}) copy-start(f32[512,3,512]{2,1,0:T(4,128)} %reshape.105) | copy-start | bytes 9437188
  65.9 13.0 %copy-start.3 = (f32[1536,512]{1,0:T(8,128)S(1)}, f32[1536,512]{1,0:T(8,128)}, u32[]{:S(2)}) copy-start(f32[1536,512]{1,0:T(8,128)} %add.201) | copy-start | bytes 9437188
  74.0 12.1 %copy-start.6 = (bf16[512,512]{1,0:T(8,128)(2,1)}, bf16[512,512]{1,0:T(8,128)(2,1)S(1)}, u32[]{:S(2)}) copy-start(bf16[512,512]{1,0:T(8,128)(2,1)S(1)} %fusion) | copy-start | bytes 1572868
  74.0 4.9 %copy-start.2 = (f32[1536,512]{1,0:T(8,128)S(1)}, f32[1536,512]{1,0:T(8,128)}, u32[]{:S(2)}) copy-start(f32[1536,512]{1,0:T(8,128)} %gather_fusion.1) | copy-start | bytes 9437188
  82.1 2.5 copy-start.10
  82.1 5.5 %copy-start.9 = (bf16[1,512,512]{2,1,0:T(8,128)(2,1)S(1)}, bf16[1,512,512]{2,1,0:T(8,128)(2,1)}, u32[]{:S(2)}) copy-start(bf16[1,512,512]{2,1,0:T(8,128)(2,1)} %param.11) | copy-start | bytes 1572868
  89.0 13.2 %copy-start.14 = (s32[1,4,16]{2,1,0:T(4,128)S(1)}, s32[1,4,16]{2,1,0:T(4,128)}, u32[]{:S(2)}) copy-start(s32[1,4,16]{2,1,0:T(4,128)} %param.13) | copy-start | bytes 772
  90.2 136.0 %copy-start.7 = (bf16[512,512]{1,0:T(8,128)(2,1)S(1)}, bf16[512,512]{1,0:T(8,128)(2,1)}, u32[]{:S(2)}) copy-start(bf16[512,512]{1,0:T(8,128)(2,1)} %copy-done.6) | copy-start | bytes 1572868
  90.2 136.0 %copy-start.12 = (bf16[512,512]{1,0:T(8,128)(2,1)S(1)}, bf16[512,512]{1,0:T(8,128)(2,1)}, u32[]{:S(2)}) copy-start(bf16[512,512]{1,0:T(8,128)(2,1)} %param.15) | copy-start | bytes 1572868
  95.7 293.6 %all-to-all-start.1 = ((bf16[64,16,512]{2,1,0:T(8,128)(2,1)}), bf16[64,16,512]{2,1,0:T(8,128)(2,1)S(1)}, u32[]{:S(2)}, u32[]{:S(2)}) async-start(bf16[64,16,512]{2,1,0:T(8,128)(2,1)} %fusion.15), calls=%async_computation.1 | async-start | bytes 2097152 | tf_op jit(solution)/shard_map/all_to_all | solution.py:46
  390.8 0.7 copy-start.4
Sparse Core Ops, SparseCore 0:
  94.5 289.8 all-reduce.2
where the time goes:
time: 400 us; the launch traced here: 398 us
  waiting for transfers between devices  165 us (41%)
  blocking collectives  123 us (31%)
  local copies, waits for them, and re-layouts  42.7 us (11%)
  other arithmetic  23.9 us (6%)
  starting transfers between devices  18.4 us (5%)
  between operations  14.4 us (4%)
  matrix products  11.4 us (3%)
    psum x1, waiting for transfers between devices, per_device(): lax.psum((send_term, recv_term, node_term, bias_term), ('dp', 'space'))  156 us
    psum x1, blocking collectives, per_device(): lax.psum((send_term, recv_term, node_term, bias_term), ('dp', 'space'))  123 us
    all_to_all x1, starting transfers between devices, fetch_halo(): lax.all_to_all(buffer, 'space', split_axis=0, concat_axis=0, tiled=True)  11.8 us
    mul x2, local copies, waits for them, and re-layouts, per_device(): edge_grad = (agg_grad[:, None, :] * silu_slope(preact)).astype(jnp.bfloat16)  8.7 us
    add x2, local copies, waits for them, and re-layouts, per_device(): sent_proj[sender_slot].reshape(count_grid, 3, width) + recv_proj[:, None, :]  8.68 us
    all_to_all x1, waiting for transfers between devices, fetch_halo(): lax.all_to_all(buffer, 'space', split_axis=0, concat_axis=0, tiled=True)  8.41 us
    reduce_sum x1, other arithmetic, per_device(): jnp.sum(edge_grad, axis=1, dtype=jnp.float32).astype(jnp.bfloat16)  8.07 us
  transfers between devices with their start and end apart: 3, of which 2 were waited for; matrix products, arithmetic and copies ran while one was open for 7% of the time, Pallas kernels for 0%

commit v1 on v0

v1 whole, which is shorter than its diff:
```python
import jax
import jax.numpy as jnp
from jax import lax
from jax.sharding import Mesh, PartitionSpec as P

SPACE = ("y", "x", "core")
BF = jnp.bfloat16
F32 = jnp.float32


def dot_bf16(left, right, left_dim, right_dim):
    return lax.dot_general(
        left.astype(BF),
        right.astype(BF),
        (((left_dim,), (right_dim,)), ((), ())),
        preferred_element_type=F32,
    )


def shift_space(value, offset):
    pieces = lax.axis_size(SPACE)
    return lax.ppermute(value, SPACE, [(i, (i + offset) % pieces) for i in range(pieces)])


def swap_cores(value):
    return lax.ppermute(value, "core", [(0, 1), (1, 0)])


def exchange(value, axes):
    return lax.all_to_all(value, axes, split_axis=0, concat_axis=0, tiled=True)


def gather_pieces(value, axes):
    spread = jnp.broadcast_to(value[None], (lax.axis_size(axes),) + value.shape)
    return exchange(spread, axes)


def reduce_weights(terms, bias, factor):
    core = lax.axis_index("core")
    halves = terms.reshape(2, 768, 512)
    mine = lax.dynamic_index_in_dim(halves, core, 0, keepdims=False)
    other = lax.dynamic_index_in_dim(halves, 1 - core, 0, keepdims=False)
    bias_low = jnp.broadcast_to(bias.astype(BF)[None], (8, 512))
    came = swap_cores(jnp.concatenate([other.astype(BF), bias_low], axis=0)).astype(F32)
    pair = (mine + came[:768]).astype(BF)
    pair_bias = (bias_low.astype(F32) + came[768:]).astype(BF)
    packed = jnp.concatenate(
        [pair.reshape(4, 192, 512), jnp.broadcast_to(pair_bias[None], (4, 8, 512))], axis=1
    )
    line = jnp.sum(exchange(packed, "x").astype(F32), axis=0)
    line_terms = line[:192].astype(BF).reshape(64, 12, 128)
    line_bias = line[192].astype(BF).reshape(1, 4, 128)
    packed = jnp.concatenate(
        [line_terms, jnp.broadcast_to(line_bias, (64, 4, 128))], axis=1
    )
    total = jnp.sum(exchange(packed, ("dp", "y")).astype(F32), axis=0) * factor
    grad_bias = total[12:].reshape(512)
    plane = gather_pieces(total[:12].astype(BF), ("dp", "y")).reshape(192, 512)
    half = gather_pieces(plane, "x").reshape(768, 512)
    partner = swap_cores(half)
    first = jnp.where(core == 0, half, partner)
    second = jnp.where(core == 0, partner, half)
    whole = jnp.concatenate([first, second], axis=0)
    return whole[:512], whole[512:1024], whole[1024:], grad_bias


def per_device(
    mesh_latent, grid_latent, cotangent, sender_slot, send_rows, w_send, w_recv, w_node, edge_bias
):
    mesh_rows = mesh_latent[0]
    grid_rows = grid_latent[0]
    upstream = cotangent[0]
    send_list = send_rows[0]
    count_mesh, width = mesh_rows.shape
    count_grid = grid_rows.shape[0]
    pieces = lax.axis_size(SPACE)
    offsets = (1, -1, max(2, pieces // 8), pieces // 2)
    pick = (
        send_list.reshape(-1)[:, None] == jnp.arange(count_mesh, dtype=jnp.int32)[None, :]
    ).astype(BF)
    outgoing = dot_bf16(pick, mesh_rows, 1, 0).astype(BF).reshape(4, -1, width)
    arrived = [shift_space(outgoing[j], offsets[j]) for j in range(4)]
    recv_proj = dot_bf16(grid_rows, w_recv, 1, 0)
    agg_grad = dot_bf16(upstream, w_node, 1, 1)
    known = jnp.concatenate([mesh_rows] + arrived, axis=0)
    sent_proj = dot_bf16(known, w_send, 1, 0)
    preact = (
        sent_proj[sender_slot].reshape(count_grid, 3, width) + recv_proj[:, None, :] + edge_bias
    )
    sigmoid = jax.nn.sigmoid(preact)
    aggregate = jnp.sum(preact * sigmoid, axis=1).astype(BF)
    slope = sigmoid * (1.0 + preact * (1.0 - sigmoid))
    edge_grad = (agg_grad[:, None, :] * slope).astype(BF)
    edge_flat = edge_grad.reshape(-1, width)
    recv_grad = jnp.sum(edge_grad, axis=1, dtype=F32).astype(BF)
    slot_table = (
        sender_slot[:, None] == jnp.arange(known.shape[0], dtype=jnp.int32)[None, :]
    ).astype(BF)
    slot_grad = dot_bf16(slot_table, edge_flat, 0, 0)
    send_term = dot_bf16(known, slot_grad, 0, 0)
    recv_term = dot_bf16(grid_rows, recv_grad, 0, 0)
    node_term = dot_bf16(aggregate, upstream, 0, 0)
    bias_term = jnp.sum(edge_flat, axis=0, dtype=F32)
    factor = float(lax.axis_size("dp") * pieces * count_grid) ** (-0.5)
    grad_w_send, grad_w_recv, grad_w_node, grad_bias = reduce_weights(
        jnp.concatenate([send_term, recv_term, node_term], axis=0), bias_term, factor
    )
    leaving = slot_grad[count_mesh:].astype(BF).reshape(4, -1, width)
    returned = jnp.concatenate(
        [shift_space(leaving[j], -offsets[j]) for j in range(4)], axis=0
    )
    sender_grad = slot_grad[:count_mesh] + dot_bf16(pick, returned, 0, 0)
    grad_mesh = dot_bf16(sender_grad, w_send, 1, 1)
    grad_grid = (upstream.astype(F32) + dot_bf16(recv_grad, w_recv, 1, 1)).astype(BF)
    return (grad_mesh[None], grad_grid[None], grad_w_send, grad_w_recv, grad_w_node, grad_bias)


def solution(mesh):
    fine = Mesh(mesh.devices.reshape(8, 8, 4, 2), ("dp",) + SPACE)
    placed = (
        P("dp", SPACE, None),
        P("dp", SPACE, None),
        P("dp", SPACE, None),
        P(SPACE),
        P(SPACE, None, None),
        P(),
        P(),
        P(),
        P(),
    )
    return jax.shard_map(
        per_device,
        mesh=fine,
        in_specs=placed,
        out_specs=(P("dp", SPACE, None), P("dp", SPACE, None), P(), P(), P(), P()),
        check_vma=False,
    )
```

time: 400 us -> 192 us (0.48)
  waiting for transfers between devices: 165 us -> 12.1 us
  blocking collectives: 123 us -> 58.8 us
  starting transfers between devices: 18.4 us -> 45.1 us
  between operations: 14.4 us -> 1.04 us
  local copies, waits for them, and re-layouts: 42.7 us -> 37.6 us
    psum x1 -> x0, waiting for transfers between devices: 156 us -> none  [per_device(): lax.psum((send_term, recv_term, node_term, bias_term), ('dp', 'space'))]
    psum x1 -> x0, blocking collectives: 123 us -> none  [per_device(): lax.psum((send_term, recv_term, node_term, bias_term), ('dp', 'space'))]
    all_to_all x0 -> x3, blocking collectives: none -> 58.8 us  [exchange(): return lax.all_to_all(value, axes, split_axis=0, concat_axis=0, tiled=True)]
    ppermute x0 -> x10, starting transfers between devices: none -> 41.6 us  [the longest x8 29.3 us: shift_space(): lax.ppermute(value, SPACE, [(i, (i + offset) % pieces) for i in range(pie...]
    all_to_all x2 -> x1, starting transfers between devices: 18.4 us -> 3.49 us  [exchange(): return lax.all_to_all(value, axes, split_axis=0, concat_axis=0, tiled=True)]
    dynamic_update_slice x8 -> x0, local copies, waits for them, and re-layouts: 7.91 us -> none  [the longest x4 5.52 us: return_halo(): lax.dynamic_update_slice(buffer, values[block_index][None], (target, jnp....]
    unnamed x32 -> x28, local copies, waits for them, and re-layouts: 0.77 us -> 5.06 us
    dot_general x9 -> x10, matrix products: 11.4 us -> 12.7 us  [dot_bf16(): lax.dot_general(left.astype(BF), right.astype(BF), (((left_dim,), (right_...]
  transfers between devices with their start and end apart: 3 -> 11, of which waited for: 2 -> 3; matrix products, arithmetic and copies ran while one was open for 7% -> 15% of each run, Pallas kernels for 0% -> 0%
where the time goes in v1:
time: 192 us; the launch traced here: 190 us
  blocking collectives  58.8 us (31%)
  starting transfers between devices  45.1 us (23%)
  local copies, waits for them, and re-layouts  37.6 us (20%)
  other arithmetic  22.9 us (12%)
  matrix products  12.7 us (7%)
  waiting for transfers between devices  12.1 us (6%)
    all_to_all x3, blocking collectives, exchange(): return lax.all_to_all(value, axes, split_axis=0, concat_axis=0, tiled=True)  58.8 us
    ppermute x8, starting transfers between devices, shift_space(): lax.ppermute(value, SPACE, [(i, (i + offset) % pieces) for i in range(pie...  29.3 us
    dot_general x10, matrix products, dot_bf16(): lax.dot_general(left.astype(BF), right.astype(BF), (((left_dim,), (right_...  12.7 us
    ppermute x2, starting transfers between devices, swap_cores(): return lax.ppermute(value, 'core', [(0, 1), (1, 0)])  12.3 us
    mul x2, local copies, waits for them, and re-layouts, per_device(): edge_grad = (agg_grad[:, None, :] * slope).astype(BF)  8.75 us
    add x2, local copies, waits for them, and re-layouts, per_device(): sent_proj[sender_slot].reshape(count_grid, 3, width) + recv_proj[:, None, :]  8.62 us
    all_to_all x1, waiting for transfers between devices, exchange(): return lax.all_to_all(value, axes, split_axis=0, concat_axis=0, tiled=True)  8.55 us
    reduce_sum x1, other arithmetic, per_device(): recv_grad = jnp.sum(edge_grad, axis=1, dtype=F32).astype(BF)  8.07 us
  transfers between devices with their start and end apart: 11, of which 3 were waited for; matrix products, arithmetic and copies ran while one was open for 15% of the time, Pallas kernels for 0%

profile of v1, /device:TPU:1, one launch (start us, length us, event | category | flops | bytes accessed | tf_op | source)
XLA Modules:
  0.0 190.3 jit_solution(8474439690218575963)
XLA Ops:
  2.6 4.5 %collective-permute-start = (bf16[16,512]{1,0:T(8,128)(2,1)S(1)}, bf16[16,512]{1,0:T(8,128)(2,1)S(1)}, u32[]{:S(2)}, u32[]{:S(2)}) collective-permute-start(bf16[16,512]{1,0:T(8,128)(2,1)S(1)} %get-tuple-element.20), channel_id=1, source_target_pairs={{0,1},{1,2},{2,3},{3,4},{4,5},{5,6},{6,7},{7,8},{8,9},{9,10},{10,1... | collective-permute-start | bytes 49160 | tf_op jit(solution)/shard_map/ppermute | solution.py:22
  7.1 6.2 %collective-permute-start.1 = (bf16[16,512]{1,0:T(8,128)(2,1)S(1)}, bf16[16,512]{1,0:T(8,128)(2,1)S(1)}, u32[]{:S(2)}, u32[]{:S(2)}) collective-permute-start(bf16[16,512]{1,0:T(8,128)(2,1)S(1)} %get-tuple-element.19), channel_id=1, source_target_pairs={{0,63},{1,0},{2,1},{3,2},{4,3},{5,4},{6,5},{7,6},{8,7},{9,8},{10,9... | collective-permute-start | bytes 49160 | tf_op jit(solution)/shard_map/ppermute | solution.py:22
  13.3 1.9 %collective-permute-start.2 = (bf16[16,512]{1,0:T(8,128)(2,1)S(1)}, bf16[16,512]{1,0:T(8,128)(2,1)S(1)}, u32[]{:S(2)}, u32[]{:S(2)}) collective-permute-start(bf16[16,512]{1,0:T(8,128)(2,1)S(1)} %get-tuple-element.18), channel_id=1, source_target_pairs={{0,8},{1,9},{2,10},{3,11},{4,12},{5,13},{6,14},{7,15},{8,16},{9,17... | collective-permute-start | bytes 49160 | tf_op jit(solution)/shard_map/ppermute | solution.py:22
  15.2 3.6 %collective-permute-start.3 = (bf16[16,512]{1,0:T(8,128)(2,1)S(1)}, bf16[16,512]{1,0:T(8,128)(2,1)S(1)}, u32[]{:S(2)}, u32[]{:S(2)}) collective-permute-start(bf16[16,512]{1,0:T(8,128)(2,1)S(1)} %get-tuple-element.17), channel_id=1, source_target_pairs={{0,32},{1,33},{2,34},{3,35},{4,36},{5,37},{6,38},{7,39},{8,40},{9,... | collective-permute-start | bytes 49160 | tf_op jit(solution)/shard_map/ppermute | solution.py:22
  18.8 1.6 bitcast_dynamic-update-slice_fusion
  22.6 1.7 fusion.13
  24.2 2.7 %add.82 = f32[512,3,512]{2,1,0:T(4,128)} broadcast(f32[512,512]{1,0:T(8,128)S(1)} %fusion.9), dimensions={0,2} | broadcast | bytes 4194304 | tf_op jit(solution)/shard_map/add | solution.py:88
  26.9 5.9 %add.83 = f32[1536,512]{1,0:T(8,128)} reshape(f32[512,3,512]{2,1,0:T(4,128)} %add.82) | data formatting | bytes 6291456 | tf_op jit(solution)/shard_map/add | solution.py:88
  32.9 2.7 %mul.46 = f32[512,3,512]{2,1,0:T(4,128)} broadcast(f32[512,512]{1,0:T(8,128)S(1)} %fusion.13), dimensions={0,2} | broadcast | bytes 4194304 | tf_op jit(solution)/shard_map/mul | solution.py:93
  35.5 6.1 %mul.47 = f32[1536,512]{1,0:T(8,128)} reshape(f32[512,3,512]{2,1,0:T(4,128)} %mul.46) | data formatting | bytes 6291456 | tf_op jit(solution)/shard_map/mul | solution.py:93
  45.3 5.0 %gather_fusion = f32[1536,512]{1,0:T(8,128)} fusion(f32[192,512]{1,0:T(8,128)S(1)} %fusion.43, s32[2048]{0:T(1024)S(1)} %pad_clamp_fusion), kind=kCustom, calls=%fused_computation | custom fusion | bytes 6297600 | tf_op jit(solution)/shard_map/gather | solution.py:88
  50.2 5.8 %reshape.82 = f32[512,3,512]{2,1,0:T(4,128)} reshape(f32[1536,512]{1,0:T(8,128)} %gather_fusion) | data formatting | bytes 6291456 | tf_op jit(solution)/shard_map/reshape | solution.py:88
  56.1 8.1 %fusion = bf16[512,512]{1,0:T(8,128)(2,1)S(1)} fusion(f32[512]{0:T(512)S(1)} %copy-done.10, f32[512,3,512]{2,1,0:T(4,128)} %reshape.82, f32[512,512]{1,0:T(8,128)S(1)} %fusion.9, f32[512,512]{1,0:T(8,128)S(1)} %fusion.13), kind=kLoop, calls=%fused_computation.7 | loop fusion | flops 9175040 | bytes 5769216 | tf_op jit(solution)/shard_map/reduce_sum | solution.py:95
  64.2 4.7 %multiply_reduce_fusion = bf16[512,512]{1,0:T(8,128)(2,1)S(1)} fusion(f32[512,3,512]{2,1,0:T(4,128)S(1)} %copy-done.1, f32[512]{0:T(512)S(1)} %copy-done.10, f32[512,512]{1,0:T(8,128)S(1)} %fusion.9), kind=kLoop, calls=%fused_computation.1 | loop fusion | flops 5242880 | bytes 4720640 | tf_op jit(solution)/shard_map/reduce_sum | solution.py:91
  68.8 3.3 %fusion.38 = (bf16[512]{0:T(512)(128)(2,1)S(1)}, bf16[1536,512]{1,0:T(8,128)(2,1)S(1)}) fusion(f32[1536,512]{1,0:T(8,128)} %mul.47, f32[512]{0:T(512)S(1)} %copy-done.10, f32[1536,512]{1,0:T(8,128)S(1)} %copy-done.2, f32[1536,512]{1,0:T(8,128)S(1)} %copy-done.3), kind=kLoop, calls=%fused_computation.64 | loop fusion | flops 9436672 | bytes 11013120 | tf_op jit(solution)/shard_map/reduce_sum | solution.py:103
  72.1 1.6 fusion.42
  76.4 1.6 copy-done.4
  78.2 5.8 %collective-permute-start.8 = (bf16[776,512]{1,0:T(8,128)(2,1)S(1)}, bf16[776,512]{1,0:T(8,128)(2,1)}, u32[]{:S(2)}, u32[]{:S(2)}) collective-permute-start(bf16[776,512]{1,0:T(8,128)(2,1)S(1)} %pad_maximum_fusion.2), channel_id=1, source_target_pairs={{0,1},{1,0},{2,3},{3,2},{4,5},{5,4},{6,7},{7,6},{8,9},{9,8},{10,11... | collective-permute-start | bytes 2383880 | tf_op jit(solution)/shard_map/ppermute | solution.py:26
  84.0 2.0 %collective-permute-done.8 = bf16[776,512]{1,0:T(8,128)(2,1)} collective-permute-done((bf16[776,512]{1,0:T(8,128)(2,1)S(1)}, bf16[776,512]{1,0:T(8,128)(2,1)}, u32[]{:S(2)}, u32[]{:S(2)}) %collective-permute-start.8) | collective-permute-done | bytes 794656 | tf_op jit(solution)/shard_map/ppermute | solution.py:26
  87.3 1.7 fusion.1
  89.1 14.6 %all_to_all.20 = bf16[4,200,512]{2,1,0:T(8,128)(2,1)S(1)} all-to-all(bf16[4,200,512]{2,1,0:T(8,128)(2,1)S(1)} %pad_maximum_fusion.1), channel_id=1, replica_groups=mesh['dp'=8,'y'=8,'x'=4,'core'=2] {'x'}, dimensions={0} | all-to-all | bytes 1638400 | tf_op jit(solution)/shard_map/all_to_all | solution.py:30
  104.3 26.0 %all_to_all.21 = bf16[64,16,128]{2,1,0:T(8,128)(2,1)S(1)} all-to-all(bf16[64,16,128]{2,1,0:T(8,128)(2,1)S(1)} %pad_maximum_fusion.4), channel_id=1, replica_groups=mesh['dp'=8,'y'=8,'x'=4,'core'=2] {'dp','y'}, dimensions={0} | all-to-all | bytes 524288 | tf_op jit(solution)/shard_map/all_to_all | solution.py:30
  130.5 18.1 %all_to_all.22 = bf16[64,12,128]{2,1,0:T(8,128)(2,1)S(1)} all-to-all(bf16[64,12,128]{2,1,0:T(8,128)(2,1)S(1)} %broadcast_in_dim.54), channel_id=1, replica_groups=mesh['dp'=8,'y'=8,'x'=4,'core'=2] {'dp','y'}, dimensions={0} | all-to-all | bytes 393216 | tf_op jit(solution)/shard_map/all_to_all | solution.py:30
  149.8 3.5 %all-to-all-start.3 = ((bf16[4,192,512]{2,1,0:T(8,128)(2,1)}), bf16[4,192,512]{2,1,0:T(8,128)(2,1)S(1)}, u32[]{:S(2)}, u32[]{:S(2)}) async-start(bf16[4,192,512]{2,1,0:T(8,128)(2,1)} %broadcast_in_dim.56), calls=%async_computation.3 | async-start | bytes 1572864 | tf_op jit(solution)/shard_map/all_to_all | solution.py:30
  153.3 8.5 %all-to-all-done.3 = bf16[4,192,512]{2,1,0:T(8,128)(2,1)S(1)} async-done(((bf16[4,192,512]{2,1,0:T(8,128)(2,1)}), bf16[4,192,512]{2,1,0:T(8,128)(2,1)S(1)}, u32[]{:S(2)}, u32[]{:S(2)}) %all-to-all-start.3) | async-done | bytes 786464 | tf_op jit(solution)/shard_map/all_to_all | solution.py:30
  161.8 6.5 %collective-permute-start.9 = (bf16[768,512]{1,0:T(8,128)(2,1)S(1)}, bf16[768,512]{1,0:T(8,128)(2,1)}, u32[]{:S(2)}, u32[]{:S(2)}) collective-permute-start(bf16[768,512]{1,0:T(8,128)(2,1)S(1)} %bitcast.48), channel_id=1, source_target_pairs={{0,1},{1,0},{2,3},{3,2},{4,5},{5,4},{6,7},{7,6},{8,9},{9,8},{10,11... | collective-permute-start | bytes 2359304 | tf_op jit(solution)/shard_map/ppermute | solution.py:26
  169.1 1.9 %collective-permute-start.4 = (bf16[16,512]{1,0:T(8,128)(2,1)S(1)}, bf16[16,512]{1,0:T(8,128)(2,1)S(1)}, u32[]{:S(2)}, u32[]{:S(2)}) collective-permute-start(bf16[16,512]{1,0:T(8,128)(2,1)S(1)} %get-tuple-element.13), channel_id=1, source_target_pairs={{0,63},{1,0},{2,1},{3,2},{4,3},{5,4},{6,5},{7,6},{8,7},{9,8},{10,9... | collective-permute-start | bytes 49160 | tf_op jit(solution)/shard_map/ppermute | solution.py:22
  171.1 3.6 %collective-permute-start.5 = (bf16[16,512]{1,0:T(8,128)(2,1)S(1)}, bf16[16,512]{1,0:T(8,128)(2,1)S(1)}, u32[]{:S(2)}, u32[]{:S(2)}) collective-permute-start(bf16[16,512]{1,0:T(8,128)(2,1)S(1)} %get-tuple-element.16), channel_id=1, source_target_pairs={{0,1},{1,2},{2,3},{3,4},{4,5},{5,6},{6,7},{7,8},{8,9},{9,10},{10,1... | collective-permute-start | bytes 49160 | tf_op jit(solution)/shard_map/ppermute | solution.py:22
  174.7 1.9 %collective-permute-start.6 = (bf16[16,512]{1,0:T(8,128)(2,1)S(1)}, bf16[16,512]{1,0:T(8,128)(2,1)S(1)}, u32[]{:S(2)}, u32[]{:S(2)}) collective-permute-start(bf16[16,512]{1,0:T(8,128)(2,1)S(1)} %get-tuple-element.15), channel_id=1, source_target_pairs={{0,56},{1,57},{2,58},{3,59},{4,60},{5,61},{6,62},{7,63},{8,0},{9,1... | collective-permute-start | bytes 49160 | tf_op jit(solution)/shard_map/ppermute | solution.py:22
  176.6 5.6 %collective-permute-start.7 = (bf16[16,512]{1,0:T(8,128)(2,1)S(1)}, bf16[16,512]{1,0:T(8,128)(2,1)S(1)}, u32[]{:S(2)}, u32[]{:S(2)}) collective-permute-start(bf16[16,512]{1,0:T(8,128)(2,1)S(1)} %get-tuple-element.14), channel_id=1, source_target_pairs={{0,32},{1,33},{2,34},{3,35},{4,36},{5,37},{6,38},{7,39},{8,40},{9,... | collective-permute-start | bytes 49160 | tf_op jit(solution)/shard_map/ppermute | solution.py:22
  183.6 1.5 collective-permute-done.7
  185.1 2.1 %convolution_bitcast_fusion.1 = f32[1,128,512]{2,1,0:T(8,128)} fusion(bf16[512,512]{1,0:T(8,128)(2,1)S(1)} %copy-done.7, f32[192,512]{1,0:T(8,128)} %get-tuple-element.22, bf16[16,512]{1,0:T(8,128)(2,1)S(1)} %collective-permute-done.7, bf16[16,512]{1,0:T(8,128)(2,1)S(1)} %collective-permute-done.6, bf16[16,512]{1,0:T(8,128)(2,1)S(1)} %collective-permute-done.5, ...), kind=kOutput, calls=%fused_computation.17 | convolution fusion | flops 75898880 | bytes 1114368 | tf_op jit(solution)/shard_map/dot_general | solution.py:12
  (71 shorter events, 18.8 us)
Async XLA Ops:
  0.6 20.4 %copy-start = (bf16[1,512,512]{2,1,0:T(8,128)(2,1)S(1)}, bf16[1,512,512]{2,1,0:T(8,128)(2,1)}, u32[]{:S(2)}) copy-start(bf16[1,512,512]{2,1,0:T(8,128)(2,1)} %param.10) | copy-start | bytes 1572868
  2.6 39.0 %collective-permute-start = (bf16[16,512]{1,0:T(8,128)(2,1)S(1)}, bf16[16,512]{1,0:T(8,128)(2,1)S(1)}, u32[]{:S(2)}, u32[]{:S(2)}) collective-permute-start(bf16[16,512]{1,0:T(8,128)(2,1)S(1)} %get-tuple-element.20), channel_id=1, source_target_pairs={{0,1},{1,2},{2,3},{3,4},{4,5},{5,6},{6,7},{7,8},{8,9},{9,10},{10,1... | collective-permute-start | bytes 49160 | tf_op jit(solution)/shard_map/ppermute | solution.py:22
  7.1 35.1 %collective-permute-start.1 = (bf16[16,512]{1,0:T(8,128)(2,1)S(1)}, bf16[16,512]{1,0:T(8,128)(2,1)S(1)}, u32[]{:S(2)}, u32[]{:S(2)}) collective-permute-start(bf16[16,512]{1,0:T(8,128)(2,1)S(1)} %get-tuple-element.19), channel_id=1, source_target_pairs={{0,63},{1,0},{2,1},{3,2},{4,3},{5,4},{6,5},{7,6},{8,7},{9,8},{10,9... | collective-permute-start | bytes 49160 | tf_op jit(solution)/shard_map/ppermute | solution.py:22
  13.3 29.5 %collective-permute-start.2 = (bf16[16,512]{1,0:T(8,128)(2,1)S(1)}, bf16[16,512]{1,0:T(8,128)(2,1)S(1)}, u32[]{:S(2)}, u32[]{:S(2)}) collective-permute-start(bf16[16,512]{1,0:T(8,128)(2,1)S(1)} %get-tuple-element.18), channel_id=1, source_target_pairs={{0,8},{1,9},{2,10},{3,11},{4,12},{5,13},{6,14},{7,15},{8,16},{9,17... | collective-permute-start | bytes 49160 | tf_op jit(solution)/shard_map/ppermute | solution.py:22
  15.2 28.2 %collective-permute-start.3 = (bf16[16,512]{1,0:T(8,128)(2,1)S(1)}, bf16[16,512]{1,0:T(8,128)(2,1)S(1)}, u32[]{:S(2)}, u32[]{:S(2)}) collective-permute-start(bf16[16,512]{1,0:T(8,128)(2,1)S(1)} %get-tuple-element.17), channel_id=1, source_target_pairs={{0,32},{1,33},{2,34},{3,35},{4,36},{5,37},{6,38},{7,39},{8,40},{9,... | collective-permute-start | bytes 49160 | tf_op jit(solution)/shard_map/ppermute | solution.py:22
  35.5 8.5 %copy-start.6 = (bf16[512,512]{1,0:T(8,128)(2,1)S(1)}, bf16[512,512]{1,0:T(8,128)(2,1)}, u32[]{:S(2)}) copy-start(bf16[512,512]{1,0:T(8,128)(2,1)} %param.14) | copy-start | bytes 1572868
  50.2 5.8 %copy-start.10 = (f32[512]{0:T(512)S(1)}, f32[512]{0:T(512)}, u32[]{:S(2)}) copy-start(f32[512]{0:T(512)} %param.17) | copy-start | bytes 6148
  56.1 8.1 %copy-start.1 = (f32[512,3,512]{2,1,0:T(4,128)S(1)}, f32[512,3,512]{2,1,0:T(4,128)}, u32[]{:S(2)}) copy-start(f32[512,3,512]{2,1,0:T(4,128)} %reshape.82) | copy-start | bytes 9437188
  56.1 12.8 %copy-start.3 = (f32[1536,512]{1,0:T(8,128)S(1)}, f32[1536,512]{1,0:T(8,128)}, u32[]{:S(2)}) copy-start(f32[1536,512]{1,0:T(8,128)} %add.83) | copy-start | bytes 9437188
  64.1 4.7 %copy-start.2 = (f32[1536,512]{1,0:T(8,128)S(1)}, f32[1536,512]{1,0:T(8,128)}, u32[]{:S(2)}) copy-start(f32[1536,512]{1,0:T(8,128)} %gather_fusion) | copy-start | bytes 9437188
  68.8 3.3 %copy-start.11 = (s32[1536]{0:T(1024)S(1)}, s32[1536]{0:T(1024)}, u32[]{:S(2)}) copy-start(s32[1536]{0:T(1024)} %param.12) | copy-start | bytes 18436
  72.1 3.5 %copy-start.5 = (bf16[1,512,512]{2,1,0:T(8,128)(2,1)S(1)}, bf16[1,512,512]{2,1,0:T(8,128)(2,1)}, u32[]{:S(2)}) copy-start(bf16[1,512,512]{2,1,0:T(8,128)(2,1)} %param.11) | copy-start | bytes 1572868
  73.8 2.6 %copy-start.9 = (bf16[192,512]{1,0:T(8,128)(2,1)}, bf16[192,512]{1,0:T(8,128)(2,1)S(1)}, u32[]{:S(2)}) copy-start(bf16[192,512]{1,0:T(8,128)(2,1)S(1)} %get-tuple-element.21) | copy-start | bytes 589828
  76.4 1.6 copy-start.4
  78.2 7.8 %collective-permute-start.8 = (bf16[776,512]{1,0:T(8,128)(2,1)S(1)}, bf16[776,512]{1,0:T(8,128)(2,1)}, u32[]{:S(2)}, u32[]{:S(2)}) collective-permute-start(bf16[776,512]{1,0:T(8,128)(2,1)S(1)} %pad_maximum_fusion.2), channel_id=1, source_target_pairs={{0,1},{1,0},{2,3},{3,2},{4,5},{5,4},{6,7},{7,6},{8,9},{9,8},{10,11... | collective-permute-start | bytes 2383880 | tf_op jit(solution)/shard_map/ppermute | solution.py:26
  103.9 78.3 %copy-start.8 = (bf16[512,512]{1,0:T(8,128)(2,1)S(1)}, bf16[512,512]{1,0:T(8,128)(2,1)}, u32[]{:S(2)}) copy-start(bf16[512,512]{1,0:T(8,128)(2,1)} %param.15) | copy-start | bytes 1572868
  130.4 54.7 %copy-start.7 = (bf16[512,512]{1,0:T(8,128)(2,1)S(1)}, bf16[512,512]{1,0:T(8,128)(2,1)}, u32[]{:S(2)}) copy-start(bf16[512,512]{1,0:T(8,128)(2,1)} %param.14) | copy-start | bytes 1572868
  149.8 12.1 %all-to-all-start.3 = ((bf16[4,192,512]{2,1,0:T(8,128)(2,1)}), bf16[4,192,512]{2,1,0:T(8,128)(2,1)S(1)}, u32[]{:S(2)}, u32[]{:S(2)}) async-start(bf16[4,192,512]{2,1,0:T(8,128)(2,1)} %broadcast_in_dim.56), calls=%async_computation.3 | async-start | bytes 1572864 | tf_op jit(solution)/shard_map/all_to_all | solution.py:30
  161.8 26.0 %collective-permute-start.9 = (bf16[768,512]{1,0:T(8,128)(2,1)S(1)}, bf16[768,512]{1,0:T(8,128)(2,1)}, u32[]{:S(2)}, u32[]{:S(2)}) collective-permute-start(bf16[768,512]{1,0:T(8,128)(2,1)S(1)} %bitcast.48), channel_id=1, source_target_pairs={{0,1},{1,0},{2,3},{3,2},{4,5},{5,4},{6,7},{7,6},{8,9},{9,8},{10,11... | collective-permute-start | bytes 2359304 | tf_op jit(solution)/shard_map/ppermute | solution.py:26
  169.1 14.4 %collective-permute-start.4 = (bf16[16,512]{1,0:T(8,128)(2,1)S(1)}, bf16[16,512]{1,0:T(8,128)(2,1)S(1)}, u32[]{:S(2)}, u32[]{:S(2)}) collective-permute-start(bf16[16,512]{1,0:T(8,128)(2,1)S(1)} %get-tuple-element.13), channel_id=1, source_target_pairs={{0,63},{1,0},{2,1},{3,2},{4,3},{5,4},{6,5},{7,6},{8,7},{9,8},{10,9... | collective-permute-start | bytes 49160 | tf_op jit(solution)/shard_map/ppermute | solution.py:22
  171.1 12.5 %collective-permute-start.5 = (bf16[16,512]{1,0:T(8,128)(2,1)S(1)}, bf16[16,512]{1,0:T(8,128)(2,1)S(1)}, u32[]{:S(2)}, u32[]{:S(2)}) collective-permute-start(bf16[16,512]{1,0:T(8,128)(2,1)S(1)} %get-tuple-element.16), channel_id=1, source_target_pairs={{0,1},{1,2},{2,3},{3,4},{4,5},{5,6},{6,7},{7,8},{8,9},{9,10},{10,1... | collective-permute-start | bytes 49160 | tf_op jit(solution)/shard_map/ppermute | solution.py:22
  174.7 8.8 %collective-permute-start.6 = (bf16[16,512]{1,0:T(8,128)(2,1)S(1)}, bf16[16,512]{1,0:T(8,128)(2,1)S(1)}, u32[]{:S(2)}, u32[]{:S(2)}) collective-permute-start(bf16[16,512]{1,0:T(8,128)(2,1)S(1)} %get-tuple-element.15), channel_id=1, source_target_pairs={{0,56},{1,57},{2,58},{3,59},{4,60},{5,61},{6,62},{7,63},{8,0},{9,1... | collective-permute-start | bytes 49160 | tf_op jit(solution)/shard_map/ppermute | solution.py:22
  176.6 8.5 %collective-permute-start.7 = (bf16[16,512]{1,0:T(8,128)(2,1)S(1)}, bf16[16,512]{1,0:T(8,128)(2,1)S(1)}, u32[]{:S(2)}, u32[]{:S(2)}) collective-permute-start(bf16[16,512]{1,0:T(8,128)(2,1)S(1)} %get-tuple-element.14), channel_id=1, source_target_pairs={{0,32},{1,33},{2,34},{3,35},{4,36},{5,37},{6,38},{7,39},{8,40},{9,... | collective-permute-start | bytes 49160 | tf_op jit(solution)/shard_map/ppermute | solution.py:22

commit v2 on v1

v2 whole, which is shorter than its diff:
```python
import jax
import jax.numpy as jnp
from jax import lax
from jax.experimental import pallas as pl
from jax.experimental.pallas import tpu as pltpu
from jax.sharding import Mesh, PartitionSpec as P

BF = jnp.bfloat16
F32 = jnp.float32


def rows_dot(left, right):
    return lax.dot_general(left, right, (((0,), (0,)), ((), ())), preferred_element_type=F32)


def half_terms(start, known_ref, slot_ref, grid_ref, recv_ref, node_ref, upstream_ref, out_ref):
    span = pl.ds(pl.multiple_of(start, 256), 256)
    pairs = ((known_ref, slot_ref), (grid_ref, recv_ref), (node_ref, upstream_ref))
    for index, (left_ref, right_ref) in enumerate(pairs):
        product = rows_dot(left_ref[:, span], right_ref[...])
        out_ref[index * 256 : (index + 1) * 256, :] = product.astype(out_ref.dtype)


def edge_kernel(
    core_ref, column_ref, row_ref, mesh_ref, h0_ref, h1_ref, h2_ref, h3_ref, recv_proj_ref, agg_grad_ref,
    w_send_ref, grid_ref, upstream_ref,
    send_ref, known_ref, slot_ref, recv_ref, node_ref, local_ref,
    table_ref, preact_ref, edge_ref, bias_ref,
):
    known_ref[0:128, :] = mesh_ref[...]
    for j, halo_ref in enumerate((h0_ref, h1_ref, h2_ref, h3_ref)):
        known_ref[128 + 16 * j : 144 + 16 * j, :] = halo_ref[...]
    sent = jnp.dot(known_ref[...], w_send_ref[...], preferred_element_type=F32)
    high = sent.astype(BF)
    table_ref[0:192, :] = high
    table_ref[192:384, :] = (sent - high.astype(F32)).astype(BF)
    lane = lax.broadcasted_iota(jnp.int32, (512, 384), 1)
    lane = jnp.where(lane >= 192, lane - 192, lane)
    for k in range(3):
        pick = (lane == column_ref[:, k : k + 1]).astype(F32).astype(BF)
        preact_ref[k * 512 : (k + 1) * 512, :] = jnp.dot(
            pick, table_ref[...], preferred_element_type=F32
        )
    bias_ref[...] = jnp.zeros_like(bias_ref)

    def chunk(step, carry):
        rows = pl.ds(pl.multiple_of(step * 16, 16), 16)
        recv_proj = recv_proj_ref[rows, :]
        agg_grad = agg_grad_ref[rows, :]
        node = jnp.zeros((16, 512), F32)
        recv = jnp.zeros((16, 512), F32)
        for k in range(3):
            edge_rows = pl.ds(pl.multiple_of(step * 16 + k * 512, 16), 16)
            preact = preact_ref[edge_rows, :] + recv_proj
            sigmoid = 0.5 * jnp.tanh(0.5 * preact) + 0.5
            silu = preact * sigmoid
            node += silu
            edge = (agg_grad * (sigmoid + silu * (1.0 - sigmoid))).astype(BF)
            edge_ref[edge_rows, :] = edge
            recv += edge.astype(F32)
        node_ref[rows, :] = node.astype(BF)
        recv_ref[rows, :] = recv.astype(BF)
        bias_ref[...] += recv[0:8] + recv[8:16]
        return carry

    lax.fori_loop(0, 32, chunk, 0)
    sublane = lax.broadcasted_iota(jnp.int32, (192, 1536), 0)
    spread = (sublane == row_ref[...]).astype(F32).astype(BF)
    slots = jnp.dot(spread, edge_ref[...], preferred_element_type=F32)
    local_ref[...] = slots[0:128]
    slot_ref[...] = slots.astype(BF)
    half_terms((1 - core_ref[0]) * 256, known_ref, slot_ref, grid_ref, recv_ref, node_ref, upstream_ref, send_ref)
    total = jnp.sum(bias_ref[...], axis=0, keepdims=True)
    send_ref[768:784, :] = jnp.broadcast_to(total, (16, 512)).astype(BF)
    leaving = pl.ds(pl.multiple_of(144 - 16 * core_ref[0], 16), 16)
    send_ref[784:800, :] = slot_ref[leaving, :]


def keep_kernel(core_ref, known_ref, slot_ref, grid_ref, recv_ref, node_ref, upstream_ref, keep_ref):
    half_terms(core_ref[0] * 256, known_ref, slot_ref, grid_ref, recv_ref, node_ref, upstream_ref, keep_ref)


VM = pl.BlockSpec(memory_space=pltpu.VMEM)
SM = pl.BlockSpec(memory_space=pltpu.SMEM)
LIMIT = pltpu.CompilerParams(vmem_limit_bytes=40 * 1024 * 1024)


def pack_kernel(keep_ref, came_ref, sent_ref, out_ref):
    bias = (sent_ref[...].astype(F32) + came_ref[768:784, :].astype(F32)).astype(BF)
    for piece in range(4):
        rows = slice(piece * 192, piece * 192 + 192)
        out_ref[piece, 0:192, :] = (keep_ref[rows, :] + came_ref[rows, :].astype(F32)).astype(BF)
        out_ref[piece, 192:208, :] = bias


def shape(rows, dtype):
    return jax.ShapeDtypeStruct((rows, 512), dtype)


def edge_step(*args):
    return pl.pallas_call(
        edge_kernel,
        out_shape=(shape(800, BF), shape(192, BF), shape(192, BF), shape(512, BF), shape(512, BF), shape(128, F32)),
        in_specs=[SM] + [VM] * 12,
        out_specs=(VM,) * 6,
        scratch_shapes=[
            pltpu.VMEM((384, 512), BF),
            pltpu.VMEM((1536, 512), F32),
            pltpu.VMEM((1536, 512), BF),
            pltpu.VMEM((8, 512), F32),
        ],
        compiler_params=LIMIT,
        name="edge_step",
        cost_estimate=pl.CostEstimate(flops=3_000_000_000, bytes_accessed=6_000_000, transcendentals=800_000),
    )(*args)


def keep_step(*args):
    return pl.pallas_call(
        keep_kernel,
        out_shape=shape(768, F32),
        in_specs=[SM] + [VM] * 6,
        out_specs=VM,
        compiler_params=LIMIT,
        name="keep_step",
        cost_estimate=pl.CostEstimate(flops=600_000_000, bytes_accessed=4_000_000, transcendentals=0),
    )(*args)


def pack_step(*args):
    return pl.pallas_call(
        pack_kernel,
        out_shape=jax.ShapeDtypeStruct((4, 208, 512), BF),
        in_specs=[VM] * 3,
        out_specs=VM,
        compiler_params=LIMIT,
        name="pack_step",
        cost_estimate=pl.CostEstimate(flops=500_000, bytes_accessed=3_000_000, transcendentals=0),
    )(*args)


SPACE = ("y", "x", "core")
PLANE = ("dp", "y")


def dot_bf16(left, right, left_dim, right_dim):
    return lax.dot_general(
        left.astype(BF),
        right.astype(BF),
        (((left_dim,), (right_dim,)), ((), ())),
        preferred_element_type=F32,
    )


def shift_space(value, offset):
    pieces = lax.axis_size(SPACE)
    return lax.ppermute(value, SPACE, [(i, (i + offset) % pieces) for i in range(pieces)])


def swap_chips(value):
    pieces = lax.axis_size(SPACE)
    return lax.ppermute(
        value, SPACE, [(i, (i - 1 + 2 * (i % 2)) % pieces) for i in range(pieces)]
    )


def swap_cores(value):
    return lax.ppermute(value, "core", [(0, 1), (1, 0)])


def exchange(value, axes):
    return lax.all_to_all(value, axes, split_axis=0, concat_axis=0, tiled=True)


def gather_pieces(value, axes):
    spread = jnp.broadcast_to(value[None], (lax.axis_size(axes),) + value.shape)
    return exchange(spread, axes)


def per_device(
    mesh_latent, grid_latent, cotangent, sender_slot, send_rows, w_send, w_recv, w_node, edge_bias
):
    mesh_rows = mesh_latent[0]
    grid_rows = grid_latent[0]
    upstream = cotangent[0]
    core = lax.axis_index("core")
    core_ref = core.astype(jnp.int32).reshape(1)
    pieces = lax.axis_size(SPACE)
    offsets = (1, -1, max(2, pieces // 8), pieces // 2)
    pick = (
        send_rows[0].reshape(-1)[:, None] == jnp.arange(128, dtype=jnp.int32)[None, :]
    ).astype(BF)
    outgoing = dot_bf16(pick, mesh_rows, 1, 0).astype(BF).reshape(4, 16, 512)
    halo = [shift_space(outgoing[j], offsets[j]) for j in range(4)]
    recv_proj = dot_bf16(grid_rows, w_recv, 1, 0) + edge_bias
    agg_grad = dot_bf16(upstream, w_node, 1, 1)
    column = sender_slot.reshape(512, 3)
    row = column.T.reshape(1, 1536)
    send, known, slot, recv_grad, node, local = edge_step(
        core_ref, column, row, mesh_rows, *halo, recv_proj, agg_grad, w_send, grid_rows, upstream
    )
    came = swap_cores(send)
    keep = keep_step(core_ref, known, slot, grid_rows, recv_grad, node, upstream)
    packed = pack_step(keep, came, send[768:784])

    line = jnp.sum(exchange(packed, "x").astype(F32), axis=0)
    line_terms = line[:192].astype(BF).reshape(64, 12, 128)
    line_bias = line[192].astype(BF).reshape(1, 4, 128)
    packed = jnp.concatenate([line_terms, jnp.broadcast_to(line_bias, (64, 4, 128))], axis=1)
    factor = float(lax.axis_size("dp") * pieces * 512) ** (-0.5)
    total = jnp.sum(exchange(packed, PLANE).astype(F32), axis=0) * factor
    grad_bias = total[12:].reshape(512)
    plane = gather_pieces(total[:12].astype(BF), PLANE).reshape(192, 512)

    near = came[784:800]
    next_chip = swap_chips(jnp.where(core == 0, slot[128:144], slot[144:160]))
    far = [shift_space(slot[128 + 16 * j : 144 + 16 * j], -offsets[j]) for j in (2, 3)]
    first = jnp.where(core == 0, near, next_chip)
    second = jnp.where(core == 0, next_chip, near)
    returned = jnp.concatenate([first, second] + far, axis=0)
    grad_mesh = dot_bf16(local + dot_bf16(pick, returned, 0, 0), w_send, 1, 1)
    grad_grid = (upstream.astype(F32) + dot_bf16(recv_grad, w_recv, 1, 1)).astype(BF)
    plane, grad_mesh, grad_grid = lax.optimization_barrier((plane, grad_mesh, grad_grid))

    half = gather_pieces(plane, "x").reshape(3, 1, 256, 512)
    partner = swap_cores(half)
    low = jnp.where(core == 0, half, partner)
    high = jnp.where(core == 0, partner, half)
    whole = jnp.concatenate([low, high], axis=1).reshape(3, 512, 512)
    return (grad_mesh[None], grad_grid[None], whole[0], whole[1], whole[2], grad_bias)


def solution(mesh):
    fine = Mesh(mesh.devices.reshape(8, 8, 4, 2), ("dp",) + SPACE)
    placed = (
        P("dp", SPACE, None),
        P("dp", SPACE, None),
        P("dp", SPACE, None),
        P(SPACE),
        P(SPACE, None, None),
        P(),
        P(),
        P(),
        P(),
    )
    return jax.shard_map(
        per_device,
        mesh=fine,
        in_specs=placed,
        out_specs=(P("dp", SPACE, None), P("dp", SPACE, None), P(), P(), P(), P()),
        check_vma=False,
    )
```

time: 192 us -> 136 us (0.71)
  local copies, waits for them, and re-layouts: 37.6 us -> 9.3 us
  blocking collectives: 58.8 us -> 32.3 us
  other arithmetic: 22.9 us -> 4.28 us
  starting transfers between devices: 45.1 us -> 62 us
  matrix products: 12.7 us -> 6.57 us
  Pallas kernels: 0 us -> 4.58 us
  waiting for transfers between devices: 12.1 us -> 14.6 us
    all_to_all x3 -> x2, blocking collectives: 58.8 us -> 32.3 us  [exchange(): return lax.all_to_all(value, axes, split_axis=0, concat_axis=0, tiled=True)]
    all_to_all x1 -> x2, starting transfers between devices: 3.49 us -> 21.1 us  [exchange(): return lax.all_to_all(value, axes, split_axis=0, concat_axis=0, tiled=True)]
    reduce_sum x5 -> x2, other arithmetic: 16.2 us -> 1.39 us  [the longest x1 1.32 us: per_device(): line = jnp.sum(exchange(packed, 'x').astype(F32), axis=0)]
    mul x2 -> x0, local copies, waits for them, and re-layouts: 8.75 us -> none  [per_device(): edge_grad = (agg_grad[:, None, :] * slope).astype(BF)]
    add x2 -> x0, local copies, waits for them, and re-layouts: 8.62 us -> none  [per_device(): sent_proj[sender_slot].reshape(count_grid, 3, width) + recv_proj[:, None, :]]
    dot_general x10 -> x5, matrix products: 12.7 us -> 6.57 us  [dot_bf16(): lax.dot_general(left.astype(BF), right.astype(BF), (((left_dim,), (right_...]
    reshape x3 -> x4, local copies, waits for them, and re-layouts: 6.6 us -> 1.17 us  [the longest x1 0.58 us: per_device(): grad_bias = total[12:].reshape(512)]
    gather x1 -> x0, local copies, waits for them, and re-layouts: 4.97 us -> none  [per_device(): sent_proj[sender_slot].reshape(count_grid, 3, width) + recv_proj[:, None, :]]
  transfers between devices with their start and end apart: 11 -> 11, of which waited for: 3 -> 4; matrix products, arithmetic and copies ran while one was open for 15% -> 6% of each run, Pallas kernels for 0% -> 0%
where the time goes in v2:
time: 136 us; the launch traced here: 135 us
  starting transfers between devices  62 us (46%)
  blocking collectives  32.3 us (24%)
  waiting for transfers between devices  14.6 us (11%)
  local copies, waits for them, and re-layouts  9.3 us (7%)
  matrix products  6.57 us (5%)
  Pallas kernels  4.58 us (3%)
  other arithmetic  4.28 us (3%)
    all_to_all x2, blocking collectives, exchange(): return lax.all_to_all(value, axes, split_axis=0, concat_axis=0, tiled=True)  32.3 us
    ppermute x6, starting transfers between devices, shift_space(): lax.ppermute(value, SPACE, [(i, (i + offset) % pieces) for i in range(pie...  25.6 us
    all_to_all x2, starting transfers between devices, exchange(): return lax.all_to_all(value, axes, split_axis=0, concat_axis=0, tiled=True)  21.1 us
    all_to_all x2, waiting for transfers between devices, exchange(): return lax.all_to_all(value, axes, split_axis=0, concat_axis=0, tiled=True)  11.7 us
    ppermute x2, starting transfers between devices, swap_cores(): return lax.ppermute(value, 'core', [(0, 1), (1, 0)])  11.4 us
    dot_general x5, matrix products, dot_bf16(): lax.dot_general(left.astype(BF), right.astype(BF), (((left_dim,), (right_...  6.57 us
    unnamed x41, local copies, waits for them, and re-layouts  6.31 us
    pallas_call x1, Pallas kernels, edge_step(): pl.pallas_call(edge_kernel, out_shape=(shape(800, BF), shape(192, BF), sh...  3.9 us
  transfers between devices with their start and end apart: 11, of which 4 were waited for; matrix products, arithmetic and copies ran while one was open for 6% of the time, Pallas kernels for 0%

profile of v2, /device:TPU:1, one launch (start us, length us, event | category | flops | bytes accessed | tf_op | source)
XLA Modules:
  0.0 134.6 jit_solution(2124294628164279398)
XLA Ops:
  0.7 0.8 eq.10
  1.5 1.2 convolution_convert_fusion
  2.7 4.5 %collective-permute-start = (bf16[16,512]{1,0:T(8,128)(2,1)S(1)}, bf16[16,512]{1,0:T(8,128)(2,1)S(1)}, u32[]{:S(2)}, u32[]{:S(2)}) collective-permute-start(bf16[16,512]{1,0:T(8,128)(2,1)S(1)} %get-tuple-element.37), channel_id=1, source_target_pairs={{0,1},{1,2},{2,3},{3,4},{4,5},{5,6},{6,7},{7,8},{8,9},{9,10},{10,1... | collective-permute-start | bytes 49160 | tf_op jit(solution)/shard_map/ppermute | solution.py:157
  7.2 6.2 %collective-permute-start.1 = (bf16[16,512]{1,0:T(8,128)(2,1)S(1)}, bf16[16,512]{1,0:T(8,128)(2,1)S(1)}, u32[]{:S(2)}, u32[]{:S(2)}) collective-permute-start(bf16[16,512]{1,0:T(8,128)(2,1)S(1)} %get-tuple-element.36), channel_id=1, source_target_pairs={{0,63},{1,0},{2,1},{3,2},{4,3},{5,4},{6,5},{7,6},{8,7},{9,8},{10,9... | collective-permute-start | bytes 49160 | tf_op jit(solution)/shard_map/ppermute | solution.py:157
  13.4 1.9 %collective-permute-start.2 = (bf16[16,512]{1,0:T(8,128)(2,1)S(1)}, bf16[16,512]{1,0:T(8,128)(2,1)S(1)}, u32[]{:S(2)}, u32[]{:S(2)}) collective-permute-start(bf16[16,512]{1,0:T(8,128)(2,1)S(1)} %get-tuple-element.35), channel_id=1, source_target_pairs={{0,8},{1,9},{2,10},{3,11},{4,12},{5,13},{6,14},{7,15},{8,16},{9,17... | collective-permute-start | bytes 49160 | tf_op jit(solution)/shard_map/ppermute | solution.py:157
  15.3 3.6 %collective-permute-start.3 = (bf16[16,512]{1,0:T(8,128)(2,1)S(1)}, bf16[16,512]{1,0:T(8,128)(2,1)S(1)}, u32[]{:S(2)}, u32[]{:S(2)}) collective-permute-start(bf16[16,512]{1,0:T(8,128)(2,1)S(1)} %get-tuple-element.34), channel_id=1, source_target_pairs={{0,32},{1,33},{2,34},{3,35},{4,36},{5,37},{6,38},{7,39},{8,40},{9,... | collective-permute-start | bytes 49160 | tf_op jit(solution)/shard_map/ppermute | solution.py:157
  18.9 1.5 %convolution_add_fusion.1.recv_proj_ref = f32[512,512]{1,0:T(8,128)S(1)} fusion(bf16[512,512]{1,0:T(8,128)(2,1)S(1)} %copy-done, f32[512]{0:T(512)} %param.17, bf16[1,512,512]{2,1,0:T(8,128)(2,1)} %param.10), kind=kOutput, calls=%fused_computation.5 | convolution fusion | flops 268697600 | bytes 2099200 | tf_op jit(solution)/shard_map/dot_general | solution.py:147
  20.5 1.5 %fusion.25.agg_grad_ref = f32[512,512]{1,0:T(8,128)} fusion(bf16[512,512]{1,0:T(8,128)(2,1)S(1)} %copy-done.16, bf16[1,512,512]{2,1,0:T(8,128)(2,1)S(1)} %copy-done.1), kind=kOutput, calls=%fused_computation.36 | convolution fusion | flops 268435456 | bytes 2097152 | tf_op jit(solution)/shard_map/dot_general | solution.py:147
  24.3 1.2 copy-done.3
  25.6 1.0 copy-done.4
  26.6 0.7 copy-done.11
  28.1 0.7 copy-done.15
  28.8 3.9 %edge_step.1 = (bf16[800,512]{1,0:T(8,128)(2,1)S(1)}, bf16[192,512]{1,0:T(8,128)(2,1)S(1)}, bf16[192,512]{1,0:T(8,128)(2,1)S(1)}, bf16[512,512]{1,0:T(8,128)(2,1...) custom-call(s32[1]{0:T(128)} %bitcast.core_ref, s32[512,3]{1,0:T(8,128)S(1)} %reshape.61.column_ref, ...), custom_call_target="tpu_custom_call" | custom-call | flops 3000000000 | bytes 6000000 | tf_op jit(solution)/shard_map/edge_step/pallas_call | solution.py:101
  32.7 8.1 %collective-permute-start.4 = (bf16[800,512]{1,0:T(8,128)(2,1)S(1)}, bf16[800,512]{1,0:T(8,128)(2,1)S(1)}, u32[]{:S(2)}, u32[]{:S(2)}) collective-permute-start(bf16[800,512]{1,0:T(8,128)(2,1)S(1)} %get-tuple-element.19), channel_id=1, source_target_pairs={{0,1},{1,0},{2,3},{3,2},{4,5},{5,4},{6,7},{7,6},{8,9},{9,8},{10,11... | collective-permute-start | bytes 2457608 | tf_op jit(solution)/shard_map/ppermute | solution.py:168
  41.4 1.4 %collective-permute-done.4.came_ref = bf16[800,512]{1,0:T(8,128)(2,1)S(1)} collective-permute-done((bf16[800,512]{1,0:T(8,128)(2,1)S(1)}, bf16[800,512]{1,0:T(8,128)(2,1)S(1)}, u32[]{:S(2)}, u32[]{:S(2)}) %collective-permute-start.4) | collective-permute-done | bytes 819232 | tf_op jit(solution)/shard_map/ppermute | solution.py:168
  42.9 15.6 %all_to_all.20 = bf16[4,208,512]{2,1,0:T(8,128)(2,1)} all-to-all(bf16[4,208,512]{2,1,0:T(8,128)(2,1)S(1)} %pack_step.1), channel_id=1, replica_groups=mesh['dp'=8,'y'=8,'x'=4,'core'=2] {'x'}, dimensions={0} | all-to-all | bytes 1703936 | tf_op jit(solution)/shard_map/all_to_all | solution.py:172
  58.5 1.3 reduce
  60.1 0.8 pad_maximum_fusion.1
  60.9 11.5 %all-to-all-start.1 = ((bf16[64,16,128]{2,1,0:T(8,128)(2,1)}), bf16[64,16,128]{2,1,0:T(8,128)(2,1)S(1)}, u32[]{:S(2)}, u32[]{:S(2)}) async-start(bf16[64,16,128]{2,1,0:T(8,128)(2,1)} %pad_maximum_fusion.1), calls=%async_computation.1 | async-start | bytes 524288 | tf_op jit(solution)/shard_map/all_to_all | solution.py:172
  72.4 0.8 slice_select_fusion
  73.1 3.8 %collective-permute-start.5 = (bf16[16,512]{1,0:T(8,128)(2,1)S(1)}, bf16[16,512]{1,0:T(8,128)(2,1)S(1)}, u32[]{:S(2)}, u32[]{:S(2)}) collective-permute-start(bf16[16,512]{1,0:T(8,128)(2,1)S(1)} %get-tuple-element.31), channel_id=1, source_target_pairs={{0,63},{1,2},{2,1},{3,4},{4,3},{5,6},{6,5},{7,8},{8,7},{9,10},{10,... | collective-permute-start | bytes 49160 | tf_op jit(solution)/shard_map/ppermute | solution.py:162
  77.0 4.4 %collective-permute-start.6 = (bf16[16,512]{1,0:T(8,128)(2,1)S(1)}, bf16[16,512]{1,0:T(8,128)(2,1)S(1)}, u32[]{:S(2)}, u32[]{:S(2)}) collective-permute-start(bf16[16,512]{1,0:T(8,128)(2,1)S(1)} %get-tuple-element.32), channel_id=1, source_target_pairs={{0,56},{1,57},{2,58},{3,59},{4,60},{5,61},{6,62},{7,63},{8,0},{9,1... | collective-permute-start | bytes 49160 | tf_op jit(solution)/shard_map/ppermute | solution.py:157
  81.5 5.0 %collective-permute-start.7 = (bf16[16,512]{1,0:T(8,128)(2,1)S(1)}, bf16[16,512]{1,0:T(8,128)(2,1)S(1)}, u32[]{:S(2)}, u32[]{:S(2)}) collective-permute-start(bf16[16,512]{1,0:T(8,128)(2,1)S(1)} %get-tuple-element.33), channel_id=1, source_target_pairs={{0,32},{1,33},{2,34},{3,35},{4,36},{5,37},{6,38},{7,39},{8,40},{9,... | collective-permute-start | bytes 49160 | tf_op jit(solution)/shard_map/ppermute | solution.py:157
  86.5 1.3 fusion
  87.9 0.7 broadcast_in_dim.11
  88.6 9.6 %all-to-all-start.2 = ((bf16[64,12,128]{2,1,0:T(8,128)(2,1)}), bf16[64,12,128]{2,1,0:T(8,128)(2,1)S(1)}, u32[]{:S(2)}, u32[]{:S(2)}) async-start(bf16[64,12,128]{2,1,0:T(8,128)(2,1)} %broadcast_in_dim.11), calls=%async_computation.2 | async-start | bytes 524288 | tf_op jit(solution)/shard_map/all_to_all | solution.py:172
  98.3 1.2 fusion.3
  99.5 11.7 %all-to-all-done.2 = bf16[64,12,128]{2,1,0:T(8,128)(2,1)S(1)} async-done(((bf16[64,12,128]{2,1,0:T(8,128)(2,1)}), bf16[64,12,128]{2,1,0:T(8,128)(2,1)S(1)}, u32[]{:S(2)}, u32[]{:S(2)}) %all-to-all-start.2) | async-done | bytes 196640 | tf_op jit(solution)/shard_map/all_to_all | solution.py:172
  111.4 16.8 %all_to_all.21 = bf16[4,192,512]{2,1,0:T(8,128)(2,1)S(1)} all-to-all(bf16[4,192,512]{2,1,0:T(8,128)(2,1)S(1)} %broadcast_in_dim.14), channel_id=1, replica_groups=mesh['dp'=8,'y'=8,'x'=4,'core'=2] {'x'}, dimensions={0} | all-to-all | bytes 1572864 | tf_op jit(solution)/shard_map/all_to_all | solution.py:172
  128.2 3.3 %collective-permute-start.8 = (bf16[3,1,256,512]{3,2,1,0:T(8,128)(2,1)S(1)}, bf16[3,1,256,512]{3,2,1,0:T(8,128)(2,1)S(1)}, u32[]{:S(2)}, u32[]{:S(2)}) collective-permute-start(bf16[3,1,256,512]{3,2,1,0:T(8,128)(2,1)S(1)} %bitcast.36), channel_id=1, source_target_pairs={{0,1},{1,0},{2,3},{3,2},{4,5},{5,4},{6,7},{7,6},{8,9},{9,8},{10,11... | collective-permute-start | bytes 2359304 | tf_op jit(solution)/shard_map/ppermute | solution.py:168
  132.0 1.3 collective-permute-done.8
  133.4 1.2 pad_maximum_fusion
  (63 shorter events, 5.1 us)
Async XLA Ops:
  0.6 18.3 %copy-start = (bf16[512,512]{1,0:T(8,128)(2,1)S(1)}, bf16[512,512]{1,0:T(8,128)(2,1)}, u32[]{:S(2)}) copy-start(bf16[512,512]{1,0:T(8,128)(2,1)} %param.15) | copy-start | bytes 1572868
  0.6 19.8 %copy-start.1 = (bf16[1,512,512]{2,1,0:T(8,128)(2,1)S(1)}, bf16[1,512,512]{2,1,0:T(8,128)(2,1)}, u32[]{:S(2)}) copy-start(bf16[1,512,512]{2,1,0:T(8,128)(2,1)} %param.11) | copy-start | bytes 1572868
  1.5 17.4 %copy-start.18 = (s32[64]{0:T(128)}, s32[64]{0:T(128)S(1)}, u32[]{:S(2)}) copy-start(s32[64]{0:T(128)S(1)} %eq.10) | copy-start | bytes 772
  1.5 18.9 %copy-start.16 = (bf16[512,512]{1,0:T(8,128)(2,1)S(1)}, bf16[512,512]{1,0:T(8,128)(2,1)}, u32[]{:S(2)}) copy-start(bf16[512,512]{1,0:T(8,128)(2,1)} %param.16) | copy-start | bytes 1572868
  2.7 19.6 %collective-permute-start = (bf16[16,512]{1,0:T(8,128)(2,1)S(1)}, bf16[16,512]{1,0:T(8,128)(2,1)S(1)}, u32[]{:S(2)}, u32[]{:S(2)}) collective-permute-start(bf16[16,512]{1,0:T(8,128)(2,1)S(1)} %get-tuple-element.37), channel_id=1, source_target_pairs={{0,1},{1,2},{2,3},{3,4},{4,5},{5,6},{6,7},{7,8},{8,9},{9,10},{10,1... | collective-permute-start | bytes 49160 | tf_op jit(solution)/shard_map/ppermute | solution.py:157
  7.2 15.1 %collective-permute-start.1 = (bf16[16,512]{1,0:T(8,128)(2,1)S(1)}, bf16[16,512]{1,0:T(8,128)(2,1)S(1)}, u32[]{:S(2)}, u32[]{:S(2)}) collective-permute-start(bf16[16,512]{1,0:T(8,128)(2,1)S(1)} %get-tuple-element.36), channel_id=1, source_target_pairs={{0,63},{1,0},{2,1},{3,2},{4,3},{5,4},{6,5},{7,6},{8,7},{9,8},{10,9... | collective-permute-start | bytes 49160 | tf_op jit(solution)/shard_map/ppermute | solution.py:157
  13.4 9.5 %collective-permute-start.2 = (bf16[16,512]{1,0:T(8,128)(2,1)S(1)}, bf16[16,512]{1,0:T(8,128)(2,1)S(1)}, u32[]{:S(2)}, u32[]{:S(2)}) collective-permute-start(bf16[16,512]{1,0:T(8,128)(2,1)S(1)} %get-tuple-element.35), channel_id=1, source_target_pairs={{0,8},{1,9},{2,10},{3,11},{4,12},{5,13},{6,14},{7,15},{8,16},{9,17... | collective-permute-start | bytes 49160 | tf_op jit(solution)/shard_map/ppermute | solution.py:157
  15.3 8.4 %collective-permute-start.3 = (bf16[16,512]{1,0:T(8,128)(2,1)S(1)}, bf16[16,512]{1,0:T(8,128)(2,1)S(1)}, u32[]{:S(2)}, u32[]{:S(2)}) collective-permute-start(bf16[16,512]{1,0:T(8,128)(2,1)S(1)} %get-tuple-element.34), channel_id=1, source_target_pairs={{0,32},{1,33},{2,34},{3,35},{4,36},{5,37},{6,38},{7,39},{8,40},{9,... | collective-permute-start | bytes 49160 | tf_op jit(solution)/shard_map/ppermute | solution.py:157
  20.4 1.5 %copy-start.17 = (s32[1536]{0:T(1024)S(1)}, s32[1536]{0:T(1024)}, u32[]{:S(2)}) copy-start(s32[1536]{0:T(1024)} %param.12) | copy-start | bytes 18436
  20.4 3.9 %copy-start.2 = (bf16[1,512,512]{2,1,0:T(8,128)(2,1)S(1)}, bf16[1,512,512]{2,1,0:T(8,128)(2,1)}, u32[]{:S(2)}) copy-start(bf16[1,512,512]{2,1,0:T(8,128)(2,1)} %param.10) | copy-start | bytes 1572868
  20.5 3.9 %copy-start.9 = (bf16[1,128,512]{2,1,0:T(8,128)(2,1)S(1)}, bf16[1,128,512]{2,1,0:T(8,128)(2,1)}, u32[]{:S(2)}) copy-start(bf16[1,128,512]{2,1,0:T(8,128)(2,1)} %param.9) | copy-start | bytes 393220
  22.3 0.6 copy-start.10
  22.9 0.6 copy-start.12
  23.7 0.6 copy-start.14
  24.3 1.2 copy-start.3
  25.6 1.0 copy-start.4
  26.6 0.7 copy-start.11
  27.3 0.7 copy-start.13
  28.0 0.7 copy-start.15
  32.7 8.7 %copy-start.6 = (bf16[192,512]{1,0:T(8,128)(2,1)}, bf16[192,512]{1,0:T(8,128)(2,1)S(1)}, u32[]{:S(2)}) copy-start(bf16[192,512]{1,0:T(8,128)(2,1)S(1)} %get-tuple-element.16.slot_ref) | copy-start | bytes 589828
  32.7 8.7 %copy-start.7 = (f32[128,512]{1,0:T(8,128)}, f32[128,512]{1,0:T(8,128)S(1)}, u32[]{:S(2)}) copy-start(f32[128,512]{1,0:T(8,128)S(1)} %get-tuple-element.20) | copy-start | bytes 786436
  32.7 10.1 %collective-permute-start.4 = (bf16[800,512]{1,0:T(8,128)(2,1)S(1)}, bf16[800,512]{1,0:T(8,128)(2,1)S(1)}, u32[]{:S(2)}, u32[]{:S(2)}) collective-permute-start(bf16[800,512]{1,0:T(8,128)(2,1)S(1)} %get-tuple-element.19), channel_id=1, source_target_pairs={{0,1},{1,0},{2,3},{3,2},{4,5},{5,4},{6,7},{7,6},{8,9},{9,8},{10,11... | collective-permute-start | bytes 2457608 | tf_op jit(solution)/shard_map/ppermute | solution.py:168
  60.9 26.9 %all-to-all-start.1 = ((bf16[64,16,128]{2,1,0:T(8,128)(2,1)}), bf16[64,16,128]{2,1,0:T(8,128)(2,1)S(1)}, u32[]{:S(2)}, u32[]{:S(2)}) async-start(bf16[64,16,128]{2,1,0:T(8,128)(2,1)} %pad_maximum_fusion.1), calls=%async_computation.1 | async-start | bytes 524288 | tf_op jit(solution)/shard_map/all_to_all | solution.py:172
  73.1 25.1 %collective-permute-start.5 = (bf16[16,512]{1,0:T(8,128)(2,1)S(1)}, bf16[16,512]{1,0:T(8,128)(2,1)S(1)}, u32[]{:S(2)}, u32[]{:S(2)}) collective-permute-start(bf16[16,512]{1,0:T(8,128)(2,1)S(1)} %get-tuple-element.31), channel_id=1, source_target_pairs={{0,63},{1,2},{2,1},{3,4},{4,3},{5,6},{6,5},{7,8},{8,7},{9,10},{10,... | collective-permute-start | bytes 49160 | tf_op jit(solution)/shard_map/ppermute | solution.py:162
  77.0 21.3 %collective-permute-start.6 = (bf16[16,512]{1,0:T(8,128)(2,1)S(1)}, bf16[16,512]{1,0:T(8,128)(2,1)S(1)}, u32[]{:S(2)}, u32[]{:S(2)}) collective-permute-start(bf16[16,512]{1,0:T(8,128)(2,1)S(1)} %get-tuple-element.32), channel_id=1, source_target_pairs={{0,56},{1,57},{2,58},{3,59},{4,60},{5,61},{6,62},{7,63},{8,0},{9,1... | collective-permute-start | bytes 49160 | tf_op jit(solution)/shard_map/ppermute | solution.py:157
  81.4 16.9 %copy-start.5 = (bf16[512,512]{1,0:T(8,128)(2,1)S(1)}, bf16[512,512]{1,0:T(8,128)(2,1)}, u32[]{:S(2)}) copy-start(bf16[512,512]{1,0:T(8,128)(2,1)} %w_send_ref.1) | copy-start | bytes 1572868
  81.4 16.9 %copy-start.8 = (f32[128,512]{1,0:T(8,128)S(1)}, f32[128,512]{1,0:T(8,128)}, u32[]{:S(2)}) copy-start(f32[128,512]{1,0:T(8,128)} %copy-done.7) | copy-start | bytes 786436
  81.4 16.9 %copy-start.19 = (s32[64]{0:T(128)S(1)}, s32[64]{0:T(128)}, u32[]{:S(2)}) copy-start(s32[64]{0:T(128)} %copy-done.18) | copy-start | bytes 772
  81.5 16.8 %collective-permute-start.7 = (bf16[16,512]{1,0:T(8,128)(2,1)S(1)}, bf16[16,512]{1,0:T(8,128)(2,1)S(1)}, u32[]{:S(2)}, u32[]{:S(2)}) collective-permute-start(bf16[16,512]{1,0:T(8,128)(2,1)S(1)} %get-tuple-element.33), channel_id=1, source_target_pairs={{0,32},{1,33},{2,34},{3,35},{4,36},{5,37},{6,38},{7,39},{8,40},{9,... | collective-permute-start | bytes 49160 | tf_op jit(solution)/shard_map/ppermute | solution.py:157
  88.6 22.6 %all-to-all-start.2 = ((bf16[64,12,128]{2,1,0:T(8,128)(2,1)}), bf16[64,12,128]{2,1,0:T(8,128)(2,1)S(1)}, u32[]{:S(2)}, u32[]{:S(2)}) async-start(bf16[64,12,128]{2,1,0:T(8,128)(2,1)} %broadcast_in_dim.11), calls=%async_computation.2 | async-start | bytes 524288 | tf_op jit(solution)/shard_map/all_to_all | solution.py:172
  128.2 5.2 %collective-permute-start.8 = (bf16[3,1,256,512]{3,2,1,0:T(8,128)(2,1)S(1)}, bf16[3,1,256,512]{3,2,1,0:T(8,128)(2,1)S(1)}, u32[]{:S(2)}, u32[]{:S(2)}) collective-permute-start(bf16[3,1,256,512]{3,2,1,0:T(8,128)(2,1)S(1)} %bitcast.36), channel_id=1, source_target_pairs={{0,1},{1,0},{2,3},{3,2},{4,5},{5,4},{6,7},{7,6},{8,9},{9,8},{10,11... | collective-permute-start | bytes 2359304 | tf_op jit(solution)/shard_map/ppermute | solution.py:168

commit v3 on v2

--- a/solution.py
+++ b/solution.py
@@ -21,15 +21,37 @@
         out_ref[index * 256 : (index + 1) * 256, :] = product.astype(out_ref.dtype)
 
 
+def pick_kernel(rows_hbm, mesh_hbm, o0_ref, o1_ref, o2_ref, o3_ref, rows_ref, mesh_ref, arrived):
+    mesh_copy = pltpu.make_async_copy(mesh_hbm, mesh_ref, arrived.at[0])
+    rows_copy = pltpu.make_async_copy(rows_hbm, rows_ref, arrived.at[1])
+    mesh_copy.start()
+    rows_copy.start()
+    rows_copy.wait()
+    mesh_copy.wait()
+    sublane = lax.broadcasted_iota(jnp.int32, (128, 16), 0)
+    for j, out_ref in enumerate((o0_ref, o1_ref, o2_ref, o3_ref)):
+        pick = (sublane == rows_ref[j : j + 1, :]).astype(F32).astype(BF)
+        out_ref[...] = rows_dot(pick, mesh_ref[...]).astype(BF)
+
+
 def edge_kernel(
-    core_ref, column_ref, row_ref, mesh_ref, h0_ref, h1_ref, h2_ref, h3_ref, recv_proj_ref, agg_grad_ref,
-    w_send_ref, grid_ref, upstream_ref,
-    send_ref, known_ref, slot_ref, recv_ref, node_ref, local_ref,
-    table_ref, preact_ref, edge_ref, bias_ref,
+    core_ref, column_ref, row_ref, mesh_ref, grid_ref, upstream_ref,
+    h0_ref, h1_ref, h2_ref, h3_ref, w_hbm, recv_proj_hbm, agg_grad_hbm,
+    send_ref, known_ref, slot_ref, recv_ref, node_ref, local_ref, next_ref, far_ref, last_ref,
+    table_ref, preact_ref, edge_ref, bias_ref, w_send_ref, recv_proj_ref, agg_grad_ref, arrived,
 ):
+    copies = [
+        pltpu.make_async_copy(halo_ref, known_ref.at[pl.ds(128 + 16 * j, 16)], arrived.at[j])
+        for j, halo_ref in enumerate((h0_ref, h1_ref, h2_ref, h3_ref))
+    ]
+    copies.append(pltpu.make_async_copy(w_hbm, w_send_ref, arrived.at[4]))
+    copies.append(pltpu.make_async_copy(recv_proj_hbm, recv_proj_ref, arrived.at[5]))
+    copies.append(pltpu.make_async_copy(agg_grad_hbm, agg_grad_ref, arrived.at[6]))
+    for copy in copies:
+        copy.start()
     known_ref[0:128, :] = mesh_ref[...]
-    for j, halo_ref in enumerate((h0_ref, h1_ref, h2_ref, h3_ref)):
-        known_ref[128 + 16 * j : 144 + 16 * j, :] = halo_ref[...]
+    for copy in copies[:5]:
+        copy.wait()
     sent = jnp.dot(known_ref[...], w_send_ref[...], preferred_element_type=F32)
     high = sent.astype(BF)
     table_ref[0:192, :] = high
@@ -41,6 +63,8 @@
         preact_ref[k * 512 : (k + 1) * 512, :] = jnp.dot(
             pick, table_ref[...], preferred_element_type=F32
         )
+    copies[5].wait()
+    copies[6].wait()
     bias_ref[...] = jnp.zeros_like(bias_ref)
 
     def chunk(step, carry):
@@ -74,6 +98,10 @@
     send_ref[768:784, :] = jnp.broadcast_to(total, (16, 512)).astype(BF)
     leaving = pl.ds(pl.multiple_of(144 - 16 * core_ref[0], 16), 16)
     send_ref[784:800, :] = slot_ref[leaving, :]
+    staying = pl.ds(pl.multiple_of(128 + 16 * core_ref[0], 16), 16)
+    next_ref[...] = slot_ref[staying, :]
+    far_ref[...] = slot_ref[160:176, :]
+    last_ref[...] = slot_ref[176:192, :]
 
 
 def keep_kernel(core_ref, known_ref, slot_ref, grid_ref, recv_ref, node_ref, upstream_ref, keep_ref):
@@ -81,11 +109,16 @@
 
 
 VM = pl.BlockSpec(memory_space=pltpu.VMEM)
+HBM = pl.BlockSpec(memory_space=pltpu.HBM)
 SM = pl.BlockSpec(memory_space=pltpu.SMEM)
-LIMIT = pltpu.CompilerParams(vmem_limit_bytes=40 * 1024 * 1024)
-
-
-def pack_kernel(keep_ref, came_ref, sent_ref, out_ref):
+
+
+def limit(mebibytes):
+    return pltpu.CompilerParams(vmem_limit_bytes=mebibytes * 1024 * 1024)
+
+
+def pack_kernel(keep_ref, came_ref, sent_ref, out_ref, near_ref):
+    near_ref[...] = came_ref[784:800, :]
     bias = (sent_ref[...].astype(F32) + came_ref[768:784, :].astype(F32)).astype(BF)
     for piece in range(4):
         rows = slice(piece * 192, piece * 192 + 192)
@@ -93,6 +126,52 @@
         out_ref[piece, 192:208, :] = bias
 
 
+def line_kernel(packed_hbm, out_ref, packed_ref, line_ref, bias_ref, arrived):
+    copies = [
+        pltpu.make_async_copy(packed_hbm.at[piece], packed_ref.at[piece], arrived.at[piece])
+        for piece in range(4)
+    ]
+    for copy in copies:
+        copy.start()
+    for copy in copies:
+        copy.wait()
+    line_ref[...] = sum(packed_ref[piece].astype(F32) for piece in range(4))
+    bias = line_ref[192:193, :]
+    for j in range(4):
+        bias_ref[12 + j : 13 + j, :] = bias[:, 128 * j : 128 * j + 128]
+    sublane = lax.broadcasted_iota(jnp.int32, (16, 128), 0)
+    for piece in range(64):
+        top, left = 12 * (piece // 4), 128 * (piece % 4)
+        tile = jnp.where(sublane < 12, line_ref[top : top + 16, left : left + 128], bias_ref[...])
+        out_ref[piece] = tile.astype(BF)
+
+
+def tail_kernel(
+    core_ref, rows_ref, local_ref, near_ref, next_ref, far_ref, last_ref, w_send_ref,
+    upstream_ref, recv_ref, w_recv_ref, mesh_ref, grid_ref,
+):
+    product = lax.dot_general(
+        recv_ref[...], w_recv_ref[...], (((1,), (1,)), ((), ())), preferred_element_type=F32
+    )
+    grid_ref[...] = (upstream_ref[...].astype(F32) + product).astype(BF)
+    first_core = core_ref[0] == 0
+    near, other = near_ref[...], next_ref[...]
+    blocks = (
+        jnp.where(first_core, near, other),
+        jnp.where(first_core, other, near),
+        far_ref[...],
+        last_ref[...],
+    )
+    sublane = lax.broadcasted_iota(jnp.int32, (128, 16), 0)
+    grad = local_ref[...]
+    for j, block in enumerate(blocks):
+        pick = (sublane == rows_ref[j : j + 1, :]).astype(F32).astype(BF)
+        grad += jnp.dot(pick, block, preferred_element_type=F32)
+    mesh_ref[...] = lax.dot_general(
+        grad.astype(BF), w_send_ref[...], (((1,), (1,)), ((), ())), preferred_element_type=F32
+    )
+
+
 def shape(rows, dtype):
     return jax.ShapeDtypeStruct((rows, 512), dtype)
 
@@ -100,16 +179,21 @@
 def edge_step(*args):
     return pl.pallas_call(
         edge_kernel,
-        out_shape=(shape(800, BF), shape(192, BF), shape(192, BF), shape(512, BF), shape(512, BF), shape(128, F32)),
-        in_specs=[SM] + [VM] * 12,
-        out_specs=(VM,) * 6,
+        out_shape=(shape(800, BF), shape(192, BF), shape(192, BF), shape(512, BF), shape(512, BF), shape(128, F32))
+        + (shape(16, BF),) * 3,
+        in_specs=[SM] + [VM] * 5 + [HBM] * 7,
+        out_specs=(VM,) * 9,
         scratch_shapes=[
             pltpu.VMEM((384, 512), BF),
             pltpu.VMEM((1536, 512), F32),
             pltpu.VMEM((1536, 512), BF),
             pltpu.VMEM((8, 512), F32),
+            pltpu.VMEM((512, 512), BF),
+            pltpu.VMEM((512, 512), F32),
+            pltpu.VMEM((512, 512), F32),
+            pltpu.SemaphoreType.DMA((7,)),
         ],
-        compiler_params=LIMIT,
+        compiler_params=limit(24),
         name="edge_step",
         cost_estimate=pl.CostEstimate(flops=3_000_000_000, bytes_accessed=6_000_000, transcendentals=800_000),
     )(*args)
@@ -121,7 +205,7 @@
         out_shape=shape(768, F32),
         in_specs=[SM] + [VM] * 6,
         out_specs=VM,
-        compiler_params=LIMIT,
+        compiler_params=limit(10),
         name="keep_step",
         cost_estimate=pl.CostEstimate(flops=600_000_000, bytes_accessed=4_000_000, transcendentals=0),
     )(*args)
@@ -130,26 +214,63 @@
 def pack_step(*args):
     return pl.pallas_call(
         pack_kernel,
-        out_shape=jax.ShapeDtypeStruct((4, 208, 512), BF),
+        out_shape=(jax.ShapeDtypeStruct((4, 208, 512), BF), shape(16, BF)),
         in_specs=[VM] * 3,
-        out_specs=VM,
-        compiler_params=LIMIT,
+        out_specs=(VM,) * 2,
+        compiler_params=limit(8),
         name="pack_step",
         cost_estimate=pl.CostEstimate(flops=500_000, bytes_accessed=3_000_000, transcendentals=0),
     )(*args)
 
 
+def pick_step(*args):
+    return pl.pallas_call(
+        pick_kernel,
+        out_shape=(shape(16, BF),) * 4,
+        in_specs=[HBM] * 2,
+        out_specs=(VM,) * 4,
+        scratch_shapes=[
+            pltpu.VMEM((4, 16), jnp.int32),
+            pltpu.VMEM((128, 512), BF),
+            pltpu.SemaphoreType.DMA((2,)),
+        ],
+        name="pick_step",
+        cost_estimate=pl.CostEstimate(flops=10_000_000, bytes_accessed=200_000, transcendentals=0),
+    )(*args)
+
+
+def line_step(packed):
+    return pl.pallas_call(
+        line_kernel,
+        out_shape=jax.ShapeDtypeStruct((64, 16, 128), BF),
+        in_specs=[HBM],
+        out_specs=VM,
+        scratch_shapes=[
+            pltpu.VMEM((4, 208, 512), BF),
+            pltpu.VMEM((208, 512), F32),
+            pltpu.VMEM((16, 128), F32),
+            pltpu.SemaphoreType.DMA((4,)),
+        ],
+        compiler_params=limit(8),
+        name="line_step",
+        cost_estimate=pl.CostEstimate(flops=500_000, bytes_accessed=1_000_000, transcendentals=0),
+    )(packed)
+
+
+def tail_step(*args):
+    return pl.pallas_call(
+        tail_kernel,
+        out_shape=(shape(128, F32), shape(512, BF)),
+        in_specs=[SM] + [VM] * 10,
+        out_specs=(VM,) * 2,
+        compiler_params=limit(8),
+        name="tail_step",
+        cost_estimate=pl.CostEstimate(flops=400_000_000, bytes_accessed=3_000_000, transcendentals=0),
+    )(*args)
+
+
 SPACE = ("y", "x", "core")
 PLANE = ("dp", "y")
-
-
-def dot_bf16(left, right, left_dim, right_dim):
-    return lax.dot_general(
-        left.astype(BF),
-        right.astype(BF),
-        (((left_dim,), (right_dim,)), ((), ())),
-        preferred_element_type=F32,
-    )
 
 
 def shift_space(value, offset):
@@ -187,40 +308,41 @@
     core_ref = core.astype(jnp.int32).reshape(1)
     pieces = lax.axis_size(SPACE)
     offsets = (1, -1, max(2, pieces // 8), pieces // 2)
-    pick = (
-        send_rows[0].reshape(-1)[:, None] == jnp.arange(128, dtype=jnp.int32)[None, :]
-    ).astype(BF)
-    outgoing = dot_bf16(pick, mesh_rows, 1, 0).astype(BF).reshape(4, 16, 512)
+    outgoing = pick_step(send_rows[0], mesh_rows)
     halo = [shift_space(outgoing[j], offsets[j]) for j in range(4)]
-    recv_proj = dot_bf16(grid_rows, w_recv, 1, 0) + edge_bias
-    agg_grad = dot_bf16(upstream, w_node, 1, 1)
+    recv_proj = lax.dot_general(
+        grid_rows, w_recv, (((1,), (0,)), ((), ())), preferred_element_type=F32
+    ) + edge_bias
+    agg_grad = lax.dot_general(
+        upstream, w_node, (((1,), (1,)), ((), ())), preferred_element_type=F32
+    )
     column = sender_slot.reshape(512, 3)
     row = column.T.reshape(1, 1536)
-    send, known, slot, recv_grad, node, local = edge_step(
-        core_ref, column, row, mesh_rows, *halo, recv_proj, agg_grad, w_send, grid_rows, upstream
+    send, known, slot, recv_grad, node, local, *leaving = edge_step(
+        core_ref, column, row, mesh_rows, grid_rows, upstream, *halo, w_send, recv_proj, agg_grad
     )
     came = swap_cores(send)
     keep = keep_step(core_ref, known, slot, grid_rows, recv_grad, node, upstream)
-    packed = pack_step(keep, came, send[768:784])
-
-    line = jnp.sum(exchange(packed, "x").astype(F32), axis=0)
-    line_terms = line[:192].astype(BF).reshape(64, 12, 128)
-    line_bias = line[192].astype(BF).reshape(1, 4, 128)
-    packed = jnp.concatenate([line_terms, jnp.broadcast_to(line_bias, (64, 4, 128))], axis=1)
+    packed, near = pack_step(keep, came, send[768:784])
+    packed, *leaving = lax.optimization_barrier((packed, *leaving))
+
+    next_chip = swap_chips(leaving[0])
+    far = shift_space(leaving[1], -offsets[2])
+    last = shift_space(leaving[2], -offsets[3])
+    line = line_step(exchange(packed, "x"))
+    line, next_chip, far, last = lax.optimization_barrier((line, next_chip, far, last))
+
     factor = float(lax.axis_size("dp") * pieces * 512) ** (-0.5)
-    total = jnp.sum(exchange(packed, PLANE).astype(F32), axis=0) * factor
+    total = jnp.sum(exchange(line, PLANE).astype(F32), axis=0) * factor
     grad_bias = total[12:].reshape(512)
-    plane = gather_pieces(total[:12].astype(BF), PLANE).reshape(192, 512)
-
-    near = came[784:800]
-    next_chip = swap_chips(jnp.where(core == 0, slot[128:144], slot[144:160]))
-    far = [shift_space(slot[128 + 16 * j : 144 + 16 * j], -offsets[j]) for j in (2, 3)]
-    first = jnp.where(core == 0, near, next_chip)
-    second = jnp.where(core == 0, next_chip, near)
-    returned = jnp.concatenate([first, second] + far, axis=0)
-    grad_mesh = dot_bf16(local + dot_bf16(pick, returned, 0, 0), w_send, 1, 1)
-    grad_grid = (upstream.astype(F32) + dot_bf16(recv_grad, w_recv, 1, 1)).astype(BF)
-    plane, grad_mesh, grad_grid = lax.optimization_barrier((plane, grad_mesh, grad_grid))
+    plane = gather_pieces(total.astype(BF), PLANE)[:, :12].reshape(16, 4, 12, 128)
+    plane = plane.transpose(0, 2, 1, 3).reshape(192, 512)
+    grad_mesh, grad_grid = tail_step(
+        core_ref, send_rows[0], local, near, next_chip, far, last, w_send, upstream, recv_grad, w_recv
+    )
+    plane, grad_mesh, grad_grid, grad_bias = lax.optimization_barrier(
+        (plane, grad_mesh, grad_grid, grad_bias)
+    )
 
     half = gather_pieces(plane, "x").reshape(3, 1, 256, 512)
     partner = swap_cores(half)

time: 136 us -> 129 us (0.949)
  starting transfers between devices: 62 us -> 52.3 us
  Pallas kernels: 4.58 us -> 9.94 us
  blocking collectives: 32.3 us -> 36.9 us
  local copies, waits for them, and re-layouts: 9.3 us -> 5.27 us
  other arithmetic: 4.28 us -> 1.37 us
  waiting for transfers between devices: 14.6 us -> 17.2 us
  matrix products: 6.57 us -> 4.06 us
    all_to_all x2, starting transfers between devices: 21.1 us -> 8.12 us  [exchange(): return lax.all_to_all(value, axes, split_axis=0, concat_axis=0, tiled=True)]
    pallas_call x1 -> x4, Pallas kernels: 0.13 us -> 4.86 us  [the longest x1 1.84 us: pick_step(): pl.pallas_call(pick_kernel, out_shape=(shape(16, BF),) * 4, in_specs=[HBM...]
    all_to_all x2, blocking collectives: 32.3 us -> 36.9 us  [exchange(): return lax.all_to_all(value, axes, split_axis=0, concat_axis=0, tiled=True)]
    ppermute x2, starting transfers between devices: 11.4 us -> 14.9 us  [swap_cores(): return lax.ppermute(value, 'core', [(0, 1), (1, 0)])]
    ppermute x6, waiting for transfers between devices: 0.23 us -> 3.51 us  [shift_space(): lax.ppermute(value, SPACE, [(i, (i + offset) % pieces) for i in range(pie...]
    unnamed x41 -> x31, local copies, waits for them, and re-layouts: 6.31 us -> 3.51 us
    dot_general x5 -> x2, matrix products: 6.57 us -> 4.06 us  [the longest x1 2.62 us: per_device(): lax.dot_general(grid_rows, w_recv, (((1,), (0,)), ((), ())), preferred_el...]
  transfers between devices with their start and end apart: 11 -> 11, of which waited for: 4 -> 5; matrix products, arithmetic and copies ran while one was open for 6% -> 4% of each run, Pallas kernels for 0% -> 3%
where the time goes in v3:
time: 129 us; the launch traced here: 128 us
  starting transfers between devices  52.3 us (41%)
  blocking collectives  36.9 us (29%)
  waiting for transfers between devices  17.2 us (13%)
  Pallas kernels  9.94 us (8%)
  local copies, waits for them, and re-layouts  5.27 us (4%)
  matrix products  4.06 us (3%)
  other arithmetic  1.37 us (1%)
    all_to_all x2, blocking collectives, exchange(): return lax.all_to_all(value, axes, split_axis=0, concat_axis=0, tiled=True)  36.9 us
    ppermute x6, starting transfers between devices, shift_space(): lax.ppermute(value, SPACE, [(i, (i + offset) % pieces) for i in range(pie...  25.3 us
    ppermute x2, starting transfers between devices, swap_cores(): return lax.ppermute(value, 'core', [(0, 1), (1, 0)])  14.9 us
    all_to_all x2, waiting for transfers between devices, exchange(): return lax.all_to_all(value, axes, split_axis=0, concat_axis=0, tiled=True)  10.4 us
    all_to_all x2, starting transfers between devices, exchange(): return lax.all_to_all(value, axes, split_axis=0, concat_axis=0, tiled=True)  8.12 us
    pallas_call x1, Pallas kernels, edge_step(): pl.pallas_call(edge_kernel, out_shape=(shape(800, BF), shape(192, BF), sh...  4.54 us
    ppermute x1, starting transfers between devices, swap_chips(): lax.ppermute(value, SPACE, [(i, (i - 1 + 2 * (i % 2)) % pieces) for i in...  3.97 us
    unnamed x31, local copies, waits for them, and re-layouts  3.51 us
  transfers between devices with their start and end apart: 11, of which 5 were waited for; matrix products, arithmetic and copies ran while one was open for 4% of the time, Pallas kernels for 3%

profile of v3, /device:TPU:1, one launch (start us, length us, event | category | flops | bytes accessed | tf_op | source)
XLA Modules:
  0.0 128.0 jit_solution(7078748996321077806)
XLA Ops:
  0.7 1.8 %pick_step.1 = (bf16[16,512]{1,0:T(8,128)(2,1)}, bf16[16,512]{1,0:T(8,128)(2,1)}, bf16[16,512]{1,0:T(8,128)(2,1)}, bf16[16,512]{1,0:T(8,128)(2,1)}) custom-call(s32[4,16]{1,0:T(4,128)} %bitcast.40, bf16[128,512]{1,0:T(8,128)(2,1)} %bitcast.38), custom_call_target="tpu_custom_call" | custom-call | flops 10000000 | bytes 200000 | tf_op jit(solution)/shard_map/pick_step/pallas_call | solution.py:227
  2.5 4.5 %collective-permute-start = (bf16[16,512]{1,0:T(8,128)(2,1)}, bf16[16,512]{1,0:T(8,128)(2,1)S(1)}, u32[]{:S(2)}, u32[]{:S(2)}) collective-permute-start(bf16[16,512]{1,0:T(8,128)(2,1)} %get-tuple-element.35), channel_id=1, source_target_pairs={{0,1},{1,2},{2,3},{3,4},{4,5},{5,6},{6,7},{7,8},{8,9},{9,10},{10,1... | collective-permute-start | bytes 49160 | tf_op jit(solution)/shard_map/ppermute | solution.py:278
  7.0 6.2 %collective-permute-start.1 = (bf16[16,512]{1,0:T(8,128)(2,1)}, bf16[16,512]{1,0:T(8,128)(2,1)S(1)}, u32[]{:S(2)}, u32[]{:S(2)}) collective-permute-start(bf16[16,512]{1,0:T(8,128)(2,1)} %get-tuple-element.36), channel_id=1, source_target_pairs={{0,63},{1,0},{2,1},{3,2},{4,3},{5,4},{6,5},{7,6},{8,7},{9,8},{10,9... | collective-permute-start | bytes 49160 | tf_op jit(solution)/shard_map/ppermute | solution.py:278
  13.2 1.9 %collective-permute-start.2 = (bf16[16,512]{1,0:T(8,128)(2,1)}, bf16[16,512]{1,0:T(8,128)(2,1)S(1)}, u32[]{:S(2)}, u32[]{:S(2)}) collective-permute-start(bf16[16,512]{1,0:T(8,128)(2,1)} %get-tuple-element.37), channel_id=1, source_target_pairs={{0,8},{1,9},{2,10},{3,11},{4,12},{5,13},{6,14},{7,15},{8,16},{9,17... | collective-permute-start | bytes 49160 | tf_op jit(solution)/shard_map/ppermute | solution.py:278
  15.2 3.6 %collective-permute-start.3 = (bf16[16,512]{1,0:T(8,128)(2,1)}, bf16[16,512]{1,0:T(8,128)(2,1)S(1)}, u32[]{:S(2)}, u32[]{:S(2)}) collective-permute-start(bf16[16,512]{1,0:T(8,128)(2,1)} %get-tuple-element.38), channel_id=1, source_target_pairs={{0,32},{1,33},{2,34},{3,35},{4,36},{5,37},{6,38},{7,39},{8,40},{9,... | collective-permute-start | bytes 49160 | tf_op jit(solution)/shard_map/ppermute | solution.py:278
  18.7 2.6 %convolution_add_fusion.recv_proj_hbm = f32[512,512]{1,0:T(8,128)} fusion(bf16[512,512]{1,0:T(8,128)(2,1)} %w_recv_ref.1, f32[512]{0:T(512)} %param.17, bf16[1,512,512]{2,1,0:T(8,128)(2,1)} %param.10), kind=kOutput, calls=%fused_computation.4 | convolution fusion | flops 268697600 | bytes 2099200 | tf_op jit(solution)/shard_map/dot_general | solution.py:313
  21.4 1.4 %fusion.2.agg_grad_hbm = f32[512,512]{1,0:T(8,128)} fusion(bf16[512,512]{1,0:T(8,128)(2,1)S(1)} %copy-done, bf16[1,512,512]{2,1,0:T(8,128)(2,1)S(1)} %copy-done.1), kind=kOutput, calls=%fused_computation.14 | convolution fusion | flops 268435456 | bytes 2097152 | tf_op jit(solution)/shard_map/dot_general | solution.py:316
  22.8 0.2 reshape.47.column_ref
  23.2 0.6 collective-permute-done.3.h3_ref
  23.8 1.2 copy-done.4
  25.0 1.2 copy-done.5
  26.2 4.5 %edge_step.1 = (bf16[800,512]{1,0:T(8,128)(2,1)S(1)}, bf16[192,512]{1,0:T(8,128)(2,1)S(1)}, bf16[192,512]{1,0:T(8,128)(2,1)S(1)}, bf16[512,512]{1,0:T(8,128)(2,1...) custom-call(s32[1]{0:T(128)} %bitcast.core_ref, ...), custom_call_target="tpu_custom_call" | custom-call | flops 3000000000 | bytes 6000000 | tf_op jit(solution)/shard_map/edge_step/pallas_call | solution.py:180
  30.8 8.1 %collective-permute-start.4 = (bf16[800,512]{1,0:T(8,128)(2,1)S(1)}, bf16[800,512]{1,0:T(8,128)(2,1)S(1)}, u32[]{:S(2)}, u32[]{:S(2)}) collective-permute-start(bf16[800,512]{1,0:T(8,128)(2,1)S(1)} %get-tuple-element.43), channel_id=1, source_target_pairs={{0,1},{1,0},{2,3},{3,2},{4,5},{5,4},{6,7},{7,6},{8,9},{9,8},{10,11... | collective-permute-start | bytes 2457608 | tf_op jit(solution)/shard_map/ppermute | solution.py:289
  38.9 0.5 keep_step.1.keep_ref
  39.5 1.4 %collective-permute-done.4.came_ref = bf16[800,512]{1,0:T(8,128)(2,1)S(1)} collective-permute-done((bf16[800,512]{1,0:T(8,128)(2,1)S(1)}, bf16[800,512]{1,0:T(8,128)(2,1)S(1)}, u32[]{:S(2)}, u32[]{:S(2)}) %collective-permute-start.4) | collective-permute-done | bytes 819232 | tf_op jit(solution)/shard_map/ppermute | solution.py:289
  41.0 0.9 copy-done.6
  41.9 3.5 %all-to-all-start = ((bf16[4,208,512]{2,1,0:T(8,128)(2,1)}), bf16[4,208,512]{2,1,0:T(8,128)(2,1)S(1)}, u32[]{:S(2)}, u32[]{:S(2)}) async-start(bf16[4,208,512]{2,1,0:T(8,128)(2,1)} %copy-done.6), calls=%async_computation | async-start | bytes 1703936 | tf_op jit(solution)/shard_map/all_to_all | solution.py:293
  45.4 4.0 %collective-permute-start.5 = (bf16[16,512]{1,0:T(8,128)(2,1)}, bf16[16,512]{1,0:T(8,128)(2,1)S(1)}, u32[]{:S(2)}, u32[]{:S(2)}) collective-permute-start(bf16[16,512]{1,0:T(8,128)(2,1)} %get-tuple-element.49), channel_id=1, source_target_pairs={{0,63},{1,2},{2,1},{3,4},{4,3},{5,6},{6,5},{7,8},{8,7},{9,10},{10,... | collective-permute-start | bytes 49160 | tf_op jit(solution)/shard_map/ppermute | solution.py:283
  49.4 4.9 %collective-permute-start.6 = (bf16[16,512]{1,0:T(8,128)(2,1)}, bf16[16,512]{1,0:T(8,128)(2,1)S(1)}, u32[]{:S(2)}, u32[]{:S(2)}) collective-permute-start(bf16[16,512]{1,0:T(8,128)(2,1)} %get-tuple-element.50), channel_id=1, source_target_pairs={{0,56},{1,57},{2,58},{3,59},{4,60},{5,61},{6,62},{7,63},{8,0},{9,1... | collective-permute-start | bytes 49160 | tf_op jit(solution)/shard_map/ppermute | solution.py:278
  54.3 4.2 %collective-permute-start.7 = (bf16[16,512]{1,0:T(8,128)(2,1)}, bf16[16,512]{1,0:T(8,128)(2,1)S(1)}, u32[]{:S(2)}, u32[]{:S(2)}) collective-permute-start(bf16[16,512]{1,0:T(8,128)(2,1)} %copy-done.12), channel_id=1, source_target_pairs={{0,32},{1,33},{2,34},{3,35},{4,36},{5,37},{6,38},{7,39},{8,40},{9,... | collective-permute-start | bytes 49160 | tf_op jit(solution)/shard_map/ppermute | solution.py:278
  58.5 1.4 %line_step.1 = bf16[64,16,128]{2,1,0:T(8,128)(2,1)S(1)} custom-call(bf16[4,208,512]{2,1,0:T(8,128)(2,1)S(1)} %all-to-all-done.packed_hbm), custom_call_target="tpu_custom_call" | custom-call | flops 500000 | bytes 1000000 | tf_op jit(solution)/shard_map/line_step/pallas_call | solution.py:243
  59.9 2.9 %collective-permute-done.7.last_ref = bf16[16,512]{1,0:T(8,128)(2,1)S(1)} collective-permute-done((bf16[16,512]{1,0:T(8,128)(2,1)}, bf16[16,512]{1,0:T(8,128)(2,1)S(1)}, u32[]{:S(2)}, u32[]{:S(2)}) %collective-permute-start.7) | collective-permute-done | bytes 16416 | tf_op jit(solution)/shard_map/ppermute | solution.py:278
  62.9 23.3 %all_to_all.20 = bf16[64,16,128]{2,1,0:T(8,128)(2,1)S(1)} all-to-all(bf16[64,16,128]{2,1,0:T(8,128)(2,1)S(1)} %line_step.1), channel_id=1, replica_groups=mesh['dp'=8,'y'=8,'x'=4,'core'=2] {'dp','y'}, dimensions={0} | all-to-all | bytes 524288 | tf_op jit(solution)/shard_map/all_to_all | solution.py:293
  86.2 0.7 broadcast_in_dim.8
  87.0 4.6 %all-to-all-start.2 = ((bf16[64,16,128]{2,1,0:T(8,128)(2,1)}), bf16[64,16,128]{2,1,0:T(8,128)(2,1)S(1)}, u32[]{:S(2)}, u32[]{:S(2)}) async-start(bf16[64,16,128]{2,1,0:T(8,128)(2,1)} %broadcast_in_dim.8), calls=%async_computation.2 | async-start | bytes 524288 | tf_op jit(solution)/shard_map/all_to_all | solution.py:293
  91.6 1.5 %tail_step.1 = (f32[128,512]{1,0:T(8,128)}, bf16[512,512]{1,0:T(8,128)(2,1)}) custom-call(s32[1]{0:T(128)} %bitcast.core_ref, s32[4,16]{1,0:T(4,128)S(1)} %bitcast.41, f32[128,512]{1,0:T(8,128)S(1)} %copy-done.9, bf16[16,512]{1,0:T(8,128)(2,1)S(1)} %get-tuple-element.54.near_ref, bf16[16,512]{1,0:T(8,128)(2,1)S(1)} %collective-permute-done.5.next_ref, ...), custom_call_target="tpu_custom_call" | custom-call | flops 400000000 | bytes 3000000 | tf_op jit(solution)/shard_map/tail_step/pallas_call | solution.py:261
  93.2 0.6 slice_bitcast_fusion
  93.7 10.4 %all-to-all-done.2 = bf16[64,16,128]{2,1,0:T(8,128)(2,1)S(1)} async-done(((bf16[64,16,128]{2,1,0:T(8,128)(2,1)}), bf16[64,16,128]{2,1,0:T(8,128)(2,1)S(1)}, u32[]{:S(2)}, u32[]{:S(2)}) %all-to-all-start.2) | async-done | bytes 262176 | tf_op jit(solution)/shard_map/all_to_all | solution.py:293
  104.4 13.6 %all_to_all.21 = bf16[4,192,512]{2,1,0:T(8,128)(2,1)S(1)} all-to-all(bf16[4,192,512]{2,1,0:T(8,128)(2,1)S(1)} %broadcast_in_dim.22), channel_id=1, replica_groups=mesh['dp'=8,'y'=8,'x'=4,'core'=2] {'x'}, dimensions={0} | all-to-all | bytes 1572864 | tf_op jit(solution)/shard_map/all_to_all | solution.py:293
  118.0 6.8 %collective-permute-start.8 = (bf16[3,1,256,512]{3,2,1,0:T(8,128)(2,1)S(1)}, bf16[3,1,256,512]{3,2,1,0:T(8,128)(2,1)S(1)}, u32[]{:S(2)}, u32[]{:S(2)}) collective-permute-start(bf16[3,1,256,512]{3,2,1,0:T(8,128)(2,1)S(1)} %bitcast.43), channel_id=1, source_target_pairs={{0,1},{1,0},{2,3},{3,2},{4,5},{5,4},{6,7},{7,6},{8,9},{9,8},{10,11... | collective-permute-start | bytes 2359304 | tf_op jit(solution)/shard_map/ppermute | solution.py:289
  124.8 1.9 %collective-permute-done.8 = bf16[3,1,256,512]{3,2,1,0:T(8,128)(2,1)S(1)} collective-permute-done((bf16[3,1,256,512]{3,2,1,0:T(8,128)(2,1)S(1)}, bf16[3,1,256,512]{3,2,1,0:T(8,128)(2,1)S(1)}, u32[]{:S(2)}, u32[]{:S(2)}) %collective-permute-start.8) | collective-permute-done | bytes 786464 | tf_op jit(solution)/shard_map/ppermute | solution.py:289
  126.8 1.2 pad_maximum_fusion
  (42 shorter events, 0.7 us)
Async XLA Ops:
  0.6 20.7 %copy-start = (bf16[512,512]{1,0:T(8,128)(2,1)S(1)}, bf16[512,512]{1,0:T(8,128)(2,1)}, u32[]{:S(2)}) copy-start(bf16[512,512]{1,0:T(8,128)(2,1)} %param.16) | copy-start | bytes 1572868
  0.6 20.7 %copy-start.1 = (bf16[1,512,512]{2,1,0:T(8,128)(2,1)S(1)}, bf16[1,512,512]{2,1,0:T(8,128)(2,1)}, u32[]{:S(2)}) copy-start(bf16[1,512,512]{2,1,0:T(8,128)(2,1)} %param.11) | copy-start | bytes 1572868
  2.5 20.7 %collective-permute-start = (bf16[16,512]{1,0:T(8,128)(2,1)}, bf16[16,512]{1,0:T(8,128)(2,1)S(1)}, u32[]{:S(2)}, u32[]{:S(2)}) collective-permute-start(bf16[16,512]{1,0:T(8,128)(2,1)} %get-tuple-element.35), channel_id=1, source_target_pairs={{0,1},{1,2},{2,3},{3,4},{4,5},{5,6},{6,7},{7,8},{8,9},{9,10},{10,1... | collective-permute-start | bytes 49160 | tf_op jit(solution)/shard_map/ppermute | solution.py:278
  7.0 16.2 %collective-permute-start.1 = (bf16[16,512]{1,0:T(8,128)(2,1)}, bf16[16,512]{1,0:T(8,128)(2,1)S(1)}, u32[]{:S(2)}, u32[]{:S(2)}) collective-permute-start(bf16[16,512]{1,0:T(8,128)(2,1)} %get-tuple-element.36), channel_id=1, source_target_pairs={{0,63},{1,0},{2,1},{3,2},{4,3},{5,4},{6,5},{7,6},{8,7},{9,8},{10,9... | collective-permute-start | bytes 49160 | tf_op jit(solution)/shard_map/ppermute | solution.py:278
  13.2 10.0 %collective-permute-start.2 = (bf16[16,512]{1,0:T(8,128)(2,1)}, bf16[16,512]{1,0:T(8,128)(2,1)S(1)}, u32[]{:S(2)}, u32[]{:S(2)}) collective-permute-start(bf16[16,512]{1,0:T(8,128)(2,1)} %get-tuple-element.37), channel_id=1, source_target_pairs={{0,8},{1,9},{2,10},{3,11},{4,12},{5,13},{6,14},{7,15},{8,16},{9,17... | collective-permute-start | bytes 49160 | tf_op jit(solution)/shard_map/ppermute | solution.py:278
  15.2 8.6 %collective-permute-start.3 = (bf16[16,512]{1,0:T(8,128)(2,1)}, bf16[16,512]{1,0:T(8,128)(2,1)S(1)}, u32[]{:S(2)}, u32[]{:S(2)}) collective-permute-start(bf16[16,512]{1,0:T(8,128)(2,1)} %get-tuple-element.38), channel_id=1, source_target_pairs={{0,32},{1,33},{2,34},{3,35},{4,36},{5,37},{6,38},{7,39},{8,40},{9,... | collective-permute-start | bytes 49160 | tf_op jit(solution)/shard_map/ppermute | solution.py:278
  21.4 1.5 %copy-start.13 = (s32[1536]{0:T(1024)S(1)}, s32[1536]{0:T(1024)}, u32[]{:S(2)}) copy-start(s32[1536]{0:T(1024)} %param.12) | copy-start | bytes 18436
  21.4 2.4 %copy-start.2 = (bf16[1,512,512]{2,1,0:T(8,128)(2,1)S(1)}, bf16[1,512,512]{2,1,0:T(8,128)(2,1)}, u32[]{:S(2)}) copy-start(bf16[1,512,512]{2,1,0:T(8,128)(2,1)} %param.10) | copy-start | bytes 1572868
  21.4 2.4 %copy-start.7 = (bf16[512,512]{1,0:T(8,128)(2,1)S(1)}, bf16[512,512]{1,0:T(8,128)(2,1)}, u32[]{:S(2)}) copy-start(bf16[512,512]{1,0:T(8,128)(2,1)} %w_send_ref.1) | copy-start | bytes 1572868
  21.4 2.4 %copy-start.10 = (bf16[1,128,512]{2,1,0:T(8,128)(2,1)S(1)}, bf16[1,128,512]{2,1,0:T(8,128)(2,1)}, u32[]{:S(2)}) copy-start(bf16[1,128,512]{2,1,0:T(8,128)(2,1)} %param.9) | copy-start | bytes 393220
  23.8 1.2 copy-start.4
  25.0 1.2 copy-start.5
  30.8 8.7 %copy-start.8 = (f32[128,512]{1,0:T(8,128)}, f32[128,512]{1,0:T(8,128)S(1)}, u32[]{:S(2)}) copy-start(f32[128,512]{1,0:T(8,128)S(1)} %get-tuple-element.53.local_ref) | copy-start | bytes 786436
  30.8 8.7 %copy-start.12 = (bf16[16,512]{1,0:T(8,128)(2,1)}, bf16[16,512]{1,0:T(8,128)(2,1)S(1)}, u32[]{:S(2)}) copy-start(bf16[16,512]{1,0:T(8,128)(2,1)S(1)} %get-tuple-element.51) | copy-start | bytes 49156
  30.8 10.0 %collective-permute-start.4 = (bf16[800,512]{1,0:T(8,128)(2,1)S(1)}, bf16[800,512]{1,0:T(8,128)(2,1)S(1)}, u32[]{:S(2)}, u32[]{:S(2)}) collective-permute-start(bf16[800,512]{1,0:T(8,128)(2,1)S(1)} %get-tuple-element.43), channel_id=1, source_target_pairs={{0,1},{1,0},{2,3},{3,2},{4,5},{5,4},{6,7},{7,6},{8,9},{9,8},{10,11... | collective-permute-start | bytes 2457608 | tf_op jit(solution)/shard_map/ppermute | solution.py:289
  41.0 0.9 copy-start.6
  41.9 16.6 %all-to-all-start = ((bf16[4,208,512]{2,1,0:T(8,128)(2,1)}), bf16[4,208,512]{2,1,0:T(8,128)(2,1)S(1)}, u32[]{:S(2)}, u32[]{:S(2)}) async-start(bf16[4,208,512]{2,1,0:T(8,128)(2,1)} %copy-done.6), calls=%async_computation | async-start | bytes 1703936 | tf_op jit(solution)/shard_map/all_to_all | solution.py:293
  45.4 46.2 %copy-start.3 = (bf16[512,512]{1,0:T(8,128)(2,1)S(1)}, bf16[512,512]{1,0:T(8,128)(2,1)}, u32[]{:S(2)}) copy-start(bf16[512,512]{1,0:T(8,128)(2,1)} %w_recv_ref.1) | copy-start | bytes 1572868
  45.4 46.2 %copy-start.11 = (s32[1,4,16]{2,1,0:T(4,128)S(1)}, s32[1,4,16]{2,1,0:T(4,128)}, u32[]{:S(2)}) copy-start(s32[1,4,16]{2,1,0:T(4,128)} %param.13) | copy-start | bytes 772
  45.4 14.5 %collective-permute-start.5 = (bf16[16,512]{1,0:T(8,128)(2,1)}, bf16[16,512]{1,0:T(8,128)(2,1)S(1)}, u32[]{:S(2)}, u32[]{:S(2)}) collective-permute-start(bf16[16,512]{1,0:T(8,128)(2,1)} %get-tuple-element.49), channel_id=1, source_target_pairs={{0,63},{1,2},{2,1},{3,4},{4,3},{5,6},{6,5},{7,8},{8,7},{9,10},{10,... | collective-permute-start | bytes 49160 | tf_op jit(solution)/shard_map/ppermute | solution.py:283
  49.4 10.5 %collective-permute-start.6 = (bf16[16,512]{1,0:T(8,128)(2,1)}, bf16[16,512]{1,0:T(8,128)(2,1)S(1)}, u32[]{:S(2)}, u32[]{:S(2)}) collective-permute-start(bf16[16,512]{1,0:T(8,128)(2,1)} %get-tuple-element.50), channel_id=1, source_target_pairs={{0,56},{1,57},{2,58},{3,59},{4,60},{5,61},{6,62},{7,63},{8,0},{9,1... | collective-permute-start | bytes 49160 | tf_op jit(solution)/shard_map/ppermute | solution.py:278
  54.3 8.6 %collective-permute-start.7 = (bf16[16,512]{1,0:T(8,128)(2,1)}, bf16[16,512]{1,0:T(8,128)(2,1)S(1)}, u32[]{:S(2)}, u32[]{:S(2)}) collective-permute-start(bf16[16,512]{1,0:T(8,128)(2,1)} %copy-done.12), channel_id=1, source_target_pairs={{0,32},{1,33},{2,34},{3,35},{4,36},{5,37},{6,38},{7,39},{8,40},{9,... | collective-permute-start | bytes 49160 | tf_op jit(solution)/shard_map/ppermute | solution.py:278
  59.9 31.7 %copy-start.9 = (f32[128,512]{1,0:T(8,128)S(1)}, f32[128,512]{1,0:T(8,128)}, u32[]{:S(2)}) copy-start(f32[128,512]{1,0:T(8,128)} %copy-done.8) | copy-start | bytes 786436
  87.0 17.2 %all-to-all-start.2 = ((bf16[64,16,128]{2,1,0:T(8,128)(2,1)}), bf16[64,16,128]{2,1,0:T(8,128)(2,1)S(1)}, u32[]{:S(2)}, u32[]{:S(2)}) async-start(bf16[64,16,128]{2,1,0:T(8,128)(2,1)} %broadcast_in_dim.8), calls=%async_computation.2 | async-start | bytes 524288 | tf_op jit(solution)/shard_map/all_to_all | solution.py:293
  118.0 8.7 %collective-permute-start.8 = (bf16[3,1,256,512]{3,2,1,0:T(8,128)(2,1)S(1)}, bf16[3,1,256,512]{3,2,1,0:T(8,128)(2,1)S(1)}, u32[]{:S(2)}, u32[]{:S(2)}) collective-permute-start(bf16[3,1,256,512]{3,2,1,0:T(8,128)(2,1)S(1)} %bitcast.43), channel_id=1, source_target_pairs={{0,1},{1,0},{2,3},{3,2},{4,5},{5,4},{6,7},{7,6},{8,9},{9,8},{10,11... | collective-permute-start | bytes 2359304 | tf_op jit(solution)/shard_map/ppermute | solution.py:289

commit v4 on v3

--- a/solution.py
+++ b/solution.py
@@ -324,16 +324,17 @@
     came = swap_cores(send)
     keep = keep_step(core_ref, known, slot, grid_rows, recv_grad, node, upstream)
     packed, near = pack_step(keep, came, send[768:784])
-    packed, *leaving = lax.optimization_barrier((packed, *leaving))
-
-    next_chip = swap_chips(leaving[0])
-    far = shift_space(leaving[1], -offsets[2])
-    last = shift_space(leaving[2], -offsets[3])
+    packed, *early = lax.optimization_barrier((packed, *leaving[:2]))
+
+    next_chip = swap_chips(early[0])
+    far = shift_space(early[1], -offsets[2])
     line = line_step(exchange(packed, "x"))
-    line, next_chip, far, last = lax.optimization_barrier((line, next_chip, far, last))
+    line, next_chip, far = lax.optimization_barrier((line, next_chip, far))
 
     factor = float(lax.axis_size("dp") * pieces * 512) ** (-0.5)
     total = jnp.sum(exchange(line, PLANE).astype(F32), axis=0) * factor
+    total, *later = lax.optimization_barrier((total, *leaving[2:]))
+    last = shift_space(later[0], -offsets[3])
     grad_bias = total[12:].reshape(512)
     plane = gather_pieces(total.astype(BF), PLANE)[:, :12].reshape(16, 4, 12, 128)
     plane = plane.transpose(0, 2, 1, 3).reshape(192, 512)

time: 129 us -> 124 us (0.961)
  waiting for transfers between devices: 17.2 us -> 11.2 us
  starting transfers between devices: 52.3 us -> 56 us
  blocking collectives: 36.9 us -> 34.7 us
    all_to_all x2, waiting for transfers between devices: 10.4 us -> 5.61 us  [exchange(): return lax.all_to_all(value, axes, split_axis=0, concat_axis=0, tiled=True)]
    ppermute x6, starting transfers between devices: 25.3 us -> 27.9 us  [shift_space(): lax.ppermute(value, SPACE, [(i, (i + offset) % pieces) for i in range(pie...]
    all_to_all x2, blocking collectives: 36.9 us -> 34.7 us  [exchange(): return lax.all_to_all(value, axes, split_axis=0, concat_axis=0, tiled=True)]
  transfers between devices with their start and end apart: 11 -> 11, of which waited for: 5 -> 6; matrix products, arithmetic and copies ran while one was open for 4% -> 4% of each run, Pallas kernels for 3% -> 3%
where the time goes in v4:
time: 124 us; the launch traced here: 123 us
  starting transfers between devices  56 us (45%)
  blocking collectives  34.7 us (28%)
  waiting for transfers between devices  11.2 us (9%)
  Pallas kernels  9.79 us (8%)
  local copies, waits for them, and re-layouts  5.28 us (4%)
  matrix products  4.07 us (3%)
  other arithmetic  1.37 us (1%)
    all_to_all x2, blocking collectives, exchange(): return lax.all_to_all(value, axes, split_axis=0, concat_axis=0, tiled=True)  34.7 us
    ppermute x6, starting transfers between devices, shift_space(): lax.ppermute(value, SPACE, [(i, (i + offset) % pieces) for i in range(pie...  27.9 us
    ppermute x2, starting transfers between devices, swap_cores(): return lax.ppermute(value, 'core', [(0, 1), (1, 0)])  15 us
    all_to_all x2, starting transfers between devices, exchange(): return lax.all_to_all(value, axes, split_axis=0, concat_axis=0, tiled=True)  9.15 us
    all_to_all x2, waiting for transfers between devices, exchange(): return lax.all_to_all(value, axes, split_axis=0, concat_axis=0, tiled=True)  5.61 us
    pallas_call x1, Pallas kernels, edge_step(): pl.pallas_call(edge_kernel, out_shape=(shape(800, BF), shape(192, BF), sh...  4.43 us
    ppermute x1, starting transfers between devices, swap_chips(): lax.ppermute(value, SPACE, [(i, (i - 1 + 2 * (i % 2)) % pieces) for i in...  3.97 us
    unnamed x31, local copies, waits for them, and re-layouts  3.52 us
  transfers between devices with their start and end apart: 11, of which 6 were waited for; matrix products, arithmetic and copies ran while one was open for 4% of the time, Pallas kernels for 3%

profile of v4, /device:TPU:1, one launch (start us, length us, event | category | flops | bytes accessed | tf_op | source)
XLA Modules:
  0.0 123.4 jit_solution(5406616060380125502)
XLA Ops:
  0.7 1.8 %pick_step.1 = (bf16[16,512]{1,0:T(8,128)(2,1)}, bf16[16,512]{1,0:T(8,128)(2,1)}, bf16[16,512]{1,0:T(8,128)(2,1)}, bf16[16,512]{1,0:T(8,128)(2,1)}) custom-call(s32[4,16]{1,0:T(4,128)} %bitcast.40, bf16[128,512]{1,0:T(8,128)(2,1)} %bitcast.38), custom_call_target="tpu_custom_call" | custom-call | flops 10000000 | bytes 200000 | tf_op jit(solution)/shard_map/pick_step/pallas_call | solution.py:227
  2.5 4.5 %collective-permute-start = (bf16[16,512]{1,0:T(8,128)(2,1)}, bf16[16,512]{1,0:T(8,128)(2,1)S(1)}, u32[]{:S(2)}, u32[]{:S(2)}) collective-permute-start(bf16[16,512]{1,0:T(8,128)(2,1)} %get-tuple-element.35), channel_id=1, source_target_pairs={{0,1},{1,2},{2,3},{3,4},{4,5},{5,6},{6,7},{7,8},{8,9},{9,10},{10,1... | collective-permute-start | bytes 49160 | tf_op jit(solution)/shard_map/ppermute | solution.py:278
  7.0 6.2 %collective-permute-start.1 = (bf16[16,512]{1,0:T(8,128)(2,1)}, bf16[16,512]{1,0:T(8,128)(2,1)S(1)}, u32[]{:S(2)}, u32[]{:S(2)}) collective-permute-start(bf16[16,512]{1,0:T(8,128)(2,1)} %get-tuple-element.36), channel_id=1, source_target_pairs={{0,63},{1,0},{2,1},{3,2},{4,3},{5,4},{6,5},{7,6},{8,7},{9,8},{10,9... | collective-permute-start | bytes 49160 | tf_op jit(solution)/shard_map/ppermute | solution.py:278
  13.2 1.9 %collective-permute-start.2 = (bf16[16,512]{1,0:T(8,128)(2,1)}, bf16[16,512]{1,0:T(8,128)(2,1)S(1)}, u32[]{:S(2)}, u32[]{:S(2)}) collective-permute-start(bf16[16,512]{1,0:T(8,128)(2,1)} %get-tuple-element.37), channel_id=1, source_target_pairs={{0,8},{1,9},{2,10},{3,11},{4,12},{5,13},{6,14},{7,15},{8,16},{9,17... | collective-permute-start | bytes 49160 | tf_op jit(solution)/shard_map/ppermute | solution.py:278
  15.2 3.6 %collective-permute-start.3 = (bf16[16,512]{1,0:T(8,128)(2,1)}, bf16[16,512]{1,0:T(8,128)(2,1)S(1)}, u32[]{:S(2)}, u32[]{:S(2)}) collective-permute-start(bf16[16,512]{1,0:T(8,128)(2,1)} %get-tuple-element.38), channel_id=1, source_target_pairs={{0,32},{1,33},{2,34},{3,35},{4,36},{5,37},{6,38},{7,39},{8,40},{9,... | collective-permute-start | bytes 49160 | tf_op jit(solution)/shard_map/ppermute | solution.py:278
  18.7 2.6 %convolution_add_fusion.recv_proj_hbm = f32[512,512]{1,0:T(8,128)} fusion(bf16[512,512]{1,0:T(8,128)(2,1)} %w_recv_ref.1, f32[512]{0:T(512)} %param.17, bf16[1,512,512]{2,1,0:T(8,128)(2,1)} %param.10), kind=kOutput, calls=%fused_computation.4 | convolution fusion | flops 268697600 | bytes 2099200 | tf_op jit(solution)/shard_map/dot_general | solution.py:313
  21.4 1.4 %fusion.2.agg_grad_hbm = f32[512,512]{1,0:T(8,128)} fusion(bf16[512,512]{1,0:T(8,128)(2,1)S(1)} %copy-done, bf16[1,512,512]{2,1,0:T(8,128)(2,1)S(1)} %copy-done.1), kind=kOutput, calls=%fused_computation.14 | convolution fusion | flops 268435456 | bytes 2097152 | tf_op jit(solution)/shard_map/dot_general | solution.py:316
  23.2 0.5 collective-permute-done.3.h3_ref
  23.8 1.2 copy-done.4
  25.0 1.2 copy-done.5
  26.2 4.4 %edge_step.1 = (bf16[800,512]{1,0:T(8,128)(2,1)S(1)}, bf16[192,512]{1,0:T(8,128)(2,1)S(1)}, bf16[192,512]{1,0:T(8,128)(2,1)S(1)}, bf16[512,512]{1,0:T(8,128)(2,1...) custom-call(s32[1]{0:T(128)} %bitcast.core_ref, ...), custom_call_target="tpu_custom_call" | custom-call | flops 3000000000 | bytes 6000000 | tf_op jit(solution)/shard_map/edge_step/pallas_call | solution.py:180
  30.7 8.1 %collective-permute-start.4 = (bf16[800,512]{1,0:T(8,128)(2,1)S(1)}, bf16[800,512]{1,0:T(8,128)(2,1)S(1)}, u32[]{:S(2)}, u32[]{:S(2)}) collective-permute-start(bf16[800,512]{1,0:T(8,128)(2,1)S(1)} %get-tuple-element.43), channel_id=1, source_target_pairs={{0,1},{1,0},{2,3},{3,2},{4,5},{5,4},{6,7},{7,6},{8,9},{9,8},{10,11... | collective-permute-start | bytes 2457608 | tf_op jit(solution)/shard_map/ppermute | solution.py:289
  38.8 0.5 keep_step.1.keep_ref
  39.4 1.4 %collective-permute-done.4.came_ref = bf16[800,512]{1,0:T(8,128)(2,1)S(1)} collective-permute-done((bf16[800,512]{1,0:T(8,128)(2,1)S(1)}, bf16[800,512]{1,0:T(8,128)(2,1)S(1)}, u32[]{:S(2)}, u32[]{:S(2)}) %collective-permute-start.4) | collective-permute-done | bytes 819232 | tf_op jit(solution)/shard_map/ppermute | solution.py:289
  40.9 0.9 copy-done.6
  41.8 3.5 %all-to-all-start = ((bf16[4,208,512]{2,1,0:T(8,128)(2,1)}), bf16[4,208,512]{2,1,0:T(8,128)(2,1)S(1)}, u32[]{:S(2)}, u32[]{:S(2)}) async-start(bf16[4,208,512]{2,1,0:T(8,128)(2,1)} %copy-done.6), calls=%async_computation | async-start | bytes 1703936 | tf_op jit(solution)/shard_map/all_to_all | solution.py:293
  45.3 4.0 %collective-permute-start.5 = (bf16[16,512]{1,0:T(8,128)(2,1)}, bf16[16,512]{1,0:T(8,128)(2,1)S(1)}, u32[]{:S(2)}, u32[]{:S(2)}) collective-permute-start(bf16[16,512]{1,0:T(8,128)(2,1)} %get-tuple-element.48), channel_id=1, source_target_pairs={{0,63},{1,2},{2,1},{3,4},{4,3},{5,6},{6,5},{7,8},{8,7},{9,10},{10,... | collective-permute-start | bytes 49160 | tf_op jit(solution)/shard_map/ppermute | solution.py:283
  49.3 4.9 %collective-permute-start.6 = (bf16[16,512]{1,0:T(8,128)(2,1)}, bf16[16,512]{1,0:T(8,128)(2,1)S(1)}, u32[]{:S(2)}, u32[]{:S(2)}) collective-permute-start(bf16[16,512]{1,0:T(8,128)(2,1)} %copy-done.12), channel_id=1, source_target_pairs={{0,56},{1,57},{2,58},{3,59},{4,60},{5,61},{6,62},{7,63},{8,0},{9,1... | collective-permute-start | bytes 49160 | tf_op jit(solution)/shard_map/ppermute | solution.py:278
  54.2 3.8 %all-to-all-done.packed_hbm = bf16[4,208,512]{2,1,0:T(8,128)(2,1)S(1)} async-done(((bf16[4,208,512]{2,1,0:T(8,128)(2,1)}), bf16[4,208,512]{2,1,0:T(8,128)(2,1)S(1)}, u32[]{:S(2)}, u32[]{:S(2)}) %all-to-all-start) | async-done | bytes 852000 | tf_op jit(solution)/shard_map/all_to_all | solution.py:293
  58.0 1.3 %line_step.1 = bf16[64,16,128]{2,1,0:T(8,128)(2,1)S(1)} custom-call(bf16[4,208,512]{2,1,0:T(8,128)(2,1)S(1)} %all-to-all-done.packed_hbm), custom_call_target="tpu_custom_call" | custom-call | flops 500000 | bytes 1000000 | tf_op jit(solution)/shard_map/line_step/pallas_call | solution.py:243
  59.4 24.0 %all_to_all.20 = bf16[64,16,128]{2,1,0:T(8,128)(2,1)S(1)} all-to-all(bf16[64,16,128]{2,1,0:T(8,128)(2,1)S(1)} %line_step.1), channel_id=1, replica_groups=mesh['dp'=8,'y'=8,'x'=4,'core'=2] {'dp','y'}, dimensions={0} | all-to-all | bytes 524288 | tf_op jit(solution)/shard_map/all_to_all | solution.py:293
  83.4 0.7 broadcast_in_dim.8
  84.2 5.6 %all-to-all-start.2 = ((bf16[64,16,128]{2,1,0:T(8,128)(2,1)}), bf16[64,16,128]{2,1,0:T(8,128)(2,1)S(1)}, u32[]{:S(2)}, u32[]{:S(2)}) async-start(bf16[64,16,128]{2,1,0:T(8,128)(2,1)} %broadcast_in_dim.8), calls=%async_computation.2 | async-start | bytes 524288 | tf_op jit(solution)/shard_map/all_to_all | solution.py:293
  89.8 6.8 %collective-permute-start.7 = (bf16[16,512]{1,0:T(8,128)(2,1)S(1)}, bf16[16,512]{1,0:T(8,128)(2,1)S(1)}, u32[]{:S(2)}, u32[]{:S(2)}) collective-permute-start(bf16[16,512]{1,0:T(8,128)(2,1)S(1)} %get-tuple-element.57), channel_id=1, source_target_pairs={{0,32},{1,33},{2,34},{3,35},{4,36},{5,37},{6,38},{7,39},{8,40},{9,... | collective-permute-start | bytes 49160 | tf_op jit(solution)/shard_map/ppermute | solution.py:278
  96.7 0.6 slice_bitcast_fusion
  97.2 1.8 %collective-permute-done.7.last_ref = bf16[16,512]{1,0:T(8,128)(2,1)S(1)} collective-permute-done((bf16[16,512]{1,0:T(8,128)(2,1)S(1)}, bf16[16,512]{1,0:T(8,128)(2,1)S(1)}, u32[]{:S(2)}, u32[]{:S(2)}) %collective-permute-start.7) | collective-permute-done | bytes 16416 | tf_op jit(solution)/shard_map/ppermute | solution.py:278
  99.0 1.5 %tail_step.1 = (f32[128,512]{1,0:T(8,128)}, bf16[512,512]{1,0:T(8,128)(2,1)}) custom-call(s32[1]{0:T(128)} %bitcast.core_ref, s32[4,16]{1,0:T(4,128)S(1)} %bitcast.41, f32[128,512]{1,0:T(8,128)S(1)} %copy-done.9, bf16[16,512]{1,0:T(8,128)(2,1)S(1)} %get-tuple-element.54.near_ref, bf16[16,512]{1,0:T(8,128)(2,1)S(1)} %collective-permute-done.5.next_ref, ...), custom_call_target="tpu_custom_call" | custom-call | flops 400000000 | bytes 3000000 | tf_op jit(solution)/shard_map/tail_step/pallas_call | solution.py:261
  100.5 1.8 %all-to-all-done.2 = bf16[64,16,128]{2,1,0:T(8,128)(2,1)S(1)} async-done(((bf16[64,16,128]{2,1,0:T(8,128)(2,1)}), bf16[64,16,128]{2,1,0:T(8,128)(2,1)S(1)}, u32[]{:S(2)}, u32[]{:S(2)}) %all-to-all-start.2) | async-done | bytes 262176 | tf_op jit(solution)/shard_map/all_to_all | solution.py:293
  102.5 10.8 %all_to_all.21 = bf16[4,192,512]{2,1,0:T(8,128)(2,1)S(1)} all-to-all(bf16[4,192,512]{2,1,0:T(8,128)(2,1)S(1)} %broadcast_in_dim.22), channel_id=1, replica_groups=mesh['dp'=8,'y'=8,'x'=4,'core'=2] {'x'}, dimensions={0} | all-to-all | bytes 1572864 | tf_op jit(solution)/shard_map/all_to_all | solution.py:293
  113.3 6.9 %collective-permute-start.8 = (bf16[3,1,256,512]{3,2,1,0:T(8,128)(2,1)S(1)}, bf16[3,1,256,512]{3,2,1,0:T(8,128)(2,1)S(1)}, u32[]{:S(2)}, u32[]{:S(2)}) collective-permute-start(bf16[3,1,256,512]{3,2,1,0:T(8,128)(2,1)S(1)} %bitcast.43), channel_id=1, source_target_pairs={{0,1},{1,0},{2,3},{3,2},{4,5},{5,4},{6,7},{7,6},{8,9},{9,8},{10,11... | collective-permute-start | bytes 2359304 | tf_op jit(solution)/shard_map/ppermute | solution.py:289
  120.2 1.9 %collective-permute-done.8 = bf16[3,1,256,512]{3,2,1,0:T(8,128)(2,1)S(1)} collective-permute-done((bf16[3,1,256,512]{3,2,1,0:T(8,128)(2,1)S(1)}, bf16[3,1,256,512]{3,2,1,0:T(8,128)(2,1)S(1)}, u32[]{:S(2)}, u32[]{:S(2)}) %collective-permute-start.8) | collective-permute-done | bytes 786464 | tf_op jit(solution)/shard_map/ppermute | solution.py:289
  122.2 1.2 pad_maximum_fusion
  (43 shorter events, 0.9 us)
Async XLA Ops:
  0.6 20.7 %copy-start = (bf16[512,512]{1,0:T(8,128)(2,1)S(1)}, bf16[512,512]{1,0:T(8,128)(2,1)}, u32[]{:S(2)}) copy-start(bf16[512,512]{1,0:T(8,128)(2,1)} %param.16) | copy-start | bytes 1572868
  0.6 20.7 %copy-start.1 = (bf16[1,512,512]{2,1,0:T(8,128)(2,1)S(1)}, bf16[1,512,512]{2,1,0:T(8,128)(2,1)}, u32[]{:S(2)}) copy-start(bf16[1,512,512]{2,1,0:T(8,128)(2,1)} %param.11) | copy-start | bytes 1572868
  2.5 20.7 %collective-permute-start = (bf16[16,512]{1,0:T(8,128)(2,1)}, bf16[16,512]{1,0:T(8,128)(2,1)S(1)}, u32[]{:S(2)}, u32[]{:S(2)}) collective-permute-start(bf16[16,512]{1,0:T(8,128)(2,1)} %get-tuple-element.35), channel_id=1, source_target_pairs={{0,1},{1,2},{2,3},{3,4},{4,5},{5,6},{6,7},{7,8},{8,9},{9,10},{10,1... | collective-permute-start | bytes 49160 | tf_op jit(solution)/shard_map/ppermute | solution.py:278
  7.0 16.2 %collective-permute-start.1 = (bf16[16,512]{1,0:T(8,128)(2,1)}, bf16[16,512]{1,0:T(8,128)(2,1)S(1)}, u32[]{:S(2)}, u32[]{:S(2)}) collective-permute-start(bf16[16,512]{1,0:T(8,128)(2,1)} %get-tuple-element.36), channel_id=1, source_target_pairs={{0,63},{1,0},{2,1},{3,2},{4,3},{5,4},{6,5},{7,6},{8,7},{9,8},{10,9... | collective-permute-start | bytes 49160 | tf_op jit(solution)/shard_map/ppermute | solution.py:278
  13.2 10.0 %collective-permute-start.2 = (bf16[16,512]{1,0:T(8,128)(2,1)}, bf16[16,512]{1,0:T(8,128)(2,1)S(1)}, u32[]{:S(2)}, u32[]{:S(2)}) collective-permute-start(bf16[16,512]{1,0:T(8,128)(2,1)} %get-tuple-element.37), channel_id=1, source_target_pairs={{0,8},{1,9},{2,10},{3,11},{4,12},{5,13},{6,14},{7,15},{8,16},{9,17... | collective-permute-start | bytes 49160 | tf_op jit(solution)/shard_map/ppermute | solution.py:278
  15.2 8.6 %collective-permute-start.3 = (bf16[16,512]{1,0:T(8,128)(2,1)}, bf16[16,512]{1,0:T(8,128)(2,1)S(1)}, u32[]{:S(2)}, u32[]{:S(2)}) collective-permute-start(bf16[16,512]{1,0:T(8,128)(2,1)} %get-tuple-element.38), channel_id=1, source_target_pairs={{0,32},{1,33},{2,34},{3,35},{4,36},{5,37},{6,38},{7,39},{8,40},{9,... | collective-permute-start | bytes 49160 | tf_op jit(solution)/shard_map/ppermute | solution.py:278
  21.4 1.5 %copy-start.13 = (s32[1536]{0:T(1024)S(1)}, s32[1536]{0:T(1024)}, u32[]{:S(2)}) copy-start(s32[1536]{0:T(1024)} %param.12) | copy-start | bytes 18436
  21.4 2.4 %copy-start.2 = (bf16[1,512,512]{2,1,0:T(8,128)(2,1)S(1)}, bf16[1,512,512]{2,1,0:T(8,128)(2,1)}, u32[]{:S(2)}) copy-start(bf16[1,512,512]{2,1,0:T(8,128)(2,1)} %param.10) | copy-start | bytes 1572868
  21.4 2.4 %copy-start.7 = (bf16[512,512]{1,0:T(8,128)(2,1)S(1)}, bf16[512,512]{1,0:T(8,128)(2,1)}, u32[]{:S(2)}) copy-start(bf16[512,512]{1,0:T(8,128)(2,1)} %w_send_ref.1) | copy-start | bytes 1572868
  21.4 2.4 %copy-start.10 = (bf16[1,128,512]{2,1,0:T(8,128)(2,1)S(1)}, bf16[1,128,512]{2,1,0:T(8,128)(2,1)}, u32[]{:S(2)}) copy-start(bf16[1,128,512]{2,1,0:T(8,128)(2,1)} %param.9) | copy-start | bytes 393220
  23.8 1.2 copy-start.4
  25.0 1.2 copy-start.5
  30.7 8.7 %copy-start.8 = (f32[128,512]{1,0:T(8,128)}, f32[128,512]{1,0:T(8,128)S(1)}, u32[]{:S(2)}) copy-start(f32[128,512]{1,0:T(8,128)S(1)} %get-tuple-element.53.local_ref) | copy-start | bytes 786436
  30.7 8.7 %copy-start.12 = (bf16[16,512]{1,0:T(8,128)(2,1)}, bf16[16,512]{1,0:T(8,128)(2,1)S(1)}, u32[]{:S(2)}) copy-start(bf16[16,512]{1,0:T(8,128)(2,1)S(1)} %get-tuple-element.49) | copy-start | bytes 49156
  30.7 10.1 %collective-permute-start.4 = (bf16[800,512]{1,0:T(8,128)(2,1)S(1)}, bf16[800,512]{1,0:T(8,128)(2,1)S(1)}, u32[]{:S(2)}, u32[]{:S(2)}) collective-permute-start(bf16[800,512]{1,0:T(8,128)(2,1)S(1)} %get-tuple-element.43), channel_id=1, source_target_pairs={{0,1},{1,0},{2,3},{3,2},{4,5},{5,4},{6,7},{7,6},{8,9},{9,8},{10,11... | collective-permute-start | bytes 2457608 | tf_op jit(solution)/shard_map/ppermute | solution.py:289
  40.9 0.9 copy-start.6
  41.8 16.2 %all-to-all-start = ((bf16[4,208,512]{2,1,0:T(8,128)(2,1)}), bf16[4,208,512]{2,1,0:T(8,128)(2,1)S(1)}, u32[]{:S(2)}, u32[]{:S(2)}) async-start(bf16[4,208,512]{2,1,0:T(8,128)(2,1)} %copy-done.6), calls=%async_computation | async-start | bytes 1703936 | tf_op jit(solution)/shard_map/all_to_all | solution.py:293
  45.3 53.7 %copy-start.3 = (bf16[512,512]{1,0:T(8,128)(2,1)S(1)}, bf16[512,512]{1,0:T(8,128)(2,1)}, u32[]{:S(2)}) copy-start(bf16[512,512]{1,0:T(8,128)(2,1)} %w_recv_ref.1) | copy-start | bytes 1572868
  45.3 53.7 %copy-start.11 = (s32[1,4,16]{2,1,0:T(4,128)S(1)}, s32[1,4,16]{2,1,0:T(4,128)}, u32[]{:S(2)}) copy-start(s32[1,4,16]{2,1,0:T(4,128)} %param.13) | copy-start | bytes 772
  45.3 14.0 %collective-permute-start.5 = (bf16[16,512]{1,0:T(8,128)(2,1)}, bf16[16,512]{1,0:T(8,128)(2,1)S(1)}, u32[]{:S(2)}, u32[]{:S(2)}) collective-permute-start(bf16[16,512]{1,0:T(8,128)(2,1)} %get-tuple-element.48), channel_id=1, source_target_pairs={{0,63},{1,2},{2,1},{3,4},{4,3},{5,6},{6,5},{7,8},{8,7},{9,10},{10,... | collective-permute-start | bytes 49160 | tf_op jit(solution)/shard_map/ppermute | solution.py:283
  49.3 10.1 %collective-permute-start.6 = (bf16[16,512]{1,0:T(8,128)(2,1)}, bf16[16,512]{1,0:T(8,128)(2,1)S(1)}, u32[]{:S(2)}, u32[]{:S(2)}) collective-permute-start(bf16[16,512]{1,0:T(8,128)(2,1)} %copy-done.12), channel_id=1, source_target_pairs={{0,56},{1,57},{2,58},{3,59},{4,60},{5,61},{6,62},{7,63},{8,0},{9,1... | collective-permute-start | bytes 49160 | tf_op jit(solution)/shard_map/ppermute | solution.py:278
  59.3 39.7 %copy-start.9 = (f32[128,512]{1,0:T(8,128)S(1)}, f32[128,512]{1,0:T(8,128)}, u32[]{:S(2)}) copy-start(f32[128,512]{1,0:T(8,128)} %copy-done.8) | copy-start | bytes 786436
  84.2 18.1 %all-to-all-start.2 = ((bf16[64,16,128]{2,1,0:T(8,128)(2,1)}), bf16[64,16,128]{2,1,0:T(8,128)(2,1)S(1)}, u32[]{:S(2)}, u32[]{:S(2)}) async-start(bf16[64,16,128]{2,1,0:T(8,128)(2,1)} %broadcast_in_dim.8), calls=%async_computation.2 | async-start | bytes 524288 | tf_op jit(solution)/shard_map/all_to_all | solution.py:293
  89.8 9.2 %collective-permute-start.7 = (bf16[16,512]{1,0:T(8,128)(2,1)S(1)}, bf16[16,512]{1,0:T(8,128)(2,1)S(1)}, u32[]{:S(2)}, u32[]{:S(2)}) collective-permute-start(bf16[16,512]{1,0:T(8,128)(2,1)S(1)} %get-tuple-element.57), channel_id=1, source_target_pairs={{0,32},{1,33},{2,34},{3,35},{4,36},{5,37},{6,38},{7,39},{8,40},{9,... | collective-permute-start | bytes 49160 | tf_op jit(solution)/shard_map/ppermute | solution.py:278
  113.3 8.8 %collective-permute-start.8 = (bf16[3,1,256,512]{3,2,1,0:T(8,128)(2,1)S(1)}, bf16[3,1,256,512]{3,2,1,0:T(8,128)(2,1)S(1)}, u32[]{:S(2)}, u32[]{:S(2)}) collective-permute-start(bf16[3,1,256,512]{3,2,1,0:T(8,128)(2,1)S(1)} %bitcast.43), channel_id=1, source_target_pairs={{0,1},{1,0},{2,3},{3,2},{4,5},{5,4},{6,7},{7,6},{8,9},{9,8},{10,11... | collective-permute-start | bytes 2359304 | tf_op jit(solution)/shard_map/ppermute | solution.py:289

commit v5 on v4

--- a/solution.py
+++ b/solution.py
@@ -146,14 +146,16 @@
         out_ref[piece] = tile.astype(BF)
 
 
-def tail_kernel(
-    core_ref, rows_ref, local_ref, near_ref, next_ref, far_ref, last_ref, w_send_ref,
-    upstream_ref, recv_ref, w_recv_ref, mesh_ref, grid_ref,
-):
+def grid_kernel(upstream_ref, recv_ref, w_recv_ref, grid_ref):
     product = lax.dot_general(
         recv_ref[...], w_recv_ref[...], (((1,), (1,)), ((), ())), preferred_element_type=F32
     )
     grid_ref[...] = (upstream_ref[...].astype(F32) + product).astype(BF)
+
+
+def mesh_kernel(
+    core_ref, rows_ref, local_ref, near_ref, next_ref, far_ref, last_ref, w_send_ref, mesh_ref
+):
     first_core = core_ref[0] == 0
     near, other = near_ref[...], next_ref[...]
     blocks = (
@@ -257,15 +259,27 @@
     )(packed)
 
 
-def tail_step(*args):
-    return pl.pallas_call(
-        tail_kernel,
-        out_shape=(shape(128, F32), shape(512, BF)),
-        in_specs=[SM] + [VM] * 10,
-        out_specs=(VM,) * 2,
-        compiler_params=limit(8),
-        name="tail_step",
-        cost_estimate=pl.CostEstimate(flops=400_000_000, bytes_accessed=3_000_000, transcendentals=0),
+def grid_step(*args):
+    return pl.pallas_call(
+        grid_kernel,
+        out_shape=shape(512, BF),
+        in_specs=[VM] * 3,
+        out_specs=VM,
+        compiler_params=limit(6),
+        name="grid_step",
+        cost_estimate=pl.CostEstimate(flops=300_000_000, bytes_accessed=2_000_000, transcendentals=0),
+    )(*args)
+
+
+def mesh_step(*args):
+    return pl.pallas_call(
+        mesh_kernel,
+        out_shape=shape(128, F32),
+        in_specs=[SM] + [VM] * 7,
+        out_specs=VM,
+        compiler_params=limit(6),
+        name="mesh_step",
+        cost_estimate=pl.CostEstimate(flops=80_000_000, bytes_accessed=1_000_000, transcendentals=0),
     )(*args)
 
 
@@ -329,7 +343,8 @@
     next_chip = swap_chips(early[0])
     far = shift_space(early[1], -offsets[2])
     line = line_step(exchange(packed, "x"))
-    line, next_chip, far = lax.optimization_barrier((line, next_chip, far))
+    grad_grid = grid_step(upstream, recv_grad, w_recv)
+    line, next_chip, far, grad_grid = lax.optimization_barrier((line, next_chip, far, grad_grid))
 
     factor = float(lax.axis_size("dp") * pieces * 512) ** (-0.5)
     total = jnp.sum(exchange(line, PLANE).astype(F32), axis=0) * factor
@@ -338,15 +353,11 @@
     grad_bias = total[12:].reshape(512)
     plane = gather_pieces(total.astype(BF), PLANE)[:, :12].reshape(16, 4, 12, 128)
     plane = plane.transpose(0, 2, 1, 3).reshape(192, 512)
-    grad_mesh, grad_grid = tail_step(
-        core_ref, send_rows[0], local, near, next_chip, far, last, w_send, upstream, recv_grad, w_recv
-    )
-    plane, grad_mesh, grad_grid, grad_bias = lax.optimization_barrier(
-        (plane, grad_mesh, grad_grid, grad_bias)
-    )
+    plane, last, grad_bias = lax.optimization_barrier((plane, last, grad_bias))
 
     half = gather_pieces(plane, "x").reshape(3, 1, 256, 512)
     partner = swap_cores(half)
+    grad_mesh = mesh_step(core_ref, send_rows[0], local, near, next_chip, far, last, w_send)
     low = jnp.where(core == 0, half, partner)
     high = jnp.where(core == 0, partner, half)
     whole = jnp.concatenate([low, high], axis=1).reshape(3, 512, 512)

time: 124 us -> 124 us (level)
    all_to_all x2, waiting for transfers between devices: 5.61 us -> 7.77 us  [exchange(): return lax.all_to_all(value, axes, split_axis=0, concat_axis=0, tiled=True)]
    ppermute x6, waiting for transfers between devices: 2.32 us -> 0.54 us  [shift_space(): lax.ppermute(value, SPACE, [(i, (i + offset) % pieces) for i in range(pie...]
    unnamed x31 -> x29, local copies, waits for them, and re-layouts: 3.52 us -> 3.51 us
  transfers between devices with their start and end apart: 11 -> 11, of which waited for: 6 -> 5; matrix products, arithmetic and copies ran while one was open for 4% -> 4% of each run, Pallas kernels for 3% -> 4%
where the time goes in v5:
time: 124 us; the launch traced here: 123 us
  starting transfers between devices  55.9 us (45%)
  blocking collectives  34.6 us (28%)
  Pallas kernels  10.8 us (9%)
  waiting for transfers between devices  10.3 us (8%)
  local copies, waits for them, and re-layouts  5.27 us (4%)
  matrix products  4.09 us (3%)
  other arithmetic  1.37 us (1%)
    all_to_all x2, blocking collectives, exchange(): return lax.all_to_all(value, axes, split_axis=0, concat_axis=0, tiled=True)  34.6 us
    ppermute x6, starting transfers between devices, shift_space(): lax.ppermute(value, SPACE, [(i, (i + offset) % pieces) for i in range(pie...  27.9 us
    ppermute x2, starting transfers between devices, swap_cores(): return lax.ppermute(value, 'core', [(0, 1), (1, 0)])  15 us
    all_to_all x2, starting transfers between devices, exchange(): return lax.all_to_all(value, axes, split_axis=0, concat_axis=0, tiled=True)  9.15 us
    all_to_all x2, waiting for transfers between devices, exchange(): return lax.all_to_all(value, axes, split_axis=0, concat_axis=0, tiled=True)  7.77 us
    pallas_call x1, Pallas kernels, edge_step(): pl.pallas_call(edge_kernel, out_shape=(shape(800, BF), shape(192, BF), sh...  4.43 us
    ppermute x1, starting transfers between devices, swap_chips(): lax.ppermute(value, SPACE, [(i, (i - 1 + 2 * (i % 2)) % pieces) for i in...  3.86 us
    unnamed x29, local copies, waits for them, and re-layouts  3.51 us
  transfers between devices with their start and end apart: 11, of which 5 were waited for; matrix products, arithmetic and copies ran while one was open for 4% of the time, Pallas kernels for 4%

profile of v5, /device:TPU:1, one launch (start us, length us, event | category | flops | bytes accessed | tf_op | source)
XLA Modules:
  0.0 123.4 jit_solution(4322857749997508698)
XLA Ops:
  0.7 1.8 %pick_step.1 = (bf16[16,512]{1,0:T(8,128)(2,1)}, bf16[16,512]{1,0:T(8,128)(2,1)}, bf16[16,512]{1,0:T(8,128)(2,1)}, bf16[16,512]{1,0:T(8,128)(2,1)}) custom-call(s32[4,16]{1,0:T(4,128)} %bitcast.40, bf16[128,512]{1,0:T(8,128)(2,1)} %bitcast.38), custom_call_target="tpu_custom_call" | custom-call | flops 10000000 | bytes 200000 | tf_op jit(solution)/shard_map/pick_step/pallas_call | solution.py:229
  2.5 4.5 %collective-permute-start = (bf16[16,512]{1,0:T(8,128)(2,1)}, bf16[16,512]{1,0:T(8,128)(2,1)S(1)}, u32[]{:S(2)}, u32[]{:S(2)}) collective-permute-start(bf16[16,512]{1,0:T(8,128)(2,1)} %get-tuple-element.33), channel_id=1, source_target_pairs={{0,1},{1,2},{2,3},{3,4},{4,5},{5,6},{6,7},{7,8},{8,9},{9,10},{10,1... | collective-permute-start | bytes 49160 | tf_op jit(solution)/shard_map/ppermute | solution.py:292
  7.0 6.2 %collective-permute-start.1 = (bf16[16,512]{1,0:T(8,128)(2,1)}, bf16[16,512]{1,0:T(8,128)(2,1)S(1)}, u32[]{:S(2)}, u32[]{:S(2)}) collective-permute-start(bf16[16,512]{1,0:T(8,128)(2,1)} %get-tuple-element.34), channel_id=1, source_target_pairs={{0,63},{1,0},{2,1},{3,2},{4,3},{5,4},{6,5},{7,6},{8,7},{9,8},{10,9... | collective-permute-start | bytes 49160 | tf_op jit(solution)/shard_map/ppermute | solution.py:292
  13.2 1.9 %collective-permute-start.2 = (bf16[16,512]{1,0:T(8,128)(2,1)}, bf16[16,512]{1,0:T(8,128)(2,1)S(1)}, u32[]{:S(2)}, u32[]{:S(2)}) collective-permute-start(bf16[16,512]{1,0:T(8,128)(2,1)} %get-tuple-element.35), channel_id=1, source_target_pairs={{0,8},{1,9},{2,10},{3,11},{4,12},{5,13},{6,14},{7,15},{8,16},{9,17... | collective-permute-start | bytes 49160 | tf_op jit(solution)/shard_map/ppermute | solution.py:292
  15.2 3.6 %collective-permute-start.3 = (bf16[16,512]{1,0:T(8,128)(2,1)}, bf16[16,512]{1,0:T(8,128)(2,1)S(1)}, u32[]{:S(2)}, u32[]{:S(2)}) collective-permute-start(bf16[16,512]{1,0:T(8,128)(2,1)} %get-tuple-element.36), channel_id=1, source_target_pairs={{0,32},{1,33},{2,34},{3,35},{4,36},{5,37},{6,38},{7,39},{8,40},{9,... | collective-permute-start | bytes 49160 | tf_op jit(solution)/shard_map/ppermute | solution.py:292
  18.7 2.7 %convolution_add_fusion.recv_proj_hbm = f32[512,512]{1,0:T(8,128)} fusion(bf16[512,512]{1,0:T(8,128)(2,1)} %w_recv_ref.1, f32[512]{0:T(512)} %param.17, bf16[1,512,512]{2,1,0:T(8,128)(2,1)} %param.10), kind=kOutput, calls=%fused_computation.4 | convolution fusion | flops 268697600 | bytes 2099200 | tf_op jit(solution)/shard_map/dot_general | solution.py:327
  21.4 1.4 %fusion.2.agg_grad_hbm = f32[512,512]{1,0:T(8,128)} fusion(bf16[512,512]{1,0:T(8,128)(2,1)S(1)} %copy-done, bf16[1,512,512]{2,1,0:T(8,128)(2,1)S(1)} %copy-done.1), kind=kOutput, calls=%fused_computation.14 | convolution fusion | flops 268435456 | bytes 2097152 | tf_op jit(solution)/shard_map/dot_general | solution.py:330
  23.2 0.5 collective-permute-done.3.h3_ref
  23.8 1.2 copy-done.4
  25.0 1.2 copy-done.5
  26.2 4.4 %edge_step.1 = (bf16[800,512]{1,0:T(8,128)(2,1)S(1)}, bf16[192,512]{1,0:T(8,128)(2,1)S(1)}, bf16[192,512]{1,0:T(8,128)(2,1)S(1)}, bf16[512,512]{1,0:T(8,128)(2,1...) custom-call(s32[1]{0:T(128)} %bitcast.core_ref, ...), custom_call_target="tpu_custom_call" | custom-call | flops 3000000000 | bytes 6000000 | tf_op jit(solution)/shard_map/edge_step/pallas_call | solution.py:182
  30.7 8.1 %collective-permute-start.4 = (bf16[800,512]{1,0:T(8,128)(2,1)S(1)}, bf16[800,512]{1,0:T(8,128)(2,1)S(1)}, u32[]{:S(2)}, u32[]{:S(2)}) collective-permute-start(bf16[800,512]{1,0:T(8,128)(2,1)S(1)} %get-tuple-element.42), channel_id=1, source_target_pairs={{0,1},{1,0},{2,3},{3,2},{4,5},{5,4},{6,7},{7,6},{8,9},{9,8},{10,11... | collective-permute-start | bytes 2457608 | tf_op jit(solution)/shard_map/ppermute | solution.py:303
  38.8 0.5 keep_step.1.keep_ref
  39.4 1.3 %collective-permute-done.4.came_ref = bf16[800,512]{1,0:T(8,128)(2,1)S(1)} collective-permute-done((bf16[800,512]{1,0:T(8,128)(2,1)S(1)}, bf16[800,512]{1,0:T(8,128)(2,1)S(1)}, u32[]{:S(2)}, u32[]{:S(2)}) %collective-permute-start.4) | collective-permute-done | bytes 819232 | tf_op jit(solution)/shard_map/ppermute | solution.py:303
  41.0 0.9 copy-done.6
  41.9 3.5 %all-to-all-start = ((bf16[4,208,512]{2,1,0:T(8,128)(2,1)}), bf16[4,208,512]{2,1,0:T(8,128)(2,1)S(1)}, u32[]{:S(2)}, u32[]{:S(2)}) async-start(bf16[4,208,512]{2,1,0:T(8,128)(2,1)} %copy-done.6), calls=%async_computation | async-start | bytes 1703936 | tf_op jit(solution)/shard_map/all_to_all | solution.py:307
  45.4 3.9 %collective-permute-start.5 = (bf16[16,512]{1,0:T(8,128)(2,1)}, bf16[16,512]{1,0:T(8,128)(2,1)S(1)}, u32[]{:S(2)}, u32[]{:S(2)}) collective-permute-start(bf16[16,512]{1,0:T(8,128)(2,1)} %get-tuple-element.48), channel_id=1, source_target_pairs={{0,63},{1,2},{2,1},{3,4},{4,3},{5,6},{6,5},{7,8},{8,7},{9,10},{10,... | collective-permute-start | bytes 49160 | tf_op jit(solution)/shard_map/ppermute | solution.py:297
  49.2 4.9 %collective-permute-start.6 = (bf16[16,512]{1,0:T(8,128)(2,1)S(1)}, bf16[16,512]{1,0:T(8,128)(2,1)S(1)}, u32[]{:S(2)}, u32[]{:S(2)}) collective-permute-start(bf16[16,512]{1,0:T(8,128)(2,1)S(1)} %get-tuple-element.49), channel_id=1, source_target_pairs={{0,56},{1,57},{2,58},{3,59},{4,60},{5,61},{6,62},{7,63},{8,0},{9,1... | collective-permute-start | bytes 49160 | tf_op jit(solution)/shard_map/ppermute | solution.py:292
  54.1 1.3 %grid_step.1 = bf16[512,512]{1,0:T(8,128)(2,1)} custom-call(bf16[512,512]{1,0:T(8,128)(2,1)S(1)} %bitcast.34, bf16[512,512]{1,0:T(8,128)(2,1)S(1)} %get-tuple-element.40.recv_ref, bf16[512,512]{1,0:T(8,128)(2,1)S(1)} %copy-done.3), custom_call_target="tpu_custom_call" | custom-call | flops 300000000 | bytes 2000000 | tf_op jit(solution)/shard_map/grid_step/pallas_call | solution.py:263
  55.4 2.7 %all-to-all-done.packed_hbm = bf16[4,208,512]{2,1,0:T(8,128)(2,1)S(1)} async-done(((bf16[4,208,512]{2,1,0:T(8,128)(2,1)}), bf16[4,208,512]{2,1,0:T(8,128)(2,1)S(1)}, u32[]{:S(2)}, u32[]{:S(2)}) %all-to-all-start) | async-done | bytes 852000 | tf_op jit(solution)/shard_map/all_to_all | solution.py:307
  58.1 1.3 %line_step.1 = bf16[64,16,128]{2,1,0:T(8,128)(2,1)S(1)} custom-call(bf16[4,208,512]{2,1,0:T(8,128)(2,1)S(1)} %all-to-all-done.packed_hbm), custom_call_target="tpu_custom_call" | custom-call | flops 500000 | bytes 1000000 | tf_op jit(solution)/shard_map/line_step/pallas_call | solution.py:245
  59.4 23.8 %all_to_all.20 = bf16[64,16,128]{2,1,0:T(8,128)(2,1)S(1)} all-to-all(bf16[64,16,128]{2,1,0:T(8,128)(2,1)S(1)} %line_step.1), channel_id=1, replica_groups=mesh['dp'=8,'y'=8,'x'=4,'core'=2] {'dp','y'}, dimensions={0} | all-to-all | bytes 524288 | tf_op jit(solution)/shard_map/all_to_all | solution.py:307
  83.4 0.7 broadcast_in_dim.8
  84.1 5.6 %all-to-all-start.2 = ((bf16[64,16,128]{2,1,0:T(8,128)(2,1)}), bf16[64,16,128]{2,1,0:T(8,128)(2,1)S(1)}, u32[]{:S(2)}, u32[]{:S(2)}) async-start(bf16[64,16,128]{2,1,0:T(8,128)(2,1)} %broadcast_in_dim.8), calls=%async_computation.2 | async-start | bytes 524288 | tf_op jit(solution)/shard_map/all_to_all | solution.py:307
  89.8 6.8 %collective-permute-start.7 = (bf16[16,512]{1,0:T(8,128)(2,1)S(1)}, bf16[16,512]{1,0:T(8,128)(2,1)S(1)}, u32[]{:S(2)}, u32[]{:S(2)}) collective-permute-start(bf16[16,512]{1,0:T(8,128)(2,1)S(1)} %get-tuple-element.55), channel_id=1, source_target_pairs={{0,32},{1,33},{2,34},{3,35},{4,36},{5,37},{6,38},{7,39},{8,40},{9,... | collective-permute-start | bytes 49160 | tf_op jit(solution)/shard_map/ppermute | solution.py:292
  96.6 0.6 slice_bitcast_fusion
  97.2 5.1 %all-to-all-done.2 = bf16[64,16,128]{2,1,0:T(8,128)(2,1)S(1)} async-done(((bf16[64,16,128]{2,1,0:T(8,128)(2,1)}), bf16[64,16,128]{2,1,0:T(8,128)(2,1)S(1)}, u32[]{:S(2)}, u32[]{:S(2)}) %all-to-all-start.2) | async-done | bytes 262176 | tf_op jit(solution)/shard_map/all_to_all | solution.py:307
  102.5 10.8 %all_to_all.21 = bf16[4,192,512]{2,1,0:T(8,128)(2,1)S(1)} all-to-all(bf16[4,192,512]{2,1,0:T(8,128)(2,1)S(1)} %broadcast_in_dim.22), channel_id=1, replica_groups=mesh['dp'=8,'y'=8,'x'=4,'core'=2] {'x'}, dimensions={0} | all-to-all | bytes 1572864 | tf_op jit(solution)/shard_map/all_to_all | solution.py:307
  113.3 6.9 %collective-permute-start.8 = (bf16[3,1,256,512]{3,2,1,0:T(8,128)(2,1)S(1)}, bf16[3,1,256,512]{3,2,1,0:T(8,128)(2,1)S(1)}, u32[]{:S(2)}, u32[]{:S(2)}) collective-permute-start(bf16[3,1,256,512]{3,2,1,0:T(8,128)(2,1)S(1)} %bitcast.43), channel_id=1, source_target_pairs={{0,1},{1,0},{2,3},{3,2},{4,5},{5,4},{6,7},{7,6},{8,9},{9,8},{10,11... | collective-permute-start | bytes 2359304 | tf_op jit(solution)/shard_map/ppermute | solution.py:303
  120.2 1.2 mesh_step.1
  121.4 0.7 collective-permute-done.8
  122.2 1.2 pad_maximum_fusion
  (42 shorter events, 1.0 us)
Async XLA Ops:
  0.6 20.7 %copy-start = (bf16[512,512]{1,0:T(8,128)(2,1)S(1)}, bf16[512,512]{1,0:T(8,128)(2,1)}, u32[]{:S(2)}) copy-start(bf16[512,512]{1,0:T(8,128)(2,1)} %param.16) | copy-start | bytes 1572868
  0.6 20.7 %copy-start.1 = (bf16[1,512,512]{2,1,0:T(8,128)(2,1)S(1)}, bf16[1,512,512]{2,1,0:T(8,128)(2,1)}, u32[]{:S(2)}) copy-start(bf16[1,512,512]{2,1,0:T(8,128)(2,1)} %param.11) | copy-start | bytes 1572868
  2.5 20.7 %collective-permute-start = (bf16[16,512]{1,0:T(8,128)(2,1)}, bf16[16,512]{1,0:T(8,128)(2,1)S(1)}, u32[]{:S(2)}, u32[]{:S(2)}) collective-permute-start(bf16[16,512]{1,0:T(8,128)(2,1)} %get-tuple-element.33), channel_id=1, source_target_pairs={{0,1},{1,2},{2,3},{3,4},{4,5},{5,6},{6,7},{7,8},{8,9},{9,10},{10,1... | collective-permute-start | bytes 49160 | tf_op jit(solution)/shard_map/ppermute | solution.py:292
  7.0 16.2 %collective-permute-start.1 = (bf16[16,512]{1,0:T(8,128)(2,1)}, bf16[16,512]{1,0:T(8,128)(2,1)S(1)}, u32[]{:S(2)}, u32[]{:S(2)}) collective-permute-start(bf16[16,512]{1,0:T(8,128)(2,1)} %get-tuple-element.34), channel_id=1, source_target_pairs={{0,63},{1,0},{2,1},{3,2},{4,3},{5,4},{6,5},{7,6},{8,7},{9,8},{10,9... | collective-permute-start | bytes 49160 | tf_op jit(solution)/shard_map/ppermute | solution.py:292
  13.2 10.0 %collective-permute-start.2 = (bf16[16,512]{1,0:T(8,128)(2,1)}, bf16[16,512]{1,0:T(8,128)(2,1)S(1)}, u32[]{:S(2)}, u32[]{:S(2)}) collective-permute-start(bf16[16,512]{1,0:T(8,128)(2,1)} %get-tuple-element.35), channel_id=1, source_target_pairs={{0,8},{1,9},{2,10},{3,11},{4,12},{5,13},{6,14},{7,15},{8,16},{9,17... | collective-permute-start | bytes 49160 | tf_op jit(solution)/shard_map/ppermute | solution.py:292
  15.2 8.6 %collective-permute-start.3 = (bf16[16,512]{1,0:T(8,128)(2,1)}, bf16[16,512]{1,0:T(8,128)(2,1)S(1)}, u32[]{:S(2)}, u32[]{:S(2)}) collective-permute-start(bf16[16,512]{1,0:T(8,128)(2,1)} %get-tuple-element.36), channel_id=1, source_target_pairs={{0,32},{1,33},{2,34},{3,35},{4,36},{5,37},{6,38},{7,39},{8,40},{9,... | collective-permute-start | bytes 49160 | tf_op jit(solution)/shard_map/ppermute | solution.py:292
  21.4 1.5 %copy-start.12 = (s32[1536]{0:T(1024)S(1)}, s32[1536]{0:T(1024)}, u32[]{:S(2)}) copy-start(s32[1536]{0:T(1024)} %param.12) | copy-start | bytes 18436
  21.4 2.4 %copy-start.2 = (bf16[1,512,512]{2,1,0:T(8,128)(2,1)S(1)}, bf16[1,512,512]{2,1,0:T(8,128)(2,1)}, u32[]{:S(2)}) copy-start(bf16[1,512,512]{2,1,0:T(8,128)(2,1)} %param.10) | copy-start | bytes 1572868
  21.4 2.4 %copy-start.7 = (bf16[512,512]{1,0:T(8,128)(2,1)S(1)}, bf16[512,512]{1,0:T(8,128)(2,1)}, u32[]{:S(2)}) copy-start(bf16[512,512]{1,0:T(8,128)(2,1)} %w_send_ref.1) | copy-start | bytes 1572868
  21.4 2.4 %copy-start.10 = (bf16[1,128,512]{2,1,0:T(8,128)(2,1)S(1)}, bf16[1,128,512]{2,1,0:T(8,128)(2,1)}, u32[]{:S(2)}) copy-start(bf16[1,128,512]{2,1,0:T(8,128)(2,1)} %param.9) | copy-start | bytes 393220
  23.8 1.2 copy-start.4
  25.0 1.2 copy-start.5
  30.7 8.7 %copy-start.8 = (f32[128,512]{1,0:T(8,128)}, f32[128,512]{1,0:T(8,128)S(1)}, u32[]{:S(2)}) copy-start(f32[128,512]{1,0:T(8,128)S(1)} %get-tuple-element.37.local_ref) | copy-start | bytes 786436
  30.7 10.1 %collective-permute-start.4 = (bf16[800,512]{1,0:T(8,128)(2,1)S(1)}, bf16[800,512]{1,0:T(8,128)(2,1)S(1)}, u32[]{:S(2)}, u32[]{:S(2)}) collective-permute-start(bf16[800,512]{1,0:T(8,128)(2,1)S(1)} %get-tuple-element.42), channel_id=1, source_target_pairs={{0,1},{1,0},{2,3},{3,2},{4,5},{5,4},{6,7},{7,6},{8,9},{9,8},{10,11... | collective-permute-start | bytes 2457608 | tf_op jit(solution)/shard_map/ppermute | solution.py:303
  39.4 14.7 %copy-start.3 = (bf16[512,512]{1,0:T(8,128)(2,1)S(1)}, bf16[512,512]{1,0:T(8,128)(2,1)}, u32[]{:S(2)}) copy-start(bf16[512,512]{1,0:T(8,128)(2,1)} %w_recv_ref.1) | copy-start | bytes 1572868
  40.9 0.9 copy-start.6
  41.9 16.2 %all-to-all-start = ((bf16[4,208,512]{2,1,0:T(8,128)(2,1)}), bf16[4,208,512]{2,1,0:T(8,128)(2,1)S(1)}, u32[]{:S(2)}, u32[]{:S(2)}) async-start(bf16[4,208,512]{2,1,0:T(8,128)(2,1)} %copy-done.6), calls=%async_computation | async-start | bytes 1703936 | tf_op jit(solution)/shard_map/all_to_all | solution.py:307
  45.4 14.0 %collective-permute-start.5 = (bf16[16,512]{1,0:T(8,128)(2,1)}, bf16[16,512]{1,0:T(8,128)(2,1)S(1)}, u32[]{:S(2)}, u32[]{:S(2)}) collective-permute-start(bf16[16,512]{1,0:T(8,128)(2,1)} %get-tuple-element.48), channel_id=1, source_target_pairs={{0,63},{1,2},{2,1},{3,4},{4,3},{5,6},{6,5},{7,8},{8,7},{9,10},{10,... | collective-permute-start | bytes 49160 | tf_op jit(solution)/shard_map/ppermute | solution.py:297
  49.2 10.2 %collective-permute-start.6 = (bf16[16,512]{1,0:T(8,128)(2,1)S(1)}, bf16[16,512]{1,0:T(8,128)(2,1)S(1)}, u32[]{:S(2)}, u32[]{:S(2)}) collective-permute-start(bf16[16,512]{1,0:T(8,128)(2,1)S(1)} %get-tuple-element.49), channel_id=1, source_target_pairs={{0,56},{1,57},{2,58},{3,59},{4,60},{5,61},{6,62},{7,63},{8,0},{9,1... | collective-permute-start | bytes 49160 | tf_op jit(solution)/shard_map/ppermute | solution.py:292
  84.1 18.1 %all-to-all-start.2 = ((bf16[64,16,128]{2,1,0:T(8,128)(2,1)}), bf16[64,16,128]{2,1,0:T(8,128)(2,1)S(1)}, u32[]{:S(2)}, u32[]{:S(2)}) async-start(bf16[64,16,128]{2,1,0:T(8,128)(2,1)} %broadcast_in_dim.8), calls=%async_computation.2 | async-start | bytes 524288 | tf_op jit(solution)/shard_map/all_to_all | solution.py:307
  89.8 12.7 %collective-permute-start.7 = (bf16[16,512]{1,0:T(8,128)(2,1)S(1)}, bf16[16,512]{1,0:T(8,128)(2,1)S(1)}, u32[]{:S(2)}, u32[]{:S(2)}) collective-permute-start(bf16[16,512]{1,0:T(8,128)(2,1)S(1)} %get-tuple-element.55), channel_id=1, source_target_pairs={{0,32},{1,33},{2,34},{3,35},{4,36},{5,37},{6,38},{7,39},{8,40},{9,... | collective-permute-start | bytes 49160 | tf_op jit(solution)/shard_map/ppermute | solution.py:292
  102.4 17.8 %copy-start.9 = (f32[128,512]{1,0:T(8,128)S(1)}, f32[128,512]{1,0:T(8,128)}, u32[]{:S(2)}) copy-start(f32[128,512]{1,0:T(8,128)} %copy-done.8) | copy-start | bytes 786436
  102.4 17.8 %copy-start.11 = (s32[1,4,16]{2,1,0:T(4,128)S(1)}, s32[1,4,16]{2,1,0:T(4,128)}, u32[]{:S(2)}) copy-start(s32[1,4,16]{2,1,0:T(4,128)} %param.13) | copy-start | bytes 772
  113.3 8.8 %collective-permute-start.8 = (bf16[3,1,256,512]{3,2,1,0:T(8,128)(2,1)S(1)}, bf16[3,1,256,512]{3,2,1,0:T(8,128)(2,1)S(1)}, u32[]{:S(2)}, u32[]{:S(2)}) collective-permute-start(bf16[3,1,256,512]{3,2,1,0:T(8,128)(2,1)S(1)} %bitcast.43), channel_id=1, source_target_pairs={{0,1},{1,0},{2,3},{3,2},{4,5},{5,4},{6,7},{7,6},{8,9},{9,8},{10,11... | collective-permute-start | bytes 2359304 | tf_op jit(solution)/shard_map/ppermute | solution.py:303

commit v6 on v4

--- a/solution.py
+++ b/solution.py
@@ -21,7 +21,7 @@
         out_ref[index * 256 : (index + 1) * 256, :] = product.astype(out_ref.dtype)
 
 
-def pick_kernel(rows_hbm, mesh_hbm, o0_ref, o1_ref, o2_ref, o3_ref, rows_ref, mesh_ref, arrived):
+def pick_kernel(core_ref, rows_hbm, mesh_hbm, o0_ref, o1_ref, o2_ref, o3_ref, rows_ref, mesh_ref, arrived):
     mesh_copy = pltpu.make_async_copy(mesh_hbm, mesh_ref, arrived.at[0])
     rows_copy = pltpu.make_async_copy(rows_hbm, rows_ref, arrived.at[1])
     mesh_copy.start()
@@ -29,8 +29,9 @@
     rows_copy.wait()
     mesh_copy.wait()
     sublane = lax.broadcasted_iota(jnp.int32, (128, 16), 0)
-    for j, out_ref in enumerate((o0_ref, o1_ref, o2_ref, o3_ref)):
-        pick = (sublane == rows_ref[j : j + 1, :]).astype(F32).astype(BF)
+    blocks = (core_ref[0], 1 - core_ref[0], 2, 3)
+    for j, out_ref in zip(blocks, (o0_ref, o1_ref, o2_ref, o3_ref)):
+        pick = (sublane == rows_ref[pl.ds(j, 1), :]).astype(F32).astype(BF)
         out_ref[...] = rows_dot(pick, mesh_ref[...]).astype(BF)
 
 
@@ -38,10 +39,10 @@
     core_ref, column_ref, row_ref, mesh_ref, grid_ref, upstream_ref,
     h0_ref, h1_ref, h2_ref, h3_ref, w_hbm, recv_proj_hbm, agg_grad_hbm,
     send_ref, known_ref, slot_ref, recv_ref, node_ref, local_ref, next_ref, far_ref, last_ref,
-    table_ref, preact_ref, edge_ref, bias_ref, w_send_ref, recv_proj_ref, agg_grad_ref, arrived,
+    table_ref, preact_ref, edge_ref, bias_ref, w_send_ref, recv_proj_ref, agg_grad_ref, halo_rows_ref, arrived,
 ):
     copies = [
-        pltpu.make_async_copy(halo_ref, known_ref.at[pl.ds(128 + 16 * j, 16)], arrived.at[j])
+        pltpu.make_async_copy(halo_ref, halo_rows_ref.at[pl.ds(16 * j, 16)], arrived.at[j])
         for j, halo_ref in enumerate((h0_ref, h1_ref, h2_ref, h3_ref))
     ]
     copies.append(pltpu.make_async_copy(w_hbm, w_send_ref, arrived.at[4]))
@@ -52,6 +53,11 @@
     known_ref[0:128, :] = mesh_ref[...]
     for copy in copies[:5]:
         copy.wait()
+    partner = pl.ds(pl.multiple_of(144 - 16 * core_ref[0], 16), 16)
+    next_chip = pl.ds(pl.multiple_of(128 + 16 * core_ref[0], 16), 16)
+    known_ref[partner, :] = halo_rows_ref[0:16, :]
+    known_ref[next_chip, :] = halo_rows_ref[16:32, :]
+    known_ref[160:192, :] = halo_rows_ref[32:64, :]
     sent = jnp.dot(known_ref[...], w_send_ref[...], preferred_element_type=F32)
     high = sent.astype(BF)
     table_ref[0:192, :] = high
@@ -191,6 +197,7 @@
             pltpu.VMEM((512, 512), BF),
             pltpu.VMEM((512, 512), F32),
             pltpu.VMEM((512, 512), F32),
+            pltpu.VMEM((64, 512), BF),
             pltpu.SemaphoreType.DMA((7,)),
         ],
         compiler_params=limit(24),
@@ -227,7 +234,7 @@
     return pl.pallas_call(
         pick_kernel,
         out_shape=(shape(16, BF),) * 4,
-        in_specs=[HBM] * 2,
+        in_specs=[SM] + [HBM] * 2,
         out_specs=(VM,) * 4,
         scratch_shapes=[
             pltpu.VMEM((4, 16), jnp.int32),
@@ -308,8 +315,9 @@
     core_ref = core.astype(jnp.int32).reshape(1)
     pieces = lax.axis_size(SPACE)
     offsets = (1, -1, max(2, pieces // 8), pieces // 2)
-    outgoing = pick_step(send_rows[0], mesh_rows)
-    halo = [shift_space(outgoing[j], offsets[j]) for j in range(4)]
+    outgoing = pick_step(core_ref, send_rows[0], mesh_rows)
+    halo = [swap_cores(outgoing[0]), swap_chips(outgoing[1])]
+    halo += [shift_space(outgoing[j], offsets[j]) for j in (2, 3)]
     recv_proj = lax.dot_general(
         grid_rows, w_recv, (((1,), (0,)), ((), ())), preferred_element_type=F32
     ) + edge_bias

time: 124 us -> 123 us (level)
  starting transfers between devices: 56 us -> 51.4 us
  blocking collectives: 34.7 us -> 37 us
    ppermute x6 -> x4, starting transfers between devices: 27.9 us -> 16.1 us  [shift_space(): lax.ppermute(value, SPACE, [(i, (i + offset) % pieces) for i in range(pie...]
    ppermute x2 -> x3, starting transfers between devices: 15 us -> 20.2 us  [swap_cores(): return lax.ppermute(value, 'core', [(0, 1), (1, 0)])]
    all_to_all x2, blocking collectives: 34.7 us -> 37 us  [exchange(): return lax.all_to_all(value, axes, split_axis=0, concat_axis=0, tiled=True)]
    ppermute x1 -> x2, starting transfers between devices: 3.97 us -> 5.89 us  [swap_chips(): lax.ppermute(value, SPACE, [(i, (i - 1 + 2 * (i % 2)) % pieces) for i in...]
    ppermute x2 -> x3, waiting for transfers between devices: 3.24 us -> 3.25 us  [swap_cores(): return lax.ppermute(value, 'core', [(0, 1), (1, 0)])]
where the time goes in v6:
time: 123 us; the launch traced here: 122 us
  starting transfers between devices  51.4 us (42%)
  blocking collectives  37 us (30%)
  waiting for transfers between devices  12.2 us (10%)
  Pallas kernels  9.69 us (8%)
  local copies, waits for them, and re-layouts  5.28 us (4%)
  matrix products  4.07 us (3%)
  other arithmetic  1.37 us (1%)
    all_to_all x2, blocking collectives, exchange(): return lax.all_to_all(value, axes, split_axis=0, concat_axis=0, tiled=True)  37 us
    ppermute x3, starting transfers between devices, swap_cores(): return lax.ppermute(value, 'core', [(0, 1), (1, 0)])  20.2 us
    ppermute x4, starting transfers between devices, shift_space(): lax.ppermute(value, SPACE, [(i, (i + offset) % pieces) for i in range(pie...  16.1 us
    all_to_all x2, starting transfers between devices, exchange(): return lax.all_to_all(value, axes, split_axis=0, concat_axis=0, tiled=True)  9.15 us
    all_to_all x2, waiting for transfers between devices, exchange(): return lax.all_to_all(value, axes, split_axis=0, concat_axis=0, tiled=True)  6.67 us
    ppermute x2, starting transfers between devices, swap_chips(): lax.ppermute(value, SPACE, [(i, (i - 1 + 2 * (i % 2)) % pieces) for i in...  5.89 us
    pallas_call x1, Pallas kernels, edge_step(): pl.pallas_call(edge_kernel, out_shape=(shape(800, BF), shape(192, BF), sh...  4.32 us
    unnamed x31, local copies, waits for them, and re-layouts  3.52 us
  transfers between devices with their start and end apart: 11, of which 6 were waited for; matrix products, arithmetic and copies ran while one was open for 4% of the time, Pallas kernels for 3%

profile of v6, /device:TPU:1, one launch (start us, length us, event | category | flops | bytes accessed | tf_op | source)
XLA Modules:
  0.0 122.0 jit_solution(7479989730181213557)
XLA Ops:
  0.7 1.8 %pick_step.1 = (bf16[16,512]{1,0:T(8,128)(2,1)}, bf16[16,512]{1,0:T(8,128)(2,1)}, bf16[16,512]{1,0:T(8,128)(2,1)}, bf16[16,512]{1,0:T(8,128)(2,1)}) custom-call(s32[1]{0:T(128)} %bitcast.core_ref, s32[4,16]{1,0:T(4,128)} %bitcast.40, bf16[128,512]{1,0:T(8,128)(2,1)} %bitcast.38), custom_call_target="tpu_custom_call" | custom-call | flops 10000000 | bytes 200000 | tf_op jit(solution)/shard_map/pick_step/pallas_call | solution.py:234
  2.5 8.8 %collective-permute-start = (bf16[16,512]{1,0:T(8,128)(2,1)}, bf16[16,512]{1,0:T(8,128)(2,1)S(1)}, u32[]{:S(2)}, u32[]{:S(2)}) collective-permute-start(bf16[16,512]{1,0:T(8,128)(2,1)} %get-tuple-element.35), channel_id=1, source_target_pairs={{0,1},{1,0},{2,3},{3,2},{4,5},{5,4},{6,7},{7,6},{8,9},{9,8},{10,11... | collective-permute-start | bytes 49160 | tf_op jit(solution)/shard_map/ppermute | solution.py:296
  11.3 1.9 %collective-permute-start.1 = (bf16[16,512]{1,0:T(8,128)(2,1)}, bf16[16,512]{1,0:T(8,128)(2,1)S(1)}, u32[]{:S(2)}, u32[]{:S(2)}) collective-permute-start(bf16[16,512]{1,0:T(8,128)(2,1)} %get-tuple-element.36), channel_id=1, source_target_pairs={{0,63},{1,2},{2,1},{3,4},{4,3},{5,6},{6,5},{7,8},{8,7},{9,10},{10,... | collective-permute-start | bytes 49160 | tf_op jit(solution)/shard_map/ppermute | solution.py:290
  13.2 1.9 %collective-permute-start.2 = (bf16[16,512]{1,0:T(8,128)(2,1)}, bf16[16,512]{1,0:T(8,128)(2,1)S(1)}, u32[]{:S(2)}, u32[]{:S(2)}) collective-permute-start(bf16[16,512]{1,0:T(8,128)(2,1)} %get-tuple-element.37), channel_id=1, source_target_pairs={{0,8},{1,9},{2,10},{3,11},{4,12},{5,13},{6,14},{7,15},{8,16},{9,17... | collective-permute-start | bytes 49160 | tf_op jit(solution)/shard_map/ppermute | solution.py:285
  15.2 3.6 %collective-permute-start.3 = (bf16[16,512]{1,0:T(8,128)(2,1)}, bf16[16,512]{1,0:T(8,128)(2,1)S(1)}, u32[]{:S(2)}, u32[]{:S(2)}) collective-permute-start(bf16[16,512]{1,0:T(8,128)(2,1)} %get-tuple-element.38), channel_id=1, source_target_pairs={{0,32},{1,33},{2,34},{3,35},{4,36},{5,37},{6,38},{7,39},{8,40},{9,... | collective-permute-start | bytes 49160 | tf_op jit(solution)/shard_map/ppermute | solution.py:285
  18.7 2.6 %convolution_add_fusion.recv_proj_hbm = f32[512,512]{1,0:T(8,128)} fusion(bf16[512,512]{1,0:T(8,128)(2,1)} %w_recv_ref.1, f32[512]{0:T(512)} %param.17, bf16[1,512,512]{2,1,0:T(8,128)(2,1)} %param.10), kind=kOutput, calls=%fused_computation.4 | convolution fusion | flops 268697600 | bytes 2099200 | tf_op jit(solution)/shard_map/dot_general | solution.py:321
  21.4 1.4 %fusion.2.agg_grad_hbm = f32[512,512]{1,0:T(8,128)} fusion(bf16[512,512]{1,0:T(8,128)(2,1)S(1)} %copy-done, bf16[1,512,512]{2,1,0:T(8,128)(2,1)S(1)} %copy-done.1), kind=kOutput, calls=%fused_computation.14 | convolution fusion | flops 268435456 | bytes 2097152 | tf_op jit(solution)/shard_map/dot_general | solution.py:324
  23.2 0.5 collective-permute-done.3.h3_ref
  23.8 1.2 copy-done.4
  25.0 1.2 %copy-done.5 = f32[512,512]{1,0:T(8,128)S(1)} copy-done((f32[512,512]{1,0:T(8,128)S(1)}, f32[512,512]{1,0:T(8,128)}, u32[]{:S(2)}) %copy-start.5) | copy-done | bytes 1048600
  26.2 4.3 %edge_step.1 = (bf16[800,512]{1,0:T(8,128)(2,1)S(1)}, bf16[192,512]{1,0:T(8,128)(2,1)S(1)}, bf16[192,512]{1,0:T(8,128)(2,1)S(1)}, bf16[512,512]{1,0:T(8,128)(2,1...) custom-call(s32[1]{0:T(128)} %bitcast.core_ref, ...), custom_call_target="tpu_custom_call" | custom-call | flops 3000000000 | bytes 6000000 | tf_op jit(solution)/shard_map/edge_step/pallas_call | solution.py:186
  30.6 4.5 %collective-permute-start.4 = (bf16[800,512]{1,0:T(8,128)(2,1)S(1)}, bf16[800,512]{1,0:T(8,128)(2,1)S(1)}, u32[]{:S(2)}, u32[]{:S(2)}) collective-permute-start(bf16[800,512]{1,0:T(8,128)(2,1)S(1)} %get-tuple-element.43), channel_id=1, source_target_pairs={{0,1},{1,0},{2,3},{3,2},{4,5},{5,4},{6,7},{7,6},{8,9},{9,8},{10,11... | collective-permute-start | bytes 2457608 | tf_op jit(solution)/shard_map/ppermute | solution.py:296
  35.1 0.5 keep_step.1.keep_ref
  35.7 1.4 %collective-permute-done.4.came_ref = bf16[800,512]{1,0:T(8,128)(2,1)S(1)} collective-permute-done((bf16[800,512]{1,0:T(8,128)(2,1)S(1)}, bf16[800,512]{1,0:T(8,128)(2,1)S(1)}, u32[]{:S(2)}, u32[]{:S(2)}) %collective-permute-start.4) | collective-permute-done | bytes 819232 | tf_op jit(solution)/shard_map/ppermute | solution.py:296
  37.2 0.9 copy-done.6
  38.1 3.5 %all-to-all-start = ((bf16[4,208,512]{2,1,0:T(8,128)(2,1)}), bf16[4,208,512]{2,1,0:T(8,128)(2,1)S(1)}, u32[]{:S(2)}, u32[]{:S(2)}) async-start(bf16[4,208,512]{2,1,0:T(8,128)(2,1)} %copy-done.6), calls=%async_computation | async-start | bytes 1703936 | tf_op jit(solution)/shard_map/all_to_all | solution.py:300
  41.6 4.0 %collective-permute-start.5 = (bf16[16,512]{1,0:T(8,128)(2,1)}, bf16[16,512]{1,0:T(8,128)(2,1)S(1)}, u32[]{:S(2)}, u32[]{:S(2)}) collective-permute-start(bf16[16,512]{1,0:T(8,128)(2,1)} %get-tuple-element.48), channel_id=1, source_target_pairs={{0,63},{1,2},{2,1},{3,4},{4,3},{5,6},{6,5},{7,8},{8,7},{9,10},{10,... | collective-permute-start | bytes 49160 | tf_op jit(solution)/shard_map/ppermute | solution.py:290
  45.6 3.8 %collective-permute-start.6 = (bf16[16,512]{1,0:T(8,128)(2,1)}, bf16[16,512]{1,0:T(8,128)(2,1)S(1)}, u32[]{:S(2)}, u32[]{:S(2)}) collective-permute-start(bf16[16,512]{1,0:T(8,128)(2,1)} %copy-done.12), channel_id=1, source_target_pairs={{0,56},{1,57},{2,58},{3,59},{4,60},{5,61},{6,62},{7,63},{8,0},{9,1... | collective-permute-start | bytes 49160 | tf_op jit(solution)/shard_map/ppermute | solution.py:285
  49.4 4.9 %all-to-all-done.packed_hbm = bf16[4,208,512]{2,1,0:T(8,128)(2,1)S(1)} async-done(((bf16[4,208,512]{2,1,0:T(8,128)(2,1)}), bf16[4,208,512]{2,1,0:T(8,128)(2,1)S(1)}, u32[]{:S(2)}, u32[]{:S(2)}) %all-to-all-start) | async-done | bytes 852000 | tf_op jit(solution)/shard_map/all_to_all | solution.py:300
  54.3 1.3 %line_step.1 = bf16[64,16,128]{2,1,0:T(8,128)(2,1)S(1)} custom-call(bf16[4,208,512]{2,1,0:T(8,128)(2,1)S(1)} %all-to-all-done.packed_hbm), custom_call_target="tpu_custom_call" | custom-call | flops 500000 | bytes 1000000 | tf_op jit(solution)/shard_map/line_step/pallas_call | solution.py:250
  55.7 26.3 %all_to_all.20 = bf16[64,16,128]{2,1,0:T(8,128)(2,1)S(1)} all-to-all(bf16[64,16,128]{2,1,0:T(8,128)(2,1)S(1)} %line_step.1), channel_id=1, replica_groups=mesh['dp'=8,'y'=8,'x'=4,'core'=2] {'dp','y'}, dimensions={0} | all-to-all | bytes 524288 | tf_op jit(solution)/shard_map/all_to_all | solution.py:300
  82.0 0.7 broadcast_in_dim.8
  82.8 5.6 %all-to-all-start.2 = ((bf16[64,16,128]{2,1,0:T(8,128)(2,1)}), bf16[64,16,128]{2,1,0:T(8,128)(2,1)S(1)}, u32[]{:S(2)}, u32[]{:S(2)}) async-start(bf16[64,16,128]{2,1,0:T(8,128)(2,1)} %broadcast_in_dim.8), calls=%async_computation.2 | async-start | bytes 524288 | tf_op jit(solution)/shard_map/all_to_all | solution.py:300
  88.4 6.8 %collective-permute-start.7 = (bf16[16,512]{1,0:T(8,128)(2,1)S(1)}, bf16[16,512]{1,0:T(8,128)(2,1)S(1)}, u32[]{:S(2)}, u32[]{:S(2)}) collective-permute-start(bf16[16,512]{1,0:T(8,128)(2,1)S(1)} %get-tuple-element.57), channel_id=1, source_target_pairs={{0,32},{1,33},{2,34},{3,35},{4,36},{5,37},{6,38},{7,39},{8,40},{9,... | collective-permute-start | bytes 49160 | tf_op jit(solution)/shard_map/ppermute | solution.py:285
  95.3 0.6 slice_bitcast_fusion
  95.8 1.8 %collective-permute-done.7.last_ref = bf16[16,512]{1,0:T(8,128)(2,1)S(1)} collective-permute-done((bf16[16,512]{1,0:T(8,128)(2,1)S(1)}, bf16[16,512]{1,0:T(8,128)(2,1)S(1)}, u32[]{:S(2)}, u32[]{:S(2)}) %collective-permute-start.7) | collective-permute-done | bytes 16416 | tf_op jit(solution)/shard_map/ppermute | solution.py:285
  97.6 1.5 %tail_step.1 = (f32[128,512]{1,0:T(8,128)}, bf16[512,512]{1,0:T(8,128)(2,1)}) custom-call(s32[1]{0:T(128)} %bitcast.core_ref, s32[4,16]{1,0:T(4,128)S(1)} %bitcast.41, f32[128,512]{1,0:T(8,128)S(1)} %copy-done.9, bf16[16,512]{1,0:T(8,128)(2,1)S(1)} %get-tuple-element.54.near_ref, bf16[16,512]{1,0:T(8,128)(2,1)S(1)} %collective-permute-done.5.next_ref, ...), custom_call_target="tpu_custom_call" | custom-call | flops 400000000 | bytes 3000000 | tf_op jit(solution)/shard_map/tail_step/pallas_call | solution.py:268
  99.1 1.8 %all-to-all-done.2 = bf16[64,16,128]{2,1,0:T(8,128)(2,1)S(1)} async-done(((bf16[64,16,128]{2,1,0:T(8,128)(2,1)}), bf16[64,16,128]{2,1,0:T(8,128)(2,1)S(1)}, u32[]{:S(2)}, u32[]{:S(2)}) %all-to-all-start.2) | async-done | bytes 262176 | tf_op jit(solution)/shard_map/all_to_all | solution.py:300
  101.1 10.8 %all_to_all.21 = bf16[4,192,512]{2,1,0:T(8,128)(2,1)S(1)} all-to-all(bf16[4,192,512]{2,1,0:T(8,128)(2,1)S(1)} %broadcast_in_dim.22), channel_id=1, replica_groups=mesh['dp'=8,'y'=8,'x'=4,'core'=2] {'x'}, dimensions={0} | all-to-all | bytes 1572864 | tf_op jit(solution)/shard_map/all_to_all | solution.py:300
  111.9 6.9 %collective-permute-start.8 = (bf16[3,1,256,512]{3,2,1,0:T(8,128)(2,1)S(1)}, bf16[3,1,256,512]{3,2,1,0:T(8,128)(2,1)S(1)}, u32[]{:S(2)}, u32[]{:S(2)}) collective-permute-start(bf16[3,1,256,512]{3,2,1,0:T(8,128)(2,1)S(1)} %bitcast.43), channel_id=1, source_target_pairs={{0,1},{1,0},{2,3},{3,2},{4,5},{5,4},{6,7},{7,6},{8,9},{9,8},{10,11... | collective-permute-start | bytes 2359304 | tf_op jit(solution)/shard_map/ppermute | solution.py:296
  118.9 1.9 %collective-permute-done.8 = bf16[3,1,256,512]{3,2,1,0:T(8,128)(2,1)S(1)} collective-permute-done((bf16[3,1,256,512]{3,2,1,0:T(8,128)(2,1)S(1)}, bf16[3,1,256,512]{3,2,1,0:T(8,128)(2,1)S(1)}, u32[]{:S(2)}, u32[]{:S(2)}) %collective-permute-start.8) | collective-permute-done | bytes 786464 | tf_op jit(solution)/shard_map/ppermute | solution.py:296
  120.8 1.2 pad_maximum_fusion
  (43 shorter events, 0.9 us)
Async XLA Ops:
  0.6 20.7 %copy-start = (bf16[512,512]{1,0:T(8,128)(2,1)S(1)}, bf16[512,512]{1,0:T(8,128)(2,1)}, u32[]{:S(2)}) copy-start(bf16[512,512]{1,0:T(8,128)(2,1)} %param.16) | copy-start | bytes 1572868
  0.6 20.7 %copy-start.1 = (bf16[1,512,512]{2,1,0:T(8,128)(2,1)S(1)}, bf16[1,512,512]{2,1,0:T(8,128)(2,1)}, u32[]{:S(2)}) copy-start(bf16[1,512,512]{2,1,0:T(8,128)(2,1)} %param.11) | copy-start | bytes 1572868
  2.5 20.7 %collective-permute-start = (bf16[16,512]{1,0:T(8,128)(2,1)}, bf16[16,512]{1,0:T(8,128)(2,1)S(1)}, u32[]{:S(2)}, u32[]{:S(2)}) collective-permute-start(bf16[16,512]{1,0:T(8,128)(2,1)} %get-tuple-element.35), channel_id=1, source_target_pairs={{0,1},{1,0},{2,3},{3,2},{4,5},{5,4},{6,7},{7,6},{8,9},{9,8},{10,11... | collective-permute-start | bytes 49160 | tf_op jit(solution)/shard_map/ppermute | solution.py:296
  11.3 11.9 %collective-permute-start.1 = (bf16[16,512]{1,0:T(8,128)(2,1)}, bf16[16,512]{1,0:T(8,128)(2,1)S(1)}, u32[]{:S(2)}, u32[]{:S(2)}) collective-permute-start(bf16[16,512]{1,0:T(8,128)(2,1)} %get-tuple-element.36), channel_id=1, source_target_pairs={{0,63},{1,2},{2,1},{3,4},{4,3},{5,6},{6,5},{7,8},{8,7},{9,10},{10,... | collective-permute-start | bytes 49160 | tf_op jit(solution)/shard_map/ppermute | solution.py:290
  13.2 10.0 %collective-permute-start.2 = (bf16[16,512]{1,0:T(8,128)(2,1)}, bf16[16,512]{1,0:T(8,128)(2,1)S(1)}, u32[]{:S(2)}, u32[]{:S(2)}) collective-permute-start(bf16[16,512]{1,0:T(8,128)(2,1)} %get-tuple-element.37), channel_id=1, source_target_pairs={{0,8},{1,9},{2,10},{3,11},{4,12},{5,13},{6,14},{7,15},{8,16},{9,17... | collective-permute-start | bytes 49160 | tf_op jit(solution)/shard_map/ppermute | solution.py:285
  15.2 8.6 %collective-permute-start.3 = (bf16[16,512]{1,0:T(8,128)(2,1)}, bf16[16,512]{1,0:T(8,128)(2,1)S(1)}, u32[]{:S(2)}, u32[]{:S(2)}) collective-permute-start(bf16[16,512]{1,0:T(8,128)(2,1)} %get-tuple-element.38), channel_id=1, source_target_pairs={{0,32},{1,33},{2,34},{3,35},{4,36},{5,37},{6,38},{7,39},{8,40},{9,... | collective-permute-start | bytes 49160 | tf_op jit(solution)/shard_map/ppermute | solution.py:285
  21.4 1.5 %copy-start.13 = (s32[1536]{0:T(1024)S(1)}, s32[1536]{0:T(1024)}, u32[]{:S(2)}) copy-start(s32[1536]{0:T(1024)} %param.12) | copy-start | bytes 18436
  21.4 2.4 %copy-start.2 = (bf16[1,512,512]{2,1,0:T(8,128)(2,1)S(1)}, bf16[1,512,512]{2,1,0:T(8,128)(2,1)}, u32[]{:S(2)}) copy-start(bf16[1,512,512]{2,1,0:T(8,128)(2,1)} %param.10) | copy-start | bytes 1572868
  21.4 2.4 %copy-start.7 = (bf16[512,512]{1,0:T(8,128)(2,1)S(1)}, bf16[512,512]{1,0:T(8,128)(2,1)}, u32[]{:S(2)}) copy-start(bf16[512,512]{1,0:T(8,128)(2,1)} %w_send_ref.1) | copy-start | bytes 1572868
  21.4 2.4 %copy-start.10 = (bf16[1,128,512]{2,1,0:T(8,128)(2,1)S(1)}, bf16[1,128,512]{2,1,0:T(8,128)(2,1)}, u32[]{:S(2)}) copy-start(bf16[1,128,512]{2,1,0:T(8,128)(2,1)} %param.9) | copy-start | bytes 393220
  23.8 1.2 %copy-start.4 = (f32[512,512]{1,0:T(8,128)S(1)}, f32[512,512]{1,0:T(8,128)}, u32[]{:S(2)}) copy-start(f32[512,512]{1,0:T(8,128)} %convolution_add_fusion.recv_proj_hbm) | copy-start | bytes 3145732
  25.0 1.2 %copy-start.5 = (f32[512,512]{1,0:T(8,128)S(1)}, f32[512,512]{1,0:T(8,128)}, u32[]{:S(2)}) copy-start(f32[512,512]{1,0:T(8,128)} %fusion.2.agg_grad_hbm) | copy-start | bytes 3145732
  30.6 5.1 %copy-start.8 = (f32[128,512]{1,0:T(8,128)}, f32[128,512]{1,0:T(8,128)S(1)}, u32[]{:S(2)}) copy-start(f32[128,512]{1,0:T(8,128)S(1)} %get-tuple-element.53.local_ref) | copy-start | bytes 786436
  30.6 5.1 %copy-start.12 = (bf16[16,512]{1,0:T(8,128)(2,1)}, bf16[16,512]{1,0:T(8,128)(2,1)S(1)}, u32[]{:S(2)}) copy-start(bf16[16,512]{1,0:T(8,128)(2,1)S(1)} %get-tuple-element.49) | copy-start | bytes 49156
  30.6 6.5 %collective-permute-start.4 = (bf16[800,512]{1,0:T(8,128)(2,1)S(1)}, bf16[800,512]{1,0:T(8,128)(2,1)S(1)}, u32[]{:S(2)}, u32[]{:S(2)}) collective-permute-start(bf16[800,512]{1,0:T(8,128)(2,1)S(1)} %get-tuple-element.43), channel_id=1, source_target_pairs={{0,1},{1,0},{2,3},{3,2},{4,5},{5,4},{6,7},{7,6},{8,9},{9,8},{10,11... | collective-permute-start | bytes 2457608 | tf_op jit(solution)/shard_map/ppermute | solution.py:296
  37.2 0.9 copy-start.6
  38.1 16.2 %all-to-all-start = ((bf16[4,208,512]{2,1,0:T(8,128)(2,1)}), bf16[4,208,512]{2,1,0:T(8,128)(2,1)S(1)}, u32[]{:S(2)}, u32[]{:S(2)}) async-start(bf16[4,208,512]{2,1,0:T(8,128)(2,1)} %copy-done.6), calls=%async_computation | async-start | bytes 1703936 | tf_op jit(solution)/shard_map/all_to_all | solution.py:300
  41.6 56.0 %copy-start.3 = (bf16[512,512]{1,0:T(8,128)(2,1)S(1)}, bf16[512,512]{1,0:T(8,128)(2,1)}, u32[]{:S(2)}) copy-start(bf16[512,512]{1,0:T(8,128)(2,1)} %w_recv_ref.1) | copy-start | bytes 1572868
  41.6 56.0 %copy-start.11 = (s32[1,4,16]{2,1,0:T(4,128)S(1)}, s32[1,4,16]{2,1,0:T(4,128)}, u32[]{:S(2)}) copy-start(s32[1,4,16]{2,1,0:T(4,128)} %param.13) | copy-start | bytes 772
  41.6 14.0 %collective-permute-start.5 = (bf16[16,512]{1,0:T(8,128)(2,1)}, bf16[16,512]{1,0:T(8,128)(2,1)S(1)}, u32[]{:S(2)}, u32[]{:S(2)}) collective-permute-start(bf16[16,512]{1,0:T(8,128)(2,1)} %get-tuple-element.48), channel_id=1, source_target_pairs={{0,63},{1,2},{2,1},{3,4},{4,3},{5,6},{6,5},{7,8},{8,7},{9,10},{10,... | collective-permute-start | bytes 49160 | tf_op jit(solution)/shard_map/ppermute | solution.py:290
  45.6 10.1 %collective-permute-start.6 = (bf16[16,512]{1,0:T(8,128)(2,1)}, bf16[16,512]{1,0:T(8,128)(2,1)S(1)}, u32[]{:S(2)}, u32[]{:S(2)}) collective-permute-start(bf16[16,512]{1,0:T(8,128)(2,1)} %copy-done.12), channel_id=1, source_target_pairs={{0,56},{1,57},{2,58},{3,59},{4,60},{5,61},{6,62},{7,63},{8,0},{9,1... | collective-permute-start | bytes 49160 | tf_op jit(solution)/shard_map/ppermute | solution.py:285
  55.6 42.0 %copy-start.9 = (f32[128,512]{1,0:T(8,128)S(1)}, f32[128,512]{1,0:T(8,128)}, u32[]{:S(2)}) copy-start(f32[128,512]{1,0:T(8,128)} %copy-done.8) | copy-start | bytes 786436
  82.8 18.1 %all-to-all-start.2 = ((bf16[64,16,128]{2,1,0:T(8,128)(2,1)}), bf16[64,16,128]{2,1,0:T(8,128)(2,1)S(1)}, u32[]{:S(2)}, u32[]{:S(2)}) async-start(bf16[64,16,128]{2,1,0:T(8,128)(2,1)} %broadcast_in_dim.8), calls=%async_computation.2 | async-start | bytes 524288 | tf_op jit(solution)/shard_map/all_to_all | solution.py:300
  88.4 9.2 %collective-permute-start.7 = (bf16[16,512]{1,0:T(8,128)(2,1)S(1)}, bf16[16,512]{1,0:T(8,128)(2,1)S(1)}, u32[]{:S(2)}, u32[]{:S(2)}) collective-permute-start(bf16[16,512]{1,0:T(8,128)(2,1)S(1)} %get-tuple-element.57), channel_id=1, source_target_pairs={{0,32},{1,33},{2,34},{3,35},{4,36},{5,37},{6,38},{7,39},{8,40},{9,... | collective-permute-start | bytes 49160 | tf_op jit(solution)/shard_map/ppermute | solution.py:285
  111.9 8.8 %collective-permute-start.8 = (bf16[3,1,256,512]{3,2,1,0:T(8,128)(2,1)S(1)}, bf16[3,1,256,512]{3,2,1,0:T(8,128)(2,1)S(1)}, u32[]{:S(2)}, u32[]{:S(2)}) collective-permute-start(bf16[3,1,256,512]{3,2,1,0:T(8,128)(2,1)S(1)} %bitcast.43), channel_id=1, source_target_pairs={{0,1},{1,0},{2,3},{3,2},{4,5},{5,4},{6,7},{7,6},{8,9},{9,8},{10,11... | collective-permute-start | bytes 2359304 | tf_op jit(solution)/shard_map/ppermute | solution.py:296
